TPU v7x, 128 devices: a whole 4x4x4 slice. The times are simulated.
128 devices in a mesh: replica: 8 (over y_lo, z), expert: 16 (over x, y_hi, core).
Axes of the slice: x: 4, y: 4 (y_hi: 2, y_lo: 2; y = y_hi * 2 + y_lo), z: 4, core: 2. Of those that a mesh axis runs over, the one named last changes fastest.
Arguments:
- hidden_states: bfloat16 [8192, 4096], P(('replica', 'expert')), may hold values from -3 to 3
- queries: bfloat16 [8192, 4096], P(('replica', 'expert')), may hold values from -8 to 8
- key_cache: bfloat16 [8192, 256, 256], P(('replica', 'expert')), may hold values from -8 to 8
- value_cache: bfloat16 [8192, 256, 256], P(('replica', 'expert')), may hold values from -6 to 6
- new_keys: bfloat16 [8192, 256], P(('replica', 'expert')), may hold values from -6 to 6
- new_values: bfloat16 [8192, 256], P(('replica', 'expert')), may hold values from -6 to 6
- cache_lengths: int32 [8192], P(('replica', 'expert')), may hold values from 2 to 256
- norm_gain: float32 [4096], replicated, may hold values from 0.1 to 1.9
- expert_ids: int32 [8192, 8], P(('replica', 'expert')), may hold values from 0 to 127, as said below
- route_weights: float32 [8192, 8], P(('replica', 'expert')), may hold values from 0.1 to 1
- finished: int32 [8192], P(('replica', 'expert')), may hold values from 0 to 1
- learner_ids: int32 [8192], P(('replica', 'expert')), may hold values from 0 to 127, as said below
- gate_weight: bfloat16 [16, 4096, 768], P(None, ('replica', 'expert')), may hold values from -0.09375 to 0.09375
- up_weight: bfloat16 [16, 4096, 768], P(None, ('replica', 'expert')), may hold values from -0.09375 to 0.09375
- down_weight: bfloat16 [16, 768, 4096], P(None, None, ('replica', 'expert')), may hold values from -0.21875 to 0.21875
Outputs:
- layer_out: bfloat16 [8192, 4096], P(('replica', 'expert'))
- learner_rows: bfloat16 [16384, 4096], P(('replica', 'expert'))
Inputs may be any that keep to these rules, and one draw needn't show every extreme that they name: `expert_ids`: each row names 8 different experts, exactly two of them below 16. In each aligned block of 64 rows no expert below 16 is named by more than 32 rows; in each run of 16 consecutive blocks, starting at block 0, one expert below 16 is named by exactly 32 rows of every block of the run. `learner_ids`: in each aligned block of 64 rows no learner is named by more than 1 row. One learner, the same for every block, is named by exactly 1 row of every block, and those rows are finished.
All inputs are finite; a program needn't handle non-finite values.
Results may differ from a plain program's by a relative error of at most 0.0085.
Values may be sent and summed in bfloat16 or wider, within the bound.
No kernel may reach another device: no remote copies, remote signals or barrier semaphores. Data moves between devices by JAX's collectives and lax.ppermute only.
A program may use at most 128 MiB of HBM per device.

v0:
```python
import math

import jax
import jax.numpy as jnp
from jax import lax
from jax.sharding import PartitionSpec as P

HDIM = 128
QHEADS = 32
KVHEADS = 2


def attend_rows(queries, key_cache, value_cache, new_keys, new_values, cache_lengths):
    row_total = queries.shape[0]
    context = key_cache.shape[1]
    per_group = QHEADS // KVHEADS
    query_parts = queries.reshape(row_total, KVHEADS, per_group, HDIM)
    key_parts = key_cache.reshape(row_total, context, KVHEADS, HDIM)
    value_parts = value_cache.reshape(row_total, context, KVHEADS, HDIM)
    fresh_key = new_keys.reshape(row_total, KVHEADS, HDIM)
    fresh_value = new_values.astype(jnp.float32).reshape(row_total, KVHEADS, HDIM)
    scaling = 1.0 / math.sqrt(HDIM)
    cached = (
        jnp.einsum("nkgd,nckd->nkgc", query_parts, key_parts, preferred_element_type=jnp.float32)
        * scaling
    )
    usable = jnp.arange(context)[None, :] < cache_lengths[:, None]
    cached = jnp.where(usable[:, None, None, :], cached, -jnp.inf)
    own_score = (
        jnp.einsum("nkgd,nkd->nkg", query_parts, fresh_key, preferred_element_type=jnp.float32)
        * scaling
    )
    highest = jnp.maximum(jnp.max(cached, axis=-1), own_score)
    cached_exp = jnp.exp(cached - highest[..., None])
    own_exp = jnp.exp(own_score - highest)
    totals = jnp.sum(cached_exp, axis=-1) + own_exp
    cached_prob = (cached_exp / totals[..., None]).astype(jnp.bfloat16)
    own_prob = (own_exp / totals).astype(jnp.bfloat16).astype(jnp.float32)
    mixture = jnp.einsum(
        "nkgc,nckd->nkgd", cached_prob, value_parts, preferred_element_type=jnp.float32
    )
    mixture = mixture + own_prob[..., None] * fresh_value[:, :, None, :]
    return mixture.reshape(row_total, QHEADS * HDIM)


def shards(
    hidden_states,
    queries,
    key_cache,
    value_cache,
    new_keys,
    new_values,
    cache_lengths,
    norm_gain,
    expert_ids,
    route_weights,
    finished,
    learner_ids,
    gate_weight,
    up_weight,
    down_weight,
):
    replicas = lax.axis_size("replica")
    experts = lax.axis_size("expert")
    row_count = hidden_states.shape[0]
    model_width = hidden_states.shape[1]
    capacity = row_count // 2
    tiled_gate = jnp.tile(gate_weight, (replicas, 1, 1))
    tiled_up = jnp.tile(up_weight, (replicas, 1, 1))
    tiled_down = jnp.tile(down_weight, (replicas, 1, 1))
    whole_gate, whole_up = (
        lax.all_to_all(tiled_gate, ("replica", "expert"), split_axis=0, concat_axis=1, tiled=True),
        lax.all_to_all(tiled_up, ("replica", "expert"), split_axis=0, concat_axis=1, tiled=True),
    )
    whole_down = lax.all_to_all(
        tiled_down, ("replica", "expert"), split_axis=0, concat_axis=2, tiled=True
    )
    attended = attend_rows(queries, key_cache, value_cache, new_keys, new_values, cache_lengths)
    middle = hidden_states.astype(jnp.float32) + attended
    spread = jnp.mean(middle * middle, axis=-1, keepdims=True)
    normed = (middle * lax.rsqrt(spread + 1e-06) * norm_gain).astype(jnp.bfloat16)
    expert_range = jnp.arange(experts, dtype=jnp.int32)
    hit_table = expert_ids[:, :, None] == expert_range[None, None, :]
    matched = jnp.any(hit_table, axis=1)
    slot_gate = jnp.sum(jnp.where(hit_table, route_weights[:, :, None], 0.0), axis=1)
    row_range = jnp.arange(row_count, dtype=jnp.int32)
    earlier = row_range[None, :] < row_range[:, None]
    slot_rank = jnp.dot(earlier.astype(jnp.int32), matched.astype(jnp.int32))
    slot_range = jnp.arange(capacity, dtype=jnp.int32)
    chosen = matched.T[:, None, :] & (slot_rank.T[:, None, :] == slot_range[None, :, None])
    source_row = jnp.sum(jnp.where(chosen, row_range[None, None, :], 0), axis=2)
    slot_live = jnp.any(chosen, axis=2)
    slot_weight = jnp.sum(jnp.where(chosen, slot_gate.T[:, None, :], 0.0), axis=2)
    outgoing = jnp.where(slot_live[:, :, None], normed[source_row], jnp.zeros((), jnp.bfloat16))
    received = lax.all_to_all(outgoing, "expert", split_axis=0, concat_axis=0, tiled=True)
    flat_rows = received.reshape(-1, model_width)
    gate_part = jnp.dot(flat_rows, whole_gate[0], preferred_element_type=jnp.float32)
    up_part = jnp.dot(flat_rows, whole_up[0], preferred_element_type=jnp.float32)
    activated = (jax.nn.silu(gate_part) * up_part).astype(jnp.bfloat16)
    expert_out = jnp.dot(activated, whole_down[0], preferred_element_type=jnp.float32).astype(
        jnp.bfloat16
    )
    returned = lax.all_to_all(
        expert_out.reshape(received.shape), "expert", split_axis=0, concat_axis=0, tiled=True
    )
    weighted = returned.astype(jnp.float32) * slot_weight[:, :, None]
    routed = (
        jnp.zeros((row_count, model_width), jnp.float32)
        .at[source_row.reshape(-1)]
        .add(weighted.reshape(-1, model_width))
    )
    layer_out = (middle + routed).astype(jnp.bfloat16)
    learners = replicas * experts
    per_pair = max(1, row_count // learners)
    finished_rows = finished > 0
    same_target = (learner_ids[:, None] == learner_ids[None, :]) & finished_rows[None, :] & earlier
    learner_rank = jnp.sum(same_target.astype(jnp.int32), axis=1)
    slot_of_row = learner_ids * per_pair + learner_rank
    slot_span = jnp.arange(learners * per_pair, dtype=jnp.int32)
    picked = finished_rows[None, :] & (slot_of_row[None, :] == slot_span[:, None])
    pick_row = jnp.sum(jnp.where(picked, row_range[None, :], 0), axis=1)
    pick_live = jnp.any(picked, axis=1)
    parcel = jnp.where(pick_live[:, None], layer_out[pick_row], jnp.zeros((), jnp.bfloat16))
    parcel = parcel.reshape(learners, per_pair, model_width)
    arrived = lax.all_to_all(parcel, ("replica", "expert"), split_axis=0, concat_axis=0, tiled=True)
    return (layer_out, arrived.reshape(-1, model_width))


def solution(mesh):
    placed = (
        P(("replica", "expert"), None),
        P(("replica", "expert"), None),
        P(("replica", "expert"), None, None),
        P(("replica", "expert"), None, None),
        P(("replica", "expert"), None),
        P(("replica", "expert"), None),
        P(("replica", "expert")),
        P(),
        P(("replica", "expert"), None),
        P(("replica", "expert"), None),
        P(("replica", "expert")),
        P(("replica", "expert")),
        P(None, ("replica", "expert"), None),
        P(None, ("replica", "expert"), None),
        P(None, None, ("replica", "expert")),
    )
    return jax.shard_map(
        shards,
        mesh=mesh,
        in_specs=placed,
        out_specs=(P(("replica", "expert"), None), P(("replica", "expert"), None)),
        check_vma=False,
    )
```

profile of v0, /device:TPU:1, one launch (start us, length us, event | category | flops | bytes accessed | tf_op | source)
XLA Modules:
  0.0 477.3 jit_solution(8260831908908150102)
XLA Ops:
  0.6 0.7 fusion.18
  2.2 0.7 iota_compare_fusion.2
  2.9 1.1 copy.62
  4.1 0.8 reshape.215
  4.9 0.4 fusion.30
  5.3 5.8 %fusion.6 = (f32[64,2,16]{2,1,0:T(2,128)S(1)}, f32[64,2,16,256]{3,2,1,0:T(8,128)S(1)}) fusion(pred[64,256]{1,0:T(8,128)(4,1)S(1)} %iota_compare_fusion.2, bf16[64,2,16,128]{3,2,1,0:T(8,128)(2,1)S(1)} %bitcast.92, bf16[64,256,256]{2,1,0:T(8,128)(2,1)} %param.17), kind=kOutput, calls=%fused_computation.15 | convolution fusion | flops 135788544 | bytes 11034624 | tf_op jit(solution)/shard_map/nkgd,nckd->nkgc/dot_general | solution.py:24
  11.3 1.0 fusion.7
  12.7 5.0 %fusion.8 = f32[64,2,16,128]{3,2,1,0:T(8,128)S(1)} fusion(f32[64,2,16,256]{3,2,1,0:T(8,128)S(1)} %get-tuple-element.7, f32[64,2,16]{2,1,0:T(2,128)S(1)} %copy.53, f32[64,2,16]{2,1,0:T(2,128)S(1)} %copy.51, pred[64,256]{1,0:T(8,128)(4,1)S(1)} %iota_compare_fusion.2, f32[64,2,128]{2,1,0:T(2,128)S(1)} %reshape.186, f32[64,2,16]{2,1,0:T(2,128)S(1)} %copy.55, ...), kind=kOutput, calls=%fused_computation.18 | convolution fusion | flops 137363456 | bytes 11640832 | tf_op jit(solution)/shard_map/nkgc,nckd->nkgd/dot_general | solution.py:39
  17.6 0.9 multiply_reduce_fusion
  18.8 4.4 gather_fusion
  23.1 2.5 broadcast_select_fusion
  25.7 58.9 %all_to_all.48 = bf16[16,32,4096]{2,1,0:T(8,128)(2,1)} all-to-all(bf16[16,32,4096]{2,1,0:T(8,128)(2,1)S(1)} %broadcast_select_fusion), channel_id=1, replica_groups=mesh['replica'=8,'expert'=16] {'expert'}, dimensions={0} | all-to-all | bytes 8388608 | tf_op jit(solution)/shard_map/all_to_all | solution.py:95
  84.6 0.8 tile.31
  85.4 82.1 %all_to_all.49 = bf16[128,768,32]{1,2,0:T(8,128)(2,1)} all-to-all(bf16[128,768,32]{1,2,0:T(8,128)(2,1)S(1)} %bitcast.83), channel_id=1, replica_groups=mesh['replica'=8,'expert'=16] {'replica','expert'}, dimensions={0} | all-to-all | bytes 12582912 | tf_op jit(solution)/shard_map/all_to_all | solution.py:75
  167.5 0.8 tile.12
  168.3 81.2 %all_to_all.50 = bf16[128,32,768]{2,1,0:T(8,128)(2,1)} all-to-all(bf16[128,32,768]{2,1,0:T(8,128)(2,1)S(1)} %bitcast.84), channel_id=1, replica_groups=mesh['replica'=8,'expert'=16] {'replica','expert'}, dimensions={0} | all-to-all | bytes 12582912 | tf_op jit(solution)/shard_map/all_to_all | solution.py:72
  249.5 3.4 tile.14
  252.8 6.4 %all-to-all-start.2 = ((bf16[128,32,768]{2,1,0:T(8,128)(2,1)}), bf16[128,32,768]{2,1,0:T(8,128)(2,1)}, u32[]{:S(2)}, u32[]{:S(2)}) async-start(bf16[128,32,768]{2,1,0:T(8,128)(2,1)} %bitcast.82), calls=%async_computation.2 | async-start | bytes 12582912 | tf_op jit(solution)/shard_map/all_to_all | solution.py:73
  259.3 7.0 %fusion.31 = f32[512,768]{1,0:T(8,128)S(1)} fusion(bf16[512,4096]{1,0:T(8,128)(2,1)} %bitcast.89, bf16[4096,768]{1,0:T(8,128)(2,1)} %bitcast.87), kind=kOutput, calls=%fused_computation.64 | convolution fusion | flops 3221225472 | bytes 12058624 | tf_op jit(solution)/shard_map/dot_general | solution.py:97
  266.3 68.8 %all-to-all-done.2 = bf16[128,32,768]{2,1,0:T(8,128)(2,1)} async-done(((bf16[128,32,768]{2,1,0:T(8,128)(2,1)}), bf16[128,32,768]{2,1,0:T(8,128)(2,1)}, u32[]{:S(2)}, u32[]{:S(2)}) %all-to-all-start.2) | async-done | bytes 6291488 | tf_op jit(solution)/shard_map/all_to_all | solution.py:73
  335.1 16.6 %convolution_convert_fusion = bf16[512,4096]{1,0:T(8,128)(2,1)} fusion(bf16[768,4096]{0,1:T(8,128)(2,1)} %bitcast.86, f32[512,768]{1,0:T(8,128)S(1)} %fusion.31, bf16[512,4096]{1,0:T(8,128)(2,1)} %bitcast.90, bf16[4096,768]{1,0:T(8,128)(2,1)} %bitcast.9), kind=kOutput, calls=%fused_computation.10 | convolution fusion | flops 6446907392 | bytes 22544384 | tf_op jit(solution)/shard_map/dot_general | solution.py:100
  351.7 10.1 %all-to-all-start.4 = ((bf16[16,32,4096]{2,1,0:T(8,128)(2,1)}), bf16[16,32,4096]{2,1,0:T(8,128)(2,1)}, u32[]{:S(2)}, u32[]{:S(2)}) async-start(bf16[16,32,4096]{2,1,0:T(8,128)(2,1)} %bitcast.88), calls=%async_computation.4 | async-start | bytes 8388608 | tf_op jit(solution)/shard_map/all_to_all | solution.py:103
  362.5 52.0 %all-to-all-done.4 = bf16[16,32,4096]{2,1,0:T(8,128)(2,1)} async-done(((bf16[16,32,4096]{2,1,0:T(8,128)(2,1)}), bf16[16,32,4096]{2,1,0:T(8,128)(2,1)}, u32[]{:S(2)}, u32[]{:S(2)}) %all-to-all-start.4) | async-done | bytes 4194336 | tf_op jit(solution)/shard_map/all_to_all | solution.py:103
  414.5 6.6 %convert_multiply_fusion = f32[16,32,4096]{2,1,0:T(8,128)} fusion(bf16[16,32,4096]{2,1,0:T(8,128)(2,1)} %all-to-all-done.4, f32[16,32]{1,0:T(8,128)S(1)} %select_reduce_fusion), kind=kLoop, calls=%fused_computation.9 | loop fusion | flops 4194304 | bytes 12584960 | tf_op jit(solution)/shard_map/mul | solution.py:106
  421.1 14.6 %scatter_fusion = f32[64,4096]{1,0:T(8,128)S(1)} fusion(f32[64,4096]{1,0:T(8,128)S(1)} %get-tuple-element.3, s32[512]{0:T(512)S(1)} %bitcast.100, f32[512,4096]{1,0:T(8,128)} %bitcast.81), kind=kCustom, calls=%fused_computation.2 | custom fusion | flops 2097152 | bytes 25167872 | tf_op jit(solution)/shard_map/scatter-add | solution.py:110
  435.7 1.2 gather_fusion.1
  437.1 0.5 broadcast.118
  437.6 1.4 reduce
  439.0 0.8 reshape.216
  439.8 34.3 %all_to_all.51 = bf16[128,2,2048]{2,1,0:T(2,128)(2,1)S(1)} all-to-all(bf16[128,2,2048]{2,1,0:T(2,128)(2,1)S(1)} %reshape.216), channel_id=1, replica_groups=mesh['replica'=8,'expert'=16] {'replica','expert'}, dimensions={0} | all-to-all | bytes 2097152 | tf_op jit(solution)/shard_map/all_to_all | solution.py:125
  474.1 1.0 reshape.217
  475.2 2.1 copy.79
  (52 shorter events, 2.6 us)
Async XLA Ops:
  5.3 7.2 %copy-start.5 = (bf16[64,256]{1,0:T(8,128)(2,1)S(1)}, bf16[64,256]{1,0:T(8,128)(2,1)}, u32[]{:S(2)}) copy-start(bf16[64,256]{1,0:T(8,128)(2,1)} %param.20) | copy-start | bytes 98308
  12.6 5.0 %copy-start.4 = (bf16[64,4096]{1,0:T(8,128)(2,1)S(1)}, bf16[64,4096]{1,0:T(8,128)(2,1)}, u32[]{:S(2)}) copy-start(bf16[64,4096]{1,0:T(8,128)(2,1)} %param.15) | copy-start | bytes 1572868
  12.6 5.9 %copy-start.6 = (f32[4096]{0:T(1024)S(1)}, f32[4096]{0:T(1024)}, u32[]{:S(2)}) copy-start(f32[4096]{0:T(1024)} %param.22) | copy-start | bytes 49156
  25.7 59.0 %copy-start.1 = (bf16[16,768,32]{1,2,0:T(8,128)(2,1)S(1)}, bf16[16,768,32]{1,2,0:T(8,128)(2,1)}, u32[]{:S(2)}) copy-start(bf16[16,768,32]{1,2,0:T(8,128)(2,1)} %param.29) | copy-start | bytes 2359300
  85.4 82.1 %copy-start.2 = (bf16[16,32,768]{2,1,0:T(8,128)(2,1)S(1)}, bf16[16,32,768]{2,1,0:T(8,128)(2,1)}, u32[]{:S(2)}) copy-start(bf16[16,32,768]{2,1,0:T(8,128)(2,1)} %param.27) | copy-start | bytes 2359300
  168.2 81.2 %copy-start.3 = (bf16[16,32,768]{2,1,0:T(8,128)(2,1)S(1)}, bf16[16,32,768]{2,1,0:T(8,128)(2,1)}, u32[]{:S(2)}) copy-start(bf16[16,32,768]{2,1,0:T(8,128)(2,1)} %param.28) | copy-start | bytes 2359300
  252.8 82.3 %all-to-all-start.2 = ((bf16[128,32,768]{2,1,0:T(8,128)(2,1)}), bf16[128,32,768]{2,1,0:T(8,128)(2,1)}, u32[]{:S(2)}, u32[]{:S(2)}) async-start(bf16[128,32,768]{2,1,0:T(8,128)(2,1)} %bitcast.82), calls=%async_computation.2 | async-start | bytes 12582912 | tf_op jit(solution)/shard_map/all_to_all | solution.py:73
  351.7 10.2 %copy-start.10 = (s32[64]{0:T(128)S(1)}, s32[64]{0:T(128)}, u32[]{:S(2)}) copy-start(s32[64]{0:T(128)} %param.25) | copy-start | bytes 772
  351.7 10.2 %copy-start.9 = (s32[64]{0:T(128)S(1)}, s32[64]{0:T(128)}, u32[]{:S(2)}) copy-start(s32[64]{0:T(128)} %param.26) | copy-start | bytes 772
  351.7 10.5 %copy-start.7 = (s32[64,8]{0,1:T(8,128)S(1)}, s32[64,8]{0,1:T(8,128)}, u32[]{:S(2)}) copy-start(s32[64,8]{0,1:T(8,128)} %param.23) | copy-start | bytes 6148
  351.7 10.5 %copy-start.8 = (f32[64,8]{0,1:T(8,128)S(1)}, f32[64,8]{0,1:T(8,128)}, u32[]{:S(2)}) copy-start(f32[64,8]{0,1:T(8,128)} %param.24) | copy-start | bytes 6148
  351.7 62.8 %all-to-all-start.4 = ((bf16[16,32,4096]{2,1,0:T(8,128)(2,1)}), bf16[16,32,4096]{2,1,0:T(8,128)(2,1)}, u32[]{:S(2)}, u32[]{:S(2)}) async-start(bf16[16,32,4096]{2,1,0:T(8,128)(2,1)} %bitcast.88), calls=%async_computation.4 | async-start | bytes 8388608 | tf_op jit(solution)/shard_map/all_to_all | solution.py:103
  435.7 1.2 copy-start
where the time goes:
time: 478 us; the launch traced here: 477 us
  blocking collectives  256 us (54%)
  waiting for transfers between devices  121 us (25%)
  matrix products  34.9 us (7%)
  other arithmetic  30 us (6%)
  local copies, waits for them, and re-layouts  17.6 us (4%)
  starting transfers between devices  16.5 us (3%)
    all_to_all x1, blocking collectives, shards(): lax.all_to_all(tiled_down, ('replica', 'expert'), split_axis=0, concat_ax...  82.1 us
    all_to_all x1, blocking collectives, shards(): lax.all_to_all(tiled_gate, ('replica', 'expert'), split_axis=0, concat_ax...  81.2 us
    all_to_all x1, waiting for transfers between devices, shards(): lax.all_to_all(tiled_up, ('replica', 'expert'), split_axis=0, concat_axis...  68.8 us
    all_to_all x1, blocking collectives, shards(): lax.all_to_all(outgoing, 'expert', split_axis=0, concat_axis=0, tiled=True)  58.9 us
    all_to_all x1, waiting for transfers between devices, shards(): lax.all_to_all(expert_out.reshape(received.shape), 'expert', split_axis=0...  52 us
    all_to_all x1, blocking collectives, shards(): lax.all_to_all(parcel, ('replica', 'expert'), split_axis=0, concat_axis=0...  34.3 us
    dot_general x1, matrix products, shards(): jnp.dot(activated, whole_down[0], preferred_element_type=jnp.float32)  16.6 us
    scatter-add x1, other arithmetic, shards(): routed = jnp.zeros((row_count, model_width), jnp.float32).at[source_row.r...  14.6 us
  transfers between devices with their start and end apart: 2, of which 2 were waited for; matrix products, arithmetic and copies ran while one was open for 2% of the time, Pallas kernels for 0%

commit v1 on v0

v1 whole, which is shorter than its diff:
```python
import math

import jax
import jax.numpy as jnp
from jax import lax
from jax.experimental import pallas as pl
from jax.experimental.pallas import tpu as pltpu
from jax.sharding import Mesh
from jax.sharding import PartitionSpec as P

HDIM = 128
QHEADS = 32
KVHEADS = 2

AXES = ("ylo", "z", "x", "yhi", "core")
PLANE = ("ylo", "x", "yhi")
RING = 4
ZUP = [(i, (i + 1) % RING) for i in range(RING)]
ZDOWN = [(i, (i - 1) % RING) for i in range(RING)]
SWAP = [(0, 1), (1, 0)]


def attend_rows(queries, key_cache, value_cache, new_keys, new_values, cache_lengths):
    row_total = queries.shape[0]
    context = key_cache.shape[1]
    per_group = QHEADS // KVHEADS
    query_parts = queries.reshape(row_total, KVHEADS, per_group, HDIM)
    key_parts = key_cache.reshape(row_total, context, KVHEADS, HDIM)
    value_parts = value_cache.reshape(row_total, context, KVHEADS, HDIM)
    fresh_key = new_keys.reshape(row_total, KVHEADS, HDIM)
    fresh_value = new_values.astype(jnp.float32).reshape(row_total, KVHEADS, HDIM)
    scaling = 1.0 / math.sqrt(HDIM)
    cached = (
        jnp.einsum("nkgd,nckd->nkgc", query_parts, key_parts, preferred_element_type=jnp.float32)
        * scaling
    )
    usable = jnp.arange(context)[None, :] < cache_lengths[:, None]
    cached = jnp.where(usable[:, None, None, :], cached, -jnp.inf)
    own_score = (
        jnp.einsum("nkgd,nkd->nkg", query_parts, fresh_key, preferred_element_type=jnp.float32)
        * scaling
    )
    highest = jnp.maximum(jnp.max(cached, axis=-1), own_score)
    cached_exp = jnp.exp(cached - highest[..., None])
    own_exp = jnp.exp(own_score - highest)
    totals = jnp.sum(cached_exp, axis=-1) + own_exp
    cached_prob = (cached_exp / totals[..., None]).astype(jnp.bfloat16)
    own_prob = (own_exp / totals).astype(jnp.bfloat16).astype(jnp.float32)
    mixture = jnp.einsum(
        "nkgc,nckd->nkgd", cached_prob, value_parts, preferred_element_type=jnp.float32
    )
    mixture = mixture + own_prob[..., None] * fresh_value[:, :, None, :]
    return mixture.reshape(row_total, QHEADS * HDIM)


def spread_piece(piece):
    half = piece.shape[0] // 2
    prev = lax.ppermute(piece, "z", ZUP)
    succ = lax.ppermute(piece, "z", ZDOWN)
    far_a = lax.ppermute(prev[:half], "z", ZUP)
    far_b = lax.ppermute(succ[half:], "z", ZDOWN)
    mine = [piece, prev, succ, far_a, far_b]
    other = [lax.ppermute(part, "core", SWAP) for part in mine]
    return mine + other


def place_copies(place_ref, parts, kinds, scratch, sem, ylos):
    z = place_ref[0]
    core = place_ref[1]
    copies = []
    for index, part in enumerate(parts):
        which = index % 5
        c = core if index < 5 else 1 - core
        step = (0, RING - 1, 1, 2, 2)[which]
        zz = lax.rem(z + step, RING)
        halves = part.shape[0]
        for lo in range(halves):
            low = lo if which != 4 else lo + ylos - halves
            if kinds:
                for kind in range(kinds):
                    copies.append(
                        pltpu.make_async_copy(
                            part.at[lo, :, kind], scratch.at[kind, low, zz, :, c], sem
                        )
                    )
            else:
                copies.append(
                    pltpu.make_async_copy(part.at[lo], scratch.at[low, zz, :, c], sem)
                )
    return copies


def hidden_kernel(place_ref, rows_ref, *refs):
    parts = refs[:10]
    out_ref, scratch, sem = refs[10:]
    copies = place_copies(place_ref, parts, 2, scratch, sem, 2)
    for copy in copies:
        copy.start()
    for copy in copies:
        copy.wait()
    width = out_ref.shape[1]
    step = 256

    @pl.loop(0, width // step)
    def _(i):
        cols = pl.ds(pl.multiple_of(i * step, step), step)
        rows = rows_ref[...]
        depth = rows.shape[1]
        gate = scratch[0, :, :, :, :, :, cols].reshape(depth, step)
        up = scratch[1, :, :, :, :, :, cols].reshape(depth, step)
        g = jnp.dot(rows, gate, preferred_element_type=jnp.float32)
        u = jnp.dot(rows, up, preferred_element_type=jnp.float32)
        out_ref[:, cols] = (g / (1.0 + jnp.exp(-g)) * u).astype(out_ref.dtype)


def hidden_call(place, rows, parts):
    count, depth = rows.shape
    width = parts[0].shape[-1]
    vmem = pl.BlockSpec(memory_space=pltpu.VMEM)
    return pl.pallas_call(
        hidden_kernel,
        out_shape=jax.ShapeDtypeStruct((count, width), jnp.bfloat16),
        in_specs=[pl.BlockSpec(memory_space=pltpu.SMEM), vmem]
        + [pl.BlockSpec(memory_space=pl.ANY)] * 10,
        out_specs=vmem,
        scratch_shapes=[
            pltpu.VMEM((2, 2, RING, 8, 2, 32, width), jnp.bfloat16),
            pltpu.SemaphoreType.DMA,
        ],
        compiler_params=pltpu.CompilerParams(vmem_limit_bytes=40 * 1024 * 1024),
        cost_estimate=pl.CostEstimate(
            flops=4 * count * depth * width,
            bytes_accessed=4 * depth * width + 2 * count * depth,
            transcendentals=count * width,
        ),
    )(place, rows, *parts)


def project_kernel(place_ref, hidden_ref, *refs):
    parts = refs[:10]
    out_ref, scratch, sem = refs[10:]
    ylos = scratch.shape[0]
    copies = place_copies(place_ref, parts, 0, scratch, sem, ylos)
    for copy in copies:
        copy.start()
    for copy in copies:
        copy.wait()
    hidden = hidden_ref[...]
    for lo in range(ylos):
        for zz in range(RING):
            weight = scratch[lo, zz].reshape(512, hidden.shape[1])
            out_ref[:, lo * 2048 + zz * 512 : lo * 2048 + (zz + 1) * 512] = lax.dot_general(
                hidden, weight, (((1,), (1,)), ((), ())), preferred_element_type=jnp.float32
            ).astype(out_ref.dtype)


def project_call(place, hidden, parts, ylos):
    count, width = hidden.shape
    depth = ylos * 2048
    vmem = pl.BlockSpec(memory_space=pltpu.VMEM)
    return pl.pallas_call(
        project_kernel,
        out_shape=jax.ShapeDtypeStruct((count, depth), jnp.bfloat16),
        in_specs=[pl.BlockSpec(memory_space=pltpu.SMEM), vmem]
        + [pl.BlockSpec(memory_space=pl.ANY)] * 10,
        out_specs=vmem,
        scratch_shapes=[
            pltpu.VMEM((ylos, RING, 8, 2, 32, width), jnp.bfloat16),
            pltpu.SemaphoreType.DMA,
        ],
        compiler_params=pltpu.CompilerParams(vmem_limit_bytes=40 * 1024 * 1024),
        cost_estimate=pl.CostEstimate(
            flops=2 * count * depth * width,
            bytes_accessed=2 * depth * width + 2 * count * depth,
            transcendentals=0,
        ),
    )(place, hidden, *parts)


def shards(
    hidden_states,
    queries,
    key_cache,
    value_cache,
    new_keys,
    new_values,
    cache_lengths,
    norm_gain,
    expert_ids,
    route_weights,
    finished,
    learner_ids,
    gate_weight,
    up_weight,
    down_weight,
):
    experts = 16
    learners = 128
    row_count, model_width = hidden_states.shape
    capacity = row_count // 2
    slots = experts * capacity
    place = jnp.stack([lax.axis_index("z"), lax.axis_index("core")]).astype(jnp.int32)

    pair = jnp.stack([gate_weight, up_weight], axis=1)
    pair = lax.all_to_all(pair, PLANE, split_axis=0, concat_axis=0, tiled=True)
    down = jnp.swapaxes(down_weight, 1, 2)
    down = lax.all_to_all(down, PLANE, split_axis=0, concat_axis=0, tiled=True)
    width = down.shape[-1]
    pair_parts = [
        part.reshape(-1, 8, 2, 32, width)
        for part in spread_piece(pair.reshape(16, 2, 32, width))
    ]
    down_parts = [
        part.reshape(-1, 8, 32, width) for part in spread_piece(down.reshape(16, 32, width))
    ]

    attended = attend_rows(queries, key_cache, value_cache, new_keys, new_values, cache_lengths)
    middle = hidden_states.astype(jnp.float32) + attended
    spread = jnp.mean(middle * middle, axis=-1, keepdims=True)
    normed = (middle * lax.rsqrt(spread + 1e-06) * norm_gain).astype(jnp.bfloat16)

    expert_range = jnp.arange(experts, dtype=jnp.int32)
    hit_table = expert_ids[:, :, None] == expert_range[None, None, :]
    matched = jnp.any(hit_table, axis=1)
    slot_gate = jnp.sum(jnp.where(hit_table, route_weights[:, :, None], 0.0), axis=1)
    row_range = jnp.arange(row_count, dtype=jnp.int32)
    earlier = row_range[None, :] < row_range[:, None]
    slot_rank = jnp.sum(
        jnp.where(earlier[:, :, None] & matched[None, :, :], 1, 0).astype(jnp.int32), axis=1
    )
    slot_range = jnp.arange(capacity, dtype=jnp.int32)
    chosen = matched[:, :, None] & (slot_rank[:, :, None] == slot_range[None, None, :])
    pick = chosen.reshape(row_count, slots).astype(jnp.bfloat16)
    weigh = jnp.where(chosen, slot_gate[:, :, None], 0.0).reshape(row_count, slots)
    weigh_high = weigh.astype(jnp.bfloat16)
    weigh_low = (weigh - weigh_high.astype(jnp.float32)).astype(jnp.bfloat16)

    outgoing = lax.dot_general(
        pick, normed, (((0,), (0,)), ((), ())), preferred_element_type=jnp.float32
    ).astype(jnp.bfloat16)
    received = lax.all_to_all(
        outgoing.reshape(experts, capacity, model_width),
        PLANE,
        split_axis=0,
        concat_axis=0,
        tiled=True,
    ).reshape(slots, model_width)

    hidden = hidden_call(place, received, pair_parts)
    expert_out = project_call(place, hidden, down_parts, 2)
    returned = lax.all_to_all(
        expert_out.reshape(experts, capacity, model_width),
        PLANE,
        split_axis=0,
        concat_axis=0,
        tiled=True,
    ).reshape(slots, model_width)
    routed = jnp.dot(weigh_high, returned, preferred_element_type=jnp.float32) + jnp.dot(
        weigh_low, returned, preferred_element_type=jnp.float32
    )
    layer_out = (middle + routed).astype(jnp.bfloat16)

    per_pair = 1
    finished_rows = finished > 0
    same_target = (learner_ids[:, None] == learner_ids[None, :]) & finished_rows[None, :] & earlier
    learner_rank = jnp.sum(same_target.astype(jnp.int32), axis=1)
    slot_of_row = learner_ids * per_pair + learner_rank
    slot_span = jnp.arange(learners * per_pair, dtype=jnp.int32)
    picked = finished_rows[None, :] & (slot_of_row[None, :] == slot_span[:, None])
    parcel = jnp.dot(
        picked.astype(jnp.bfloat16), layer_out, preferred_element_type=jnp.float32
    ).astype(jnp.bfloat16)
    parcel = parcel.reshape(learners, per_pair, model_width)
    arrived = lax.all_to_all(parcel, AXES, split_axis=0, concat_axis=0, tiled=True)
    return (layer_out, arrived.reshape(-1, model_width))


def solution(mesh):
    fine = Mesh(mesh.devices.reshape(2, 4, 4, 2, 2), AXES)
    rows = P(AXES)
    placed = (
        P(AXES, None),
        P(AXES, None),
        P(AXES, None, None),
        P(AXES, None, None),
        P(AXES, None),
        P(AXES, None),
        P(AXES),
        P(),
        P(AXES, None),
        P(AXES, None),
        P(AXES),
        P(AXES),
        P(None, AXES, None),
        P(None, AXES, None),
        P(None, None, AXES),
    )
    return jax.shard_map(
        shards,
        mesh=fine,
        in_specs=placed,
        out_specs=(P(AXES, None), P(AXES, None)),
        check_vma=False,
    )
```

time: 478 us -> 296 us (0.62)
  blocking collectives: 256 us -> 26.9 us
  starting transfers between devices: 16.5 us -> 46.1 us
  other arithmetic: 30 us -> 8.25 us
  waiting for transfers between devices: 121 us -> 142 us
  Pallas kernels: 0 us -> 18.7 us
  matrix products: 34.9 us -> 22.6 us
  local copies, waits for them, and re-layouts: 17.6 us -> 29.5 us
    all_to_all x4 -> x1, blocking collectives: 256 us -> 26.9 us  [shards(): lax.all_to_all(parcel, AXES, split_axis=0, concat_axis=0, tiled=True)]
    ppermute x0 -> x18, waiting for transfers between devices: none -> 62.3 us  [the longest x2 46.6 us: spread_piece(): prev = lax.ppermute(piece, 'z', ZUP)]
    all_to_all x2 -> x4, waiting for transfers between devices: 121 us -> 79.3 us  [the longest x1 66.6 us: shards(): lax.all_to_all(expert_out.reshape(experts, capacity, model_width), PLANE,...]
    ppermute x0 -> x18, starting transfers between devices: none -> 18.7 us  [the longest x10 6.55 us: spread_piece(): other = [lax.ppermute(part, 'core', SWAP) for part in mine]]
    pallas_call x0 -> x2, Pallas kernels: none -> 18.7 us  [the longest x1 12.5 us: hidden_call(): pl.pallas_call(hidden_kernel, out_shape=jax.ShapeDtypeStruct((count, widt...]
    unnamed x26 -> x60, local copies, waits for them, and re-layouts: 5.15 us -> 23.5 us
    scatter-add x1 -> x0, other arithmetic: 14.6 us -> none  [shards(): routed = jnp.zeros((row_count, model_width), jnp.float32).at[source_row.r...]
    dot_general x3 -> x4, matrix products: 23.8 us -> 10.6 us  [the longest x1 3.61 us: shards(): jnp.dot(weigh_low, returned, preferred_element_type=jnp.float32)]
  transfers between devices with their start and end apart: 2 -> 22, of which waited for: 2 -> 4; matrix products, arithmetic and copies ran while one was open for 2% -> 10% of each run, Pallas kernels for 0% -> 4%
where the time goes in v1:
time: 296 us; the launch traced here: 295 us
  waiting for transfers between devices  142 us (48%)
  starting transfers between devices  46.1 us (16%)
  local copies, waits for them, and re-layouts  29.5 us (10%)
  blocking collectives  26.9 us (9%)
  matrix products  22.6 us (8%)
  Pallas kernels  18.7 us (6%)
  other arithmetic  8.25 us (3%)
    all_to_all x1, waiting for transfers between devices, shards(): lax.all_to_all(expert_out.reshape(experts, capacity, model_width), PLANE,...  66.6 us
    ppermute x2, waiting for transfers between devices, spread_piece(): prev = lax.ppermute(piece, 'z', ZUP)  46.6 us
    all_to_all x1, blocking collectives, shards(): lax.all_to_all(parcel, AXES, split_axis=0, concat_axis=0, tiled=True)  26.9 us
    unnamed x60, local copies, waits for them, and re-layouts  23.5 us
    ppermute x2, waiting for transfers between devices, spread_piece(): far_a = lax.ppermute(prev[:half], 'z', ZUP)  15.6 us
    all_to_all x1, waiting for transfers between devices, shards(): pair = lax.all_to_all(pair, PLANE, split_axis=0, concat_axis=0, tiled=True)  12.7 us
    pallas_call x1, Pallas kernels, hidden_call(): pl.pallas_call(hidden_kernel, out_shape=jax.ShapeDtypeStruct((count, widt...  12.5 us
    all_to_all x1, starting transfers between devices, shards(): down = lax.all_to_all(down, PLANE, split_axis=0, concat_axis=0, tiled=True)  7.6 us
  transfers between devices with their start and end apart: 22, of which 4 were waited for; matrix products, arithmetic and copies ran while one was open for 10% of the time, Pallas kernels for 4%

profile of v1, /device:TPU:1, one launch (start us, length us, event | category | flops | bytes accessed | tf_op | source)
XLA Modules:
  0.0 294.7 jit_solution(609901595207585130)
XLA Ops:
  0.6 7.6 %all-to-all-start.2 = ((bf16[16,32,768]{2,1,0:T(8,128)(2,1)}), bf16[16,32,768]{2,1,0:T(8,128)(2,1)S(1)}, u32[]{:S(2)}, u32[]{:S(2)}) async-start(bf16[16,32,768]{2,1,0:T(8,128)(2,1)} %bitcast.122), calls=%async_computation.2 | async-start | bytes 1572864 | tf_op jit(solution)/shard_map/all_to_all | solution.py:207
  10.1 5.8 %fusion.10 = (f32[64,2,16]{2,1,0:T(2,128)S(1)}, f32[64,2,16,256]{3,2,1,0:T(8,128)S(1)}) fusion(pred[64,256]{1,0:T(8,128)(4,1)S(1)} %iota_compare_fusion.3, bf16[64,2,16,128]{3,2,1,0:T(8,128)(2,1)S(1)} %bitcast.119, bf16[64,256,256]{2,1,0:T(8,128)(2,1)} %param.17), kind=kOutput, calls=%fused_computation.17 | convolution fusion | flops 135788544 | bytes 11034624 | tf_op jit(solution)/shard_map/nkgd,nckd->nkgc/dot_general | solution.py:34
  16.8 1.2 fusion.46
  21.7 2.7 pad_maximum_fusion
  24.4 6.8 %all-to-all-start.1 = ((bf16[16,2,32,768]{3,2,1,0:T(8,128)(2,1)}), bf16[16,2,32,768]{3,2,1,0:T(8,128)(2,1)S(1)}, u32[]{:S(2)}, u32[]{:S(2)}) async-start(bf16[16,2,32,768]{3,2,1,0:T(8,128)(2,1)} %pad_maximum_fusion), calls=%async_computation.1 | async-start | bytes 3145728 | tf_op jit(solution)/shard_map/all_to_all | solution.py:205
  31.2 4.9 %fusion.12 = f32[64,2,16,128]{3,2,1,0:T(8,128)S(1)} fusion(f32[64,2,16,256]{3,2,1,0:T(8,128)} %copy-done.15, f32[64,2,16]{2,1,0:T(2,128)S(1)} %copy.49, f32[64,2,16]{2,1,0:T(2,128)S(1)} %copy.47, pred[64,256]{1,0:T(8,128)(4,1)S(1)} %iota_compare_fusion.3, f32[64,2,128]{2,1,0:T(2,128)S(1)} %copy-done.19, f32[64,2,16]{2,1,0:T(2,128)S(1)} %copy.51, ...), kind=kOutput, calls=%fused_computation.20 | convolution fusion | flops 137363456 | bytes 11640832 | tf_op jit(solution)/shard_map/nkgc,nckd->nkgd/dot_general | solution.py:49
  37.1 3.5 %convolution_convert_fusion = bf16[512,4096]{1,0:T(8,128)(2,1)} fusion(pred[64,512]{0,1:T(32,128)(4,1)S(1)} %fusion.24, f32[4096]{0:T(1024)S(1)} %copy-done.22, f32[64]{0:T(128)S(1)} %add_rsqrt_fusion, f32[8,8,32,128]{3,2,1,0:T(8,128)S(1)} %bitcast.117, bf16[64,4096]{1,0:T(8,128)(2,1)S(1)} %copy-done.16), kind=kOutput, calls=%fused_computation.6 | convolution fusion | flops 271843328 | bytes 5816576 | tf_op jit(solution)/shard_map/dot_general | solution.py:238
  40.7 12.7 %all-to-all-done.1 = bf16[16,2,32,768]{3,2,1,0:T(8,128)(2,1)S(1)} async-done(((bf16[16,2,32,768]{3,2,1,0:T(8,128)(2,1)}), bf16[16,2,32,768]{3,2,1,0:T(8,128)(2,1)S(1)}, u32[]{:S(2)}, u32[]{:S(2)}) %all-to-all-start.1) | async-done | bytes 1572896 | tf_op jit(solution)/shard_map/all_to_all | solution.py:205
  53.4 6.2 %all-to-all-start = ((bf16[16,32,4096]{2,1,0:T(8,128)(2,1)}), bf16[16,32,4096]{2,1,0:T(8,128)(2,1)}, u32[]{:S(2)}, u32[]{:S(2)}) async-start(bf16[16,32,4096]{2,1,0:T(8,128)(2,1)} %bitcast.115), calls=%async_computation | async-start | bytes 8388608 | tf_op jit(solution)/shard_map/all_to_all | solution.py:241
  59.6 1.7 collective-permute-start
  61.3 2.2 collective-permute-start.1
  63.5 2.7 collective-permute-start.10
  66.1 46.6 %collective-permute-done.9 = bf16[16,32,768]{2,1,0:T(8,128)(2,1)S(1)} collective-permute-done((bf16[16,32,768]{2,1,0:T(8,128)(2,1)S(1)}, bf16[16,32,768]{2,1,0:T(8,128)(2,1)S(1)}, u32[]{:S(2)}, u32[]{:S(2)}) %collective-permute-start.9) | collective-permute-done | bytes 786464 | tf_op jit(solution)/shard_map/ppermute | solution.py:58
  113.9 2.7 collective-permute-start.12
  116.6 3.4 %collective-permute-start.4 = (bf16[16,2,32,768]{3,2,1,0:T(8,128)(2,1)S(1)}, bf16[16,2,32,768]{3,2,1,0:T(8,128)(2,1)S(1)}, u32[]{:S(2)}, u32[]{:S(2)}) collective-permute-start(bf16[16,2,32,768]{3,2,1,0:T(8,128)(2,1)S(1)} %all-to-all-done.1), channel_id=1, source_target_pairs={{0,1},{1,0},{2,3},{3,2},{4,5},{5,4},{6,7},{7,6},{8,9},{9,8},{10,11... | collective-permute-start | bytes 4718600 | tf_op jit(solution)/shard_map/ppermute | solution.py:63
  120.0 1.2 slice.16
  121.3 1.2 slice.17
  122.5 2.7 collective-permute-start.3
  126.1 15.6 %collective-permute-done.2 = bf16[8,2,32,768]{3,2,1,0:T(8,128)(2,1)S(1)} collective-permute-done((bf16[8,2,32,768]{3,2,1,0:T(8,128)(2,1)S(1)}, bf16[8,2,32,768]{3,2,1,0:T(8,128)(2,1)S(1)}, u32[]{:S(2)}, u32[]{:S(2)}) %collective-permute-start.2) | collective-permute-done | bytes 786464 | tf_op jit(solution)/shard_map/ppermute | solution.py:60
  144.2 1.2 copy-done.1
  148.9 1.4 copy-done.2
  154.8 12.5 %shard_map.158.hidden_ref = bf16[512,768]{1,0:T(8,128)(2,1)S(1)} custom-call(s32[2]{0:T(128)S(1)} %pad_add_fusion.place_ref, bf16[512,4096]{1,0:T(8,128)(2,1)} %bitcast.6.rows_ref, bf16[2,8,2,32,768]{4,3,2,1,0:T(8,128)(2,1)S(1)} %bitcast.105, bf16[2,8,2,32,768]{4,3,2,1,0:T(8,128)(2,1)} %bitcast.10.refs_1_, bf16[2,8,2,32,768]{4,3,2,1,0:T(8,128)(2,1)} %bitcast.11.refs_2_, ...), custom_call_target="tpu_custom_call" | custom-call | flops 6442450944 | bytes 16777216 | tf_op jit(solution)/shard_map/pallas_call | solution.py:120
  167.4 6.3 %shard_map.159 = bf16[512,4096]{1,0:T(8,128)(2,1)S(1)} custom-call(s32[2]{0:T(128)S(1)} %pad_add_fusion.place_ref, bf16[512,768]{1,0:T(8,128)(2,1)S(1)} %shard_map.158.hidden_ref, bf16[2,8,32,768]{3,2,1,0:T(8,128)(2,1)S(1)} %bitcast.106, bf16[2,8,32,768]{3,2,1,0:T(8,128)(2,1)S(1)} %bitcast.107, bf16[2,8,32,768]{3,2,1,0:T(8,128)(2,1)} %bitcast.22.refs_2_, ...), custom_call_target="tpu_custom_call" | custom-call | flops 3221225472 | bytes 10485760 | tf_op jit(solution)/shard_map/pallas_call | solution.py:161
  173.6 2.0 copy-done
  175.7 6.7 %all-to-all-start.3 = ((bf16[16,32,4096]{2,1,0:T(8,128)(2,1)}), bf16[16,32,4096]{2,1,0:T(8,128)(2,1)}, u32[]{:S(2)}, u32[]{:S(2)}) async-start(bf16[16,32,4096]{2,1,0:T(8,128)(2,1)} %bitcast.104), calls=%async_computation.3 | async-start | bytes 8388608 | tf_op jit(solution)/shard_map/all_to_all | solution.py:251
  182.7 66.6 %all-to-all-done.3 = bf16[16,32,4096]{2,1,0:T(8,128)(2,1)} async-done(((bf16[16,32,4096]{2,1,0:T(8,128)(2,1)}), bf16[16,32,4096]{2,1,0:T(8,128)(2,1)}, u32[]{:S(2)}, u32[]{:S(2)}) %all-to-all-start.3) | async-done | bytes 4194336 | tf_op jit(solution)/shard_map/all_to_all | solution.py:251
  249.3 3.1 %convolution_bitcast_fusion.1 = f32[64,4096]{1,0:T(8,128)S(1)} fusion(bf16[16,32,4096]{2,1,0:T(8,128)(2,1)} %all-to-all-done.3, f32[64,16]{0,1:T(8,128)S(1)} %select_reduce_fusion.1, s32[64,16]{0,1:T(8,128)S(1)} %copy.52, pred[64,16]{0,1:T(8,128)(4,1)S(1)} %fusion.34), kind=kOutput, calls=%fused_computation.12 | convolution fusion | flops 268533760 | bytes 5252096 | tf_op jit(solution)/shard_map/dot_general | solution.py:258
  252.4 3.6 %fusion.9 = bf16[64,4096]{1,0:T(8,128)(2,1)S(1)} fusion(f32[64,4096]{1,0:T(8,128)S(1)} %convolution_bitcast_fusion.1, bf16[16,32,4096]{2,1,0:T(8,128)(2,1)} %all-to-all-done.3, f32[8,8,32,128]{3,2,1,0:T(8,128)S(1)} %bitcast.118, bf16[64,4096]{1,0:T(8,128)(2,1)S(1)} %copy-done.17, f32[64,16]{0,1:T(8,128)S(1)} %select_reduce_fusion.1, ...), kind=kOutput, calls=%fused_computation.13 | convolution fusion | flops 269975552 | bytes 7349248 | tf_op jit(solution)/shard_map/dot_general | solution.py:258
  257.0 1.4 reduce
  259.2 26.9 %all_to_all.25 = bf16[128,2,2048]{2,1,0:T(2,128)(2,1)} all-to-all(bf16[128,2,2048]{2,1,0:T(2,128)(2,1)S(1)} %reshape.205), channel_id=1, replica_groups=mesh['ylo'=2,'z'=4,'x'=4,'yhi'=2,'core'=2] {'ylo','z','x','yhi','core'}, dimensions={0} | all-to-all | bytes 2097152 | tf_op jit(solution)/shard_map/all_to_all | solution.py:274
  286.1 6.5 %reshape.206 = bf16[128,1,4096]{2,1,0:T(2,128)(2,1)S(1)} reshape(bf16[128,2,2048]{2,1,0:T(2,128)(2,1)} %all_to_all.25) | data formatting | bytes 2097152
  292.6 2.1 copy.82
  (115 shorter events, 21.9 us)
Async XLA Ops:
  0.6 23.7 %all-to-all-start.2 = ((bf16[16,32,768]{2,1,0:T(8,128)(2,1)}), bf16[16,32,768]{2,1,0:T(8,128)(2,1)S(1)}, u32[]{:S(2)}, u32[]{:S(2)}) async-start(bf16[16,32,768]{2,1,0:T(8,128)(2,1)} %bitcast.122), calls=%async_computation.2 | async-start | bytes 1572864 | tf_op jit(solution)/shard_map/all_to_all | solution.py:207
  15.9 8.4 %copy-start.15 = (f32[64,2,16,256]{3,2,1,0:T(8,128)}, f32[64,2,16,256]{3,2,1,0:T(8,128)S(1)}, u32[]{:S(2)}) copy-start(f32[64,2,16,256]{3,2,1,0:T(8,128)S(1)} %get-tuple-element.5) | copy-start | bytes 6291460
  24.4 6.8 %copy-start.19 = (f32[64,2,128]{2,1,0:T(2,128)S(1)}, f32[64,2,128]{2,1,0:T(2,128)}, u32[]{:S(2)}) copy-start(f32[64,2,128]{2,1,0:T(2,128)} %reshape.198) | copy-start | bytes 196612
  24.4 29.0 %all-to-all-start.1 = ((bf16[16,2,32,768]{3,2,1,0:T(8,128)(2,1)}), bf16[16,2,32,768]{3,2,1,0:T(8,128)(2,1)S(1)}, u32[]{:S(2)}, u32[]{:S(2)}) async-start(bf16[16,2,32,768]{3,2,1,0:T(8,128)(2,1)} %pad_maximum_fusion), calls=%async_computation.1 | async-start | bytes 3145728 | tf_op jit(solution)/shard_map/all_to_all | solution.py:205
  53.4 95.5 %all-to-all-start = ((bf16[16,32,4096]{2,1,0:T(8,128)(2,1)}), bf16[16,32,4096]{2,1,0:T(8,128)(2,1)}, u32[]{:S(2)}, u32[]{:S(2)}) async-start(bf16[16,32,4096]{2,1,0:T(8,128)(2,1)} %bitcast.115), calls=%async_computation | async-start | bytes 8388608 | tf_op jit(solution)/shard_map/all_to_all | solution.py:241
  59.6 60.5 %collective-permute-start = (bf16[16,2,32,768]{3,2,1,0:T(8,128)(2,1)S(1)}, bf16[16,2,32,768]{3,2,1,0:T(8,128)(2,1)}, u32[]{:S(2)}, u32[]{:S(2)}) collective-permute-start(bf16[16,2,32,768]{3,2,1,0:T(8,128)(2,1)S(1)} %all-to-all-done.1), channel_id=1, source_target_pairs={{0,16},{16,32},{32,48},{48,0},{1,17},{17,33},{33,49},{49,1},{2,18}... | collective-permute-start | bytes 4718600 | tf_op jit(solution)/shard_map/ppermute | solution.py:58
  61.3 60.0 %collective-permute-start.1 = (bf16[16,2,32,768]{3,2,1,0:T(8,128)(2,1)S(1)}, bf16[16,2,32,768]{3,2,1,0:T(8,128)(2,1)}, u32[]{:S(2)}, u32[]{:S(2)}) collective-permute-start(bf16[16,2,32,768]{3,2,1,0:T(8,128)(2,1)S(1)} %all-to-all-done.1), channel_id=1, source_target_pairs={{0,48},{16,0},{32,16},{48,32},{1,49},{17,1},{33,17},{49,33},{2,50}... | collective-permute-start | bytes 4718600 | tf_op jit(solution)/shard_map/ppermute | solution.py:59
  63.5 49.3 %collective-permute-start.9 = (bf16[16,32,768]{2,1,0:T(8,128)(2,1)S(1)}, bf16[16,32,768]{2,1,0:T(8,128)(2,1)S(1)}, u32[]{:S(2)}, u32[]{:S(2)}) collective-permute-start(bf16[16,32,768]{2,1,0:T(8,128)(2,1)S(1)} %all-to-all-done.2), channel_id=1, source_target_pairs={{0,16},{16,32},{32,48},{48,0},{1,17},{17,33},{33,49},{49,1},{2,18}... | collective-permute-start | bytes 2359304 | tf_op jit(solution)/shard_map/ppermute | solution.py:58
  63.5 49.4 %collective-permute-start.10 = (bf16[16,32,768]{2,1,0:T(8,128)(2,1)S(1)}, bf16[16,32,768]{2,1,0:T(8,128)(2,1)}, u32[]{:S(2)}, u32[]{:S(2)}) collective-permute-start(bf16[16,32,768]{2,1,0:T(8,128)(2,1)S(1)} %all-to-all-done.2), channel_id=1, source_target_pairs={{0,48},{16,0},{32,16},{48,32},{1,49},{17,1},{33,17},{49,33},{2,50}... | collective-permute-start | bytes 2359304 | tf_op jit(solution)/shard_map/ppermute | solution.py:59
  112.8 12.4 %collective-permute-start.11 = (bf16[8,32,768]{2,1,0:T(8,128)(2,1)S(1)}, bf16[8,32,768]{2,1,0:T(8,128)(2,1)S(1)}, u32[]{:S(2)}, u32[]{:S(2)}) collective-permute-start(bf16[8,32,768]{2,1,0:T(8,128)(2,1)S(1)} %slice.18), channel_id=1, source_target_pairs={{0,16},{16,32},{32,48},{48,0},{1,17},{17,33},{33,49},{49,1},{2,18}... | collective-permute-start | bytes 1179656 | tf_op jit(solution)/shard_map/ppermute | solution.py:60
  113.9 11.9 %collective-permute-start.12 = (bf16[8,32,768]{2,1,0:T(8,128)(2,1)S(1)}, bf16[8,32,768]{2,1,0:T(8,128)(2,1)S(1)}, u32[]{:S(2)}, u32[]{:S(2)}) collective-permute-start(bf16[8,32,768]{2,1,0:T(8,128)(2,1)S(1)} %slice.19), channel_id=1, source_target_pairs={{0,48},{16,0},{32,16},{48,32},{1,49},{17,1},{33,17},{49,33},{2,50}... | collective-permute-start | bytes 1179656 | tf_op jit(solution)/shard_map/ppermute | solution.py:61
  116.6 27.6 %collective-permute-start.4 = (bf16[16,2,32,768]{3,2,1,0:T(8,128)(2,1)S(1)}, bf16[16,2,32,768]{3,2,1,0:T(8,128)(2,1)S(1)}, u32[]{:S(2)}, u32[]{:S(2)}) collective-permute-start(bf16[16,2,32,768]{3,2,1,0:T(8,128)(2,1)S(1)} %all-to-all-done.1), channel_id=1, source_target_pairs={{0,1},{1,0},{2,3},{3,2},{4,5},{5,4},{6,7},{7,6},{8,9},{9,8},{10,11... | collective-permute-start | bytes 4718600 | tf_op jit(solution)/shard_map/ppermute | solution.py:63
  121.2 20.5 %collective-permute-start.2 = (bf16[8,2,32,768]{3,2,1,0:T(8,128)(2,1)S(1)}, bf16[8,2,32,768]{3,2,1,0:T(8,128)(2,1)S(1)}, u32[]{:S(2)}, u32[]{:S(2)}) collective-permute-start(bf16[8,2,32,768]{3,2,1,0:T(8,128)(2,1)S(1)} %slice.16), channel_id=1, source_target_pairs={{0,16},{16,32},{32,48},{48,0},{1,17},{17,33},{33,49},{49,1},{2,18}... | collective-permute-start | bytes 2359304 | tf_op jit(solution)/shard_map/ppermute | solution.py:60
  122.5 20.8 %collective-permute-start.3 = (bf16[8,2,32,768]{3,2,1,0:T(8,128)(2,1)S(1)}, bf16[8,2,32,768]{3,2,1,0:T(8,128)(2,1)S(1)}, u32[]{:S(2)}, u32[]{:S(2)}) collective-permute-start(bf16[8,2,32,768]{3,2,1,0:T(8,128)(2,1)S(1)} %slice.17), channel_id=1, source_target_pairs={{0,48},{16,0},{32,16},{48,32},{1,49},{17,1},{33,17},{49,33},{2,50}... | collective-permute-start | bytes 2359304 | tf_op jit(solution)/shard_map/ppermute | solution.py:61
  125.2 23.1 %collective-permute-start.5 = (bf16[16,2,32,768]{3,2,1,0:T(8,128)(2,1)}, bf16[16,2,32,768]{3,2,1,0:T(8,128)(2,1)}, u32[]{:S(2)}, u32[]{:S(2)}) collective-permute-start(bf16[16,2,32,768]{3,2,1,0:T(8,128)(2,1)} %collective-permute-done), channel_id=1, source_target_pairs={{0,1},{1,0},{2,3},{3,2},{4,5},{5,4},{6,7},{7,6},{8,9},{9,8},{10,11... | collective-permute-start | bytes 4718600 | tf_op jit(solution)/shard_map/ppermute | solution.py:63
  125.8 21.0 %copy-start.11 = (bf16[8,32,768]{2,1,0:T(8,128)(2,1)}, bf16[8,32,768]{2,1,0:T(8,128)(2,1)S(1)}, u32[]{:S(2)}) copy-start(bf16[8,32,768]{2,1,0:T(8,128)(2,1)S(1)} %collective-permute-done.12) | copy-start | bytes 1179652
  125.8 22.6 %collective-permute-start.6 = (bf16[16,2,32,768]{3,2,1,0:T(8,128)(2,1)}, bf16[16,2,32,768]{3,2,1,0:T(8,128)(2,1)}, u32[]{:S(2)}, u32[]{:S(2)}) collective-permute-start(bf16[16,2,32,768]{3,2,1,0:T(8,128)(2,1)} %collective-permute-done.1), channel_id=1, source_target_pairs={{0,1},{1,0},{2,3},{3,2},{4,5},{5,4},{6,7},{7,6},{8,9},{9,8},{10,11... | collective-permute-start | bytes 4718600 | tf_op jit(solution)/shard_map/ppermute | solution.py:63
  141.7 4.2 %collective-permute-start.7 = (bf16[8,2,32,768]{3,2,1,0:T(8,128)(2,1)S(1)}, bf16[8,2,32,768]{3,2,1,0:T(8,128)(2,1)S(1)}, u32[]{:S(2)}, u32[]{:S(2)}) collective-permute-start(bf16[8,2,32,768]{3,2,1,0:T(8,128)(2,1)S(1)} %collective-permute-done.2), channel_id=1, source_target_pairs={{0,1},{1,0},{2,3},{3,2},{4,5},{5,4},{6,7},{7,6},{8,9},{9,8},{10,11... | collective-permute-start | bytes 2359304 | tf_op jit(solution)/shard_map/ppermute | solution.py:63
  143.3 3.5 %collective-permute-start.8 = (bf16[8,2,32,768]{3,2,1,0:T(8,128)(2,1)S(1)}, bf16[8,2,32,768]{3,2,1,0:T(8,128)(2,1)S(1)}, u32[]{:S(2)}, u32[]{:S(2)}) collective-permute-start(bf16[8,2,32,768]{3,2,1,0:T(8,128)(2,1)S(1)} %collective-permute-done.3), channel_id=1, source_target_pairs={{0,1},{1,0},{2,3},{3,2},{4,5},{5,4},{6,7},{7,6},{8,9},{9,8},{10,11... | collective-permute-start | bytes 2359304 | tf_op jit(solution)/shard_map/ppermute | solution.py:63
  145.4 21.9 %collective-permute-start.13 = (bf16[16,32,768]{2,1,0:T(8,128)(2,1)S(1)}, bf16[16,32,768]{2,1,0:T(8,128)(2,1)}, u32[]{:S(2)}, u32[]{:S(2)}) collective-permute-start(bf16[16,32,768]{2,1,0:T(8,128)(2,1)S(1)} %all-to-all-done.2), channel_id=1, source_target_pairs={{0,1},{1,0},{2,3},{3,2},{4,5},{5,4},{6,7},{7,6},{8,9},{9,8},{10,11... | collective-permute-start | bytes 2359304 | tf_op jit(solution)/shard_map/ppermute | solution.py:63
  146.8 20.5 %collective-permute-start.14 = (bf16[16,32,768]{2,1,0:T(8,128)(2,1)S(1)}, bf16[16,32,768]{2,1,0:T(8,128)(2,1)}, u32[]{:S(2)}, u32[]{:S(2)}) collective-permute-start(bf16[16,32,768]{2,1,0:T(8,128)(2,1)S(1)} %collective-permute-done.9), channel_id=1, source_target_pairs={{0,1},{1,0},{2,3},{3,2},{4,5},{5,4},{6,7},{7,6},{8,9},{9,8},{10,11... | collective-permute-start | bytes 2359304 | tf_op jit(solution)/shard_map/ppermute | solution.py:63
  147.8 19.6 %collective-permute-start.15 = (bf16[16,32,768]{2,1,0:T(8,128)(2,1)}, bf16[16,32,768]{2,1,0:T(8,128)(2,1)}, u32[]{:S(2)}, u32[]{:S(2)}) collective-permute-start(bf16[16,32,768]{2,1,0:T(8,128)(2,1)} %collective-permute-done.10), channel_id=1, source_target_pairs={{0,1},{1,0},{2,3},{3,2},{4,5},{5,4},{6,7},{7,6},{8,9},{9,8},{10,11... | collective-permute-start | bytes 2359304 | tf_op jit(solution)/shard_map/ppermute | solution.py:63
  148.3 19.0 %collective-permute-start.16 = (bf16[8,32,768]{2,1,0:T(8,128)(2,1)S(1)}, bf16[8,32,768]{2,1,0:T(8,128)(2,1)}, u32[]{:S(2)}, u32[]{:S(2)}) collective-permute-start(bf16[8,32,768]{2,1,0:T(8,128)(2,1)S(1)} %collective-permute-done.11), channel_id=1, source_target_pairs={{0,1},{1,0},{2,3},{3,2},{4,5},{5,4},{6,7},{7,6},{8,9},{9,8},{10,11... | collective-permute-start | bytes 1179656 | tf_op jit(solution)/shard_map/ppermute | solution.py:63
  148.4 18.9 %collective-permute-start.17 = (bf16[8,32,768]{2,1,0:T(8,128)(2,1)}, bf16[8,32,768]{2,1,0:T(8,128)(2,1)}, u32[]{:S(2)}, u32[]{:S(2)}) collective-permute-start(bf16[8,32,768]{2,1,0:T(8,128)(2,1)} %copy-done.11), channel_id=1, source_target_pairs={{0,1},{1,0},{2,3},{3,2},{4,5},{5,4},{6,7},{7,6},{8,9},{9,8},{10,11... | collective-permute-start | bytes 1179656 | tf_op jit(solution)/shard_map/ppermute | solution.py:63
  154.8 12.5 %copy-start.12 = (bf16[8,32,768]{2,1,0:T(8,128)(2,1)S(1)}, bf16[8,32,768]{2,1,0:T(8,128)(2,1)}, u32[]{:S(2)}) copy-start(bf16[8,32,768]{2,1,0:T(8,128)(2,1)} %copy-done.11) | copy-start | bytes 1179652
  175.6 6.8 %copy-start.27 = (s32[64]{0:T(128)S(1)}, s32[64]{0:T(128)}, u32[]{:S(2)}) copy-start(s32[64]{0:T(128)} %param.25) | copy-start | bytes 772
  175.6 6.8 %copy-start.26 = (s32[64]{0:T(128)S(1)}, s32[64]{0:T(128)}, u32[]{:S(2)}) copy-start(s32[64]{0:T(128)} %param.26) | copy-start | bytes 772
  175.7 7.0 %copy-start.24 = (s32[64,8]{0,1:T(8,128)S(1)}, s32[64,8]{0,1:T(8,128)}, u32[]{:S(2)}) copy-start(s32[64,8]{0,1:T(8,128)} %param.23) | copy-start | bytes 6148
  175.7 7.0 %copy-start.25 = (f32[64,8]{0,1:T(8,128)S(1)}, f32[64,8]{0,1:T(8,128)}, u32[]{:S(2)}) copy-start(f32[64,8]{0,1:T(8,128)} %param.24) | copy-start | bytes 6148
  175.7 73.6 %all-to-all-start.3 = ((bf16[16,32,4096]{2,1,0:T(8,128)(2,1)}), bf16[16,32,4096]{2,1,0:T(8,128)(2,1)}, u32[]{:S(2)}, u32[]{:S(2)}) async-start(bf16[16,32,4096]{2,1,0:T(8,128)(2,1)} %bitcast.104), calls=%async_computation.3 | async-start | bytes 8388608 | tf_op jit(solution)/shard_map/all_to_all | solution.py:251
  182.7 69.7 %copy-start.14 = (f32[64,2,16,128]{3,2,1,0:T(8,128)S(1)}, f32[64,2,16,128]{3,2,1,0:T(8,128)}, u32[]{:S(2)}) copy-start(f32[64,2,16,128]{3,2,1,0:T(8,128)} %copy-done.13) | copy-start | bytes 3145732
  182.7 69.7 %copy-start.17 = (bf16[64,4096]{1,0:T(8,128)(2,1)S(1)}, bf16[64,4096]{1,0:T(8,128)(2,1)}, u32[]{:S(2)}) copy-start(bf16[64,4096]{1,0:T(8,128)(2,1)} %param.15) | copy-start | bytes 1572868
  (18 other events, 40.6 us)

commit v2 on v1

v2 whole, which is shorter than its diff:
```python
import functools
import math

import jax
import jax.numpy as jnp
from jax import lax
from jax.experimental import pallas as pl
from jax.experimental.pallas import tpu as pltpu
from jax.sharding import Mesh
from jax.sharding import PartitionSpec as P

HDIM = 128
QHEADS = 32
KVHEADS = 2

AXES = ("ylo", "z", "x", "yhi", "core")
PLANE = ("ylo", "x", "yhi")
RING = 4
ZUP = [(i, (i + 1) % RING) for i in range(RING)]
ZDOWN = [(i, (i - 1) % RING) for i in range(RING)]
SWAP = [(0, 1), (1, 0)]
LINE = 128
LINES = 32
MIB = 1024 * 1024


def attend_rows(queries, key_cache, value_cache, new_keys, new_values, cache_lengths):
    row_total = queries.shape[0]
    context = key_cache.shape[1]
    per_group = QHEADS // KVHEADS
    query_parts = queries.reshape(row_total, KVHEADS, per_group, HDIM)
    key_parts = key_cache.reshape(row_total, context, KVHEADS, HDIM)
    value_parts = value_cache.reshape(row_total, context, KVHEADS, HDIM)
    fresh_key = new_keys.reshape(row_total, KVHEADS, HDIM)
    fresh_value = new_values.astype(jnp.float32).reshape(row_total, KVHEADS, HDIM)
    scaling = 1.0 / math.sqrt(HDIM)
    cached = (
        jnp.einsum("nkgd,nckd->nkgc", query_parts, key_parts, preferred_element_type=jnp.float32)
        * scaling
    )
    usable = jnp.arange(context)[None, :] < cache_lengths[:, None]
    cached = jnp.where(usable[:, None, None, :], cached, -jnp.inf)
    own_score = (
        jnp.einsum("nkgd,nkd->nkg", query_parts, fresh_key, preferred_element_type=jnp.float32)
        * scaling
    )
    highest = jnp.maximum(jnp.max(cached, axis=-1), own_score)
    cached_exp = jnp.exp(cached - highest[..., None])
    own_exp = jnp.exp(own_score - highest)
    totals = jnp.sum(cached_exp, axis=-1) + own_exp
    cached_prob = (cached_exp / totals[..., None]).astype(jnp.bfloat16)
    own_prob = (own_exp / totals).astype(jnp.bfloat16).astype(jnp.float32)
    mixture = jnp.einsum(
        "nkgc,nckd->nkgd", cached_prob, value_parts, preferred_element_type=jnp.float32
    )
    mixture = mixture + own_prob[..., None] * fresh_value[:, :, None, :]
    return mixture.reshape(row_total, QHEADS * HDIM)


def spread_piece(piece, way):
    half = piece.shape[0] // 2
    prev = lax.ppermute(piece, "z", ZUP)
    succ = lax.ppermute(piece, "z", ZDOWN)
    if way > 0:
        far = [lax.ppermute(prev, "z", ZUP)]
    elif way < 0:
        far = [lax.ppermute(succ, "z", ZDOWN)]
    else:
        far = [
            lax.ppermute(prev[:half], "z", ZUP),
            lax.ppermute(succ[half:], "z", ZDOWN),
        ]
    mine = [piece, prev, succ] + far
    other = [lax.ppermute(part, "core", SWAP) for part in mine]
    return [part.reshape(-1, 8, 32, part.shape[-1]) for part in mine + other]


def place_copies(place_ref, parts, scratch, sem):
    z = place_ref[0]
    core = place_ref[1]
    count = len(parts) // 2
    copies = []
    for index, part in enumerate(parts):
        which = index % count
        c = core if index < count else 1 - core
        zz = lax.rem(z + (0, RING - 1, 1, 2, 2)[which], RING)
        for lo in range(part.shape[0]):
            low = lo if which != 4 else 1
            copies.append(pltpu.make_async_copy(part.at[lo], scratch.at[low, zz, :, c], sem))
    return copies


def hidden_kernel(gate_count, place_ref, rows_any, *refs):
    gate_parts = refs[:gate_count]
    up_parts = refs[gate_count:-6]
    out_ref, rows_ref, gate_ref, up_ref, acc_ref, sem = refs[-6:]
    rows_copy = pltpu.make_async_copy(rows_any, rows_ref, sem.at[2])
    rows_copy.start()
    gate_copies = place_copies(place_ref, gate_parts, gate_ref, sem.at[0])
    up_copies = place_copies(place_ref, up_parts, up_ref, sem.at[1])
    for copy in gate_copies + up_copies:
        copy.start()
    rows_copy.wait()
    for copy in gate_copies:
        copy.wait()
    depth = rows_ref.shape[1]
    width = out_ref.shape[1]
    step = 256

    @pl.loop(0, width // step)
    def _(i):
        cols = pl.ds(pl.multiple_of(i * step, step), step)
        gate = gate_ref[:, :, :, :, :, cols].reshape(depth, step)
        g = jnp.dot(rows_ref[...], gate, preferred_element_type=jnp.float32)
        acc_ref[:, cols] = g / (1.0 + jnp.exp(-g))

    for copy in up_copies:
        copy.wait()

    @pl.loop(0, width // step)
    def _(i):
        cols = pl.ds(pl.multiple_of(i * step, step), step)
        up = up_ref[:, :, :, :, :, cols].reshape(depth, step)
        u = jnp.dot(rows_ref[...], up, preferred_element_type=jnp.float32)
        out_ref[:, cols] = (acc_ref[:, cols] * u).astype(out_ref.dtype)


def hidden_call(place, rows, gate_parts, up_parts):
    count, depth = rows.shape
    width = gate_parts[0].shape[-1]
    hbm = pl.BlockSpec(memory_space=pl.ANY)
    weight = pltpu.VMEM((2, RING, 8, 2, 32, width), jnp.bfloat16)
    return pl.pallas_call(
        functools.partial(hidden_kernel, len(gate_parts)),
        out_shape=jax.ShapeDtypeStruct((count, width), jnp.bfloat16),
        in_specs=[pl.BlockSpec(memory_space=pltpu.SMEM)]
        + [hbm] * (1 + len(gate_parts) + len(up_parts)),
        out_specs=pl.BlockSpec(memory_space=pltpu.VMEM),
        scratch_shapes=[
            pltpu.VMEM((count, depth), jnp.bfloat16),
            weight,
            weight,
            pltpu.VMEM((count, width), jnp.float32),
            pltpu.SemaphoreType.DMA((3,)),
        ],
        compiler_params=pltpu.CompilerParams(vmem_limit_bytes=24 * MIB),
        cost_estimate=pl.CostEstimate(
            flops=4 * count * depth * width,
            bytes_accessed=4 * depth * width + 2 * count * depth,
            transcendentals=count * width,
        ),
        name="hidden",
    )(place, rows, *gate_parts, *up_parts)


def project_kernel(place_ref, hidden_ref, *refs):
    parts = refs[:-5]
    out_any, scratch, out_ref, sem, out_sem = refs[-5:]
    copies = place_copies(place_ref, parts, scratch, sem)
    for copy in copies:
        copy.start()
    for copy in copies:
        copy.wait()
    hidden = hidden_ref[...]
    outs = []
    for chunk in range(2 * RING):
        weight = scratch[chunk // RING, chunk % RING].reshape(512, hidden.shape[1])
        cols = slice(chunk * 512, (chunk + 1) * 512)
        out_ref[:, cols] = lax.dot_general(
            hidden, weight, (((1,), (1,)), ((), ())), preferred_element_type=jnp.float32
        ).astype(out_ref.dtype)
        out = pltpu.make_async_copy(out_ref.at[:, cols], out_any.at[:, cols], out_sem.at[chunk])
        out.start()
        outs.append(out)
    for out in outs:
        out.wait()


def project_call(place, hidden, parts):
    count, width = hidden.shape
    depth = 4096
    hbm = pl.BlockSpec(memory_space=pl.ANY)
    return pl.pallas_call(
        project_kernel,
        out_shape=jax.ShapeDtypeStruct((count, depth), jnp.bfloat16),
        in_specs=[
            pl.BlockSpec(memory_space=pltpu.SMEM),
            pl.BlockSpec(memory_space=pltpu.VMEM),
        ]
        + [hbm] * len(parts),
        out_specs=hbm,
        scratch_shapes=[
            pltpu.VMEM((2, RING, 8, 2, 32, width), jnp.bfloat16),
            pltpu.VMEM((count, depth), jnp.bfloat16),
            pltpu.SemaphoreType.DMA,
            pltpu.SemaphoreType.DMA((2 * RING,)),
        ],
        compiler_params=pltpu.CompilerParams(vmem_limit_bytes=18 * MIB),
        cost_estimate=pl.CostEstimate(
            flops=2 * count * depth * width,
            bytes_accessed=2 * depth * width + 2 * count * depth,
            transcendentals=0,
        ),
        name="project",
    )(place, hidden, *parts)


def combine_kernel(high_ref, low_ref, picked_ref, middle_ref, back_ref, layer_ref, parcel_ref, rows_ref):
    step = pl.program_id(0)
    back = back_ref[...]
    routed = jnp.dot(high_ref[...], back, preferred_element_type=jnp.float32) + jnp.dot(
        low_ref[...], back, preferred_element_type=jnp.float32
    )
    layer = (middle_ref[...] + routed).astype(jnp.bfloat16)
    layer_ref[...] = layer
    lines = picked_ref.shape[0]
    taken = jnp.dot(picked_ref[...], layer, preferred_element_type=jnp.float32)
    per_step = layer.shape[1] // LINE
    for part in range(per_step):
        rows_ref[pl.ds(step * per_step + part, lines, stride=LINES), :] = taken[
            :, part * LINE : (part + 1) * LINE
        ]

    @pl.when(step == pl.num_programs(0) - 1)
    def _():
        parcel_ref[...] = rows_ref[...].reshape(parcel_ref.shape).astype(parcel_ref.dtype)


def combine_call(high, low, picked, middle, back):
    rows, width = middle.shape
    slots = back.shape[0]
    learners = picked.shape[0]
    step = 512
    whole = lambda shape: pl.BlockSpec(shape, lambda i: (0,) * len(shape))
    column = lambda count: pl.BlockSpec((count, step), lambda i: (0, i))
    return pl.pallas_call(
        combine_kernel,
        grid=(width // step,),
        out_shape=(
            jax.ShapeDtypeStruct((rows, width), jnp.bfloat16),
            jax.ShapeDtypeStruct((learners, LINES, LINE), jnp.bfloat16),
        ),
        in_specs=[
            whole((rows, slots)),
            whole((rows, slots)),
            whole((learners, rows)),
            column(rows),
            column(slots),
        ],
        out_specs=(column(rows), whole((learners, LINES, LINE))),
        scratch_shapes=[pltpu.VMEM((learners * LINES, LINE), jnp.float32)],
        compiler_params=pltpu.CompilerParams(vmem_limit_bytes=16 * MIB),
        name="combine",
    )(high, low, picked, middle, back)


def unpack_kernel(lines_ref, out_ref, rows_ref):
    count = lines_ref.shape[0]
    rows_ref[...] = lines_ref[...].reshape(rows_ref.shape).astype(jnp.float32)
    for part in range(LINES):
        out_ref[:, part * LINE : (part + 1) * LINE] = rows_ref[
            pl.ds(part, count, stride=LINES), :
        ].astype(out_ref.dtype)


def unpack_call(lines):
    count = lines.shape[0]
    vmem = pl.BlockSpec(memory_space=pltpu.VMEM)
    return pl.pallas_call(
        unpack_kernel,
        out_shape=jax.ShapeDtypeStruct((count, LINES * LINE), jnp.bfloat16),
        in_specs=[vmem],
        out_specs=vmem,
        scratch_shapes=[pltpu.VMEM((count * LINES, LINE), jnp.float32)],
        compiler_params=pltpu.CompilerParams(vmem_limit_bytes=16 * MIB),
        name="unpack",
    )(lines)


def shards(
    hidden_states,
    queries,
    key_cache,
    value_cache,
    new_keys,
    new_values,
    cache_lengths,
    norm_gain,
    expert_ids,
    route_weights,
    finished,
    learner_ids,
    gate_weight,
    up_weight,
    down_weight,
):
    experts = 16
    learners = 128
    row_count, model_width = hidden_states.shape
    capacity = row_count // 2
    slots = experts * capacity
    place = jnp.stack([lax.axis_index("z"), lax.axis_index("core")]).astype(jnp.int32)

    to_chip = lambda part: lax.all_to_all(part, PLANE, split_axis=0, concat_axis=0, tiled=True)
    gate = to_chip(gate_weight)
    up = to_chip(up_weight)
    down = to_chip(jnp.swapaxes(down_weight, 1, 2))
    gate_parts = spread_piece(gate, 1)
    up_parts = spread_piece(up, -1)
    down_parts = spread_piece(down, 0)

    queries, _ = lax.optimization_barrier((queries, gate))
    attended = attend_rows(queries, key_cache, value_cache, new_keys, new_values, cache_lengths)
    middle = hidden_states.astype(jnp.float32) + attended
    spread = jnp.mean(middle * middle, axis=-1, keepdims=True)
    normed = (middle * lax.rsqrt(spread + 1e-06) * norm_gain).astype(jnp.bfloat16)

    expert_range = jnp.arange(experts, dtype=jnp.int32)
    hit_table = expert_ids[:, :, None] == expert_range[None, None, :]
    matched = jnp.any(hit_table, axis=1)
    slot_gate = jnp.sum(jnp.where(hit_table, route_weights[:, :, None], 0.0), axis=1)
    row_range = jnp.arange(row_count, dtype=jnp.int32)
    earlier = row_range[None, :] < row_range[:, None]
    slot_rank = jnp.sum(
        jnp.where(earlier[:, :, None] & matched[None, :, :], 1, 0).astype(jnp.int32), axis=1
    )
    slot_range = jnp.arange(capacity, dtype=jnp.int32)
    chosen = matched[:, :, None] & (slot_rank[:, :, None] == slot_range[None, None, :])
    pick = chosen.reshape(row_count, slots).astype(jnp.bfloat16)
    weigh = jnp.where(chosen, slot_gate[:, :, None], 0.0).reshape(row_count, slots)
    weigh_high = weigh.astype(jnp.bfloat16)
    weigh_low = (weigh - weigh_high.astype(jnp.float32)).astype(jnp.bfloat16)

    outgoing = lax.dot_general(
        pick, normed, (((0,), (0,)), ((), ())), preferred_element_type=jnp.float32
    ).astype(jnp.bfloat16)
    outgoing, _, _, _ = lax.optimization_barrier((outgoing, gate_parts[1], gate_parts[2], down))
    received = lax.all_to_all(
        outgoing.reshape(experts, capacity, model_width),
        PLANE,
        split_axis=0,
        concat_axis=0,
        tiled=True,
    ).reshape(slots, model_width)

    hidden = hidden_call(place, received, gate_parts, up_parts)
    expert_out = project_call(place, hidden, down_parts)
    returned = lax.all_to_all(
        expert_out.reshape(experts, capacity, model_width),
        PLANE,
        split_axis=0,
        concat_axis=0,
        tiled=True,
    ).reshape(slots, model_width)

    finished_rows = finished > 0
    same_target = (learner_ids[:, None] == learner_ids[None, :]) & finished_rows[None, :] & earlier
    learner_rank = jnp.sum(same_target.astype(jnp.int32), axis=1)
    slot_of_row = learner_ids + learner_rank
    slot_span = jnp.arange(learners, dtype=jnp.int32)
    picked = finished_rows[None, :] & (slot_of_row[None, :] == slot_span[:, None])
    layer_out, parcel = combine_call(
        weigh_high, weigh_low, picked.astype(jnp.bfloat16), middle, returned
    )
    arrived = lax.all_to_all(parcel, AXES, split_axis=0, concat_axis=0, tiled=True)
    return (layer_out, unpack_call(arrived))


def solution(mesh):
    fine = Mesh(mesh.devices.reshape(2, 4, 4, 2, 2), AXES)
    rows = P(AXES)
    placed = (
        P(AXES, None),
        P(AXES, None),
        P(AXES, None, None),
        P(AXES, None, None),
        P(AXES, None),
        P(AXES, None),
        P(AXES),
        P(),
        P(AXES, None),
        P(AXES, None),
        P(AXES),
        P(AXES),
        P(None, AXES, None),
        P(None, AXES, None),
        P(None, None, AXES),
    )
    return jax.shard_map(
        shards,
        mesh=fine,
        in_specs=placed,
        out_specs=(P(AXES, None), P(AXES, None)),
        check_vma=False,
    )
```

time: 296 us -> 292 us (0.986)
  Pallas kernels: 18.7 us -> 31.3 us
  waiting for transfers between devices: 142 us -> 130 us
  local copies, waits for them, and re-layouts: 29.5 us -> 20.6 us
  starting transfers between devices: 46.1 us -> 54.2 us
  matrix products: 22.6 us -> 17.3 us
    ppermute x2 -> x3, waiting for transfers between devices: 46.6 us -> 2.28 us  [spread_piece(): prev = lax.ppermute(piece, 'z', ZUP)]
    ppermute x2 -> x3, waiting for transfers between devices: 0.01 us -> 26 us  [spread_piece(): succ = lax.ppermute(piece, 'z', ZDOWN)]
    pallas_call x1 -> x3, Pallas kernels: 12.5 us -> 22.2 us  [the longest x1 11.4 us: hidden_call(): pl.pallas_call(functools.partial(hidden_kernel, len(gate_parts)), out_sha...]
    dot_general x3 -> x0, matrix products: 7.1 us -> none  [the longest x1 3.61 us: shards(): jnp.dot(weigh_low, returned, preferred_element_type=jnp.float32)]
    unnamed x60 -> x53, local copies, waits for them, and re-layouts: 23.5 us -> 17.4 us
    all_to_all x2 -> x3, starting transfers between devices: 14.4 us -> 19.2 us  [shards(): lax.all_to_all(part, PLANE, split_axis=0, concat_axis=0, tiled=True)]
    ppermute x4, waiting for transfers between devices: 15.6 us -> 19.3 us  [the longest x1 19.3 us: spread_piece(): lax.ppermute(prev[:half], 'z', ZUP)]
    ppermute x10 -> x13, starting transfers between devices: 6.55 us -> 9.8 us  [spread_piece(): other = [lax.ppermute(part, 'core', SWAP) for part in mine]]
  transfers between devices with their start and end apart: 22 -> 28, of which waited for: 4 -> 8; matrix products, arithmetic and copies ran while one was open for 10% -> 10% of each run, Pallas kernels for 4% -> 4%
where the time goes in v2:
time: 292 us; the launch traced here: 291 us
  waiting for transfers between devices  130 us (45%)
  starting transfers between devices  54.2 us (19%)
  Pallas kernels  31.3 us (11%)
  blocking collectives  28.1 us (10%)
  local copies, waits for them, and re-layouts  20.6 us (7%)
  matrix products  17.3 us (6%)
  other arithmetic  7.76 us (3%)
    all_to_all x1, waiting for transfers between devices, shards(): lax.all_to_all(expert_out.reshape(experts, capacity, model_width), PLANE,...  66.2 us
    all_to_all x1, blocking collectives, shards(): lax.all_to_all(parcel, AXES, split_axis=0, concat_axis=0, tiled=True)  28.1 us
    ppermute x3, waiting for transfers between devices, spread_piece(): succ = lax.ppermute(piece, 'z', ZDOWN)  26 us
    ppermute x1, waiting for transfers between devices, spread_piece(): lax.ppermute(prev[:half], 'z', ZUP)  19.3 us
    all_to_all x3, starting transfers between devices, shards(): lax.all_to_all(part, PLANE, split_axis=0, concat_axis=0, tiled=True)  19.2 us
    unnamed x53, local copies, waits for them, and re-layouts  17.4 us
    all_to_all x3, waiting for transfers between devices, shards(): lax.all_to_all(part, PLANE, split_axis=0, concat_axis=0, tiled=True)  15.4 us
    pallas_call x1, Pallas kernels, hidden_call(): pl.pallas_call(functools.partial(hidden_kernel, len(gate_parts)), out_sha...  11.4 us
  transfers between devices with their start and end apart: 28, of which 8 were waited for; matrix products, arithmetic and copies ran while one was open for 10% of the time, Pallas kernels for 4%

profile of v2, /device:TPU:1, one launch (start us, length us, event | category | flops | bytes accessed | tf_op | source)
XLA Modules:
  0.0 290.6 jit_solution(2889925857866246860)
XLA Ops:
  0.7 7.7 %all-to-all-start = ((bf16[16,32,768]{2,1,0:T(8,128)(2,1)}), bf16[16,32,768]{2,1,0:T(8,128)(2,1)S(1)}, u32[]{:S(2)}, u32[]{:S(2)}) async-start(bf16[16,32,768]{2,1,0:T(8,128)(2,1)} %param.27), calls=%async_computation | async-start | bytes 1572864 | tf_op jit(solution)/shard_map/all_to_all | solution.py:304
  11.9 9.5 %all-to-all-done = bf16[16,32,768]{2,1,0:T(8,128)(2,1)S(1)} async-done(((bf16[16,32,768]{2,1,0:T(8,128)(2,1)}), bf16[16,32,768]{2,1,0:T(8,128)(2,1)S(1)}, u32[]{:S(2)}, u32[]{:S(2)}) %all-to-all-start) | async-done | bytes 786464 | tf_op jit(solution)/shard_map/all_to_all | solution.py:304
  21.4 4.6 %all-to-all-start.1 = ((bf16[16,32,768]{2,1,0:T(8,128)(2,1)}), bf16[16,32,768]{2,1,0:T(8,128)(2,1)S(1)}, u32[]{:S(2)}, u32[]{:S(2)}) async-start(bf16[16,32,768]{2,1,0:T(8,128)(2,1)} %bitcast.8), calls=%async_computation.1 | async-start | bytes 1572864 | tf_op jit(solution)/shard_map/all_to_all | solution.py:304
  26.7 7.1 %fusion.6 = (f32[64,2,16]{2,1,0:T(2,128)S(1)}, f32[64,2,16,256]{3,2,1,0:T(8,128)}) fusion(pred[64,256]{1,0:T(8,128)(4,1)S(1)} %iota_compare_fusion, bf16[64,2,16,128]{3,2,1,0:T(8,128)(2,1)S(1)} %bitcast.96, bf16[64,256,256]{2,1,0:T(8,128)(2,1)} %param.17), kind=kOutput, calls=%fused_computation.10 | convolution fusion | flops 135788544 | bytes 11034624 | tf_op jit(solution)/shard_map/nkgd,nckd->nkgc/dot_general | solution.py:38
  33.9 2.4 fusion.7
  36.7 1.7 collective-permute-start
  38.4 2.2 collective-permute-start.1
  40.6 6.4 %fusion.8 = f32[64,2,16,128]{3,2,1,0:T(8,128)} fusion(f32[64,2,16,256]{3,2,1,0:T(8,128)} %get-tuple-element.17, f32[64,2,16]{2,1,0:T(2,128)S(1)} %copy.52, f32[64,2,16]{2,1,0:T(2,128)S(1)} %copy.50, pred[64,256]{1,0:T(8,128)(4,1)S(1)} %iota_compare_fusion, f32[64,2,128]{2,1,0:T(2,128)S(1)} %reshape.205, f32[64,2,16]{2,1,0:T(2,128)S(1)} %copy.54, ...), kind=kOutput, calls=%fused_computation.12 | convolution fusion | flops 137363456 | bytes 11640832 | tf_op jit(solution)/shard_map/nkgc,nckd->nkgd/dot_general | solution.py:53
  47.0 6.8 %all-to-all-start.3 = ((bf16[16,32,768]{2,1,0:T(8,128)(2,1)}), bf16[16,32,768]{2,1,0:T(8,128)(2,1)S(1)}, u32[]{:S(2)}, u32[]{:S(2)}) async-start(bf16[16,32,768]{2,1,0:T(8,128)(2,1)} %param.28), calls=%async_computation.3 | async-start | bytes 1572864 | tf_op jit(solution)/shard_map/all_to_all | solution.py:304
  53.8 2.2 multiply_reduce_fusion
  56.0 3.4 %convolution_convert_fusion = bf16[512,4096]{1,0:T(8,128)(2,1)} fusion(pred[64,512]{1,0:T(32,128)(4,1)S(1)} %get-tuple-element.13, f32[64,4096]{1,0:T(8,128)S(1)} %get-tuple-element.11.middle_ref, f32[4096]{0:T(1024)S(1)} %copy-done.22, f32[64]{0:T(128)S(1)} %add_rsqrt_fusion), kind=kOutput, calls=%fused_computation.6 | convolution fusion | flops 271319040 | bytes 5292288 | tf_op jit(solution)/shard_map/dot_general | solution.py:334
  59.4 5.9 %all-to-all-done.3 = bf16[16,32,768]{2,1,0:T(8,128)(2,1)S(1)} async-done(((bf16[16,32,768]{2,1,0:T(8,128)(2,1)}), bf16[16,32,768]{2,1,0:T(8,128)(2,1)S(1)}, u32[]{:S(2)}, u32[]{:S(2)}) %all-to-all-start.3) | async-done | bytes 786464 | tf_op jit(solution)/shard_map/all_to_all | solution.py:304
  65.2 5.1 %all-to-all-start.2 = ((bf16[16,32,4096]{2,1,0:T(8,128)(2,1)}), bf16[16,32,4096]{2,1,0:T(8,128)(2,1)}, u32[]{:S(2)}, u32[]{:S(2)}) async-start(bf16[16,32,4096]{2,1,0:T(8,128)(2,1)} %bitcast.94), calls=%async_computation.2 | async-start | bytes 8388608 | tf_op jit(solution)/shard_map/all_to_all | solution.py:338
  70.3 3.3 %collective-permute-start.3 = (bf16[16,32,768]{2,1,0:T(8,128)(2,1)S(1)}, bf16[16,32,768]{2,1,0:T(8,128)(2,1)S(1)}, u32[]{:S(2)}, u32[]{:S(2)}) collective-permute-start(bf16[16,32,768]{2,1,0:T(8,128)(2,1)S(1)} %all-to-all-done), channel_id=1, source_target_pairs={{0,1},{1,0},{2,3},{3,2},{4,5},{5,4},{6,7},{7,6},{8,9},{9,8},{10,11... | collective-permute-start | bytes 2359304 | tf_op jit(solution)/shard_map/ppermute | solution.py:74
  73.7 1.4 collective-permute-start.8
  75.1 2.6 collective-permute-start.15
  79.5 13.3 %collective-permute-done.8 = bf16[16,32,768]{2,1,0:T(8,128)(2,1)S(1)} collective-permute-done((bf16[16,32,768]{2,1,0:T(8,128)(2,1)S(1)}, bf16[16,32,768]{2,1,0:T(8,128)(2,1)S(1)}, u32[]{:S(2)}, u32[]{:S(2)}) %collective-permute-start.8) | collective-permute-done | bytes 786464 | tf_op jit(solution)/shard_map/ppermute | solution.py:63
  92.9 2.3 collective-permute-done.14
  95.2 2.0 collective-permute-start.4
  97.1 12.6 %collective-permute-done.15 = bf16[16,32,768]{2,1,0:T(8,128)(2,1)} collective-permute-done((bf16[16,32,768]{2,1,0:T(8,128)(2,1)S(1)}, bf16[16,32,768]{2,1,0:T(8,128)(2,1)}, u32[]{:S(2)}, u32[]{:S(2)}) %collective-permute-start.15) | collective-permute-done | bytes 786464 | tf_op jit(solution)/shard_map/ppermute | solution.py:63
  109.7 2.6 collective-permute-start.9
  115.3 2.7 collective-permute-start.17
  118.0 19.3 %collective-permute-done.16 = bf16[8,32,768]{2,1,0:T(8,128)(2,1)} collective-permute-done((bf16[8,32,768]{2,1,0:T(8,128)(2,1)S(1)}, bf16[8,32,768]{2,1,0:T(8,128)(2,1)}, u32[]{:S(2)}, u32[]{:S(2)}) %collective-permute-start.16) | collective-permute-done | bytes 393248 | tf_op jit(solution)/shard_map/ppermute | solution.py:70
  145.1 1.2 collective-permute-done.13
  155.8 11.4 %hidden.1.hidden_ref = bf16[512,768]{1,0:T(8,128)(2,1)S(1)} custom-call(s32[2]{0:T(128)S(1)} %pad_add_fusion.place_ref, bf16[512,4096]{1,0:T(8,128)(2,1)} %bitcast.10.rows_any, bf16[2,8,32,768]{3,2,1,0:T(8,128)(2,1)S(1)} %bitcast.83, bf16[2,8,32,768]{3,2,1,0:T(8,128)(2,1)} %bitcast.6.refs_1_, bf16[2,8,32,768]{3,2,1,0:T(8,128)(2,1)} %bitcast.7.refs_2_, ...), custom_call_target="tpu_custom_call" | custom-call | flops 6442450944 | bytes 16777216 | tf_op jit(solution)/shard_map/hidden/pallas_call | solution.py:133
  167.2 9.1 %project.1 = bf16[512,4096]{1,0:T(8,128)(2,1)S(1)} custom-call(s32[2]{0:T(128)S(1)} %pad_add_fusion.place_ref, bf16[512,768]{1,0:T(8,128)(2,1)S(1)} %hidden.1.hidden_ref, bf16[2,8,32,768]{3,2,1,0:T(8,128)(2,1)S(1)} %bitcast.84, bf16[2,8,32,768]{3,2,1,0:T(8,128)(2,1)} %bitcast.26.refs_1_, bf16[2,8,32,768]{3,2,1,0:T(8,128)(2,1)} %bitcast.27.refs_2_, ...), custom_call_target="tpu_custom_call" | custom-call | flops 3221225472 | bytes 10485760 | tf_op jit(solution)/shard_map/project/pallas_call | solution.py:183
  176.4 2.0 copy-done
  178.4 6.9 %all-to-all-start.4 = ((bf16[16,32,4096]{2,1,0:T(8,128)(2,1)}), bf16[16,32,4096]{2,1,0:T(8,128)(2,1)}, u32[]{:S(2)}, u32[]{:S(2)}) async-start(bf16[16,32,4096]{2,1,0:T(8,128)(2,1)} %bitcast.82), calls=%async_computation.4 | async-start | bytes 8388608 | tf_op jit(solution)/shard_map/all_to_all | solution.py:348
  185.6 66.2 %all-to-all-done.4 = bf16[16,32,4096]{2,1,0:T(8,128)(2,1)} async-done(((bf16[16,32,4096]{2,1,0:T(8,128)(2,1)}), bf16[16,32,4096]{2,1,0:T(8,128)(2,1)}, u32[]{:S(2)}, u32[]{:S(2)}) %all-to-all-start.4) | async-done | bytes 4194336 | tf_op jit(solution)/shard_map/all_to_all | solution.py:348
  251.8 8.0 %combine.1 = (bf16[64,4096]{1,0:T(8,128)(2,1)}, bf16[128,32,128]{2,1,0:T(8,128)(2,1)S(1)}) custom-call(bf16[64,512]{1,0:T(8,128)(2,1)S(1)} %select_convert_fusion.high_ref, bf16[64,512]{1,0:T(8,128)(2,1)S(1)} %get-tuple-element.12.low_ref, bf16[128,64]{1,0:T(8,128)(2,1)S(1)} %fusion.20.picked_ref, f32[64,4096]{1,0:T(8,128)S(1)} %get-tuple-element.11.middle_ref, ...), custom_call_target="tpu_custom_call" | custom-call | tf_op jit(solution)/shard_map/combine/pallas_call | solution.py:236
  259.8 28.1 %all_to_all.30.lines_ref = bf16[128,32,128]{2,1,0:T(8,128)(2,1)S(1)} all-to-all(bf16[128,32,128]{2,1,0:T(8,128)(2,1)S(1)} %get-tuple-element.9), channel_id=1, replica_groups=mesh['ylo'=2,'z'=4,'x'=4,'yhi'=2,'core'=2] {'ylo','z','x','yhi','core'}, dimensions={0} | all-to-all | bytes 2097152 | tf_op jit(solution)/shard_map/all_to_all | solution.py:365
  287.9 2.8 unpack.1
  (122 shorter events, 26.8 us)
Async XLA Ops:
  0.7 11.1 %copy-start.24 = (s32[64]{0:T(128)S(1)}, s32[64]{0:T(128)}, u32[]{:S(2)}) copy-start(s32[64]{0:T(128)} %param.21) | copy-start | bytes 772
  0.7 20.8 %all-to-all-start = ((bf16[16,32,768]{2,1,0:T(8,128)(2,1)}), bf16[16,32,768]{2,1,0:T(8,128)(2,1)S(1)}, u32[]{:S(2)}, u32[]{:S(2)}) async-start(bf16[16,32,768]{2,1,0:T(8,128)(2,1)} %param.27), calls=%async_computation | async-start | bytes 1572864 | tf_op jit(solution)/shard_map/all_to_all | solution.py:304
  8.4 17.7 %copy-start.19 = (bf16[64,4096]{1,0:T(8,128)(2,1)S(1)}, bf16[64,4096]{1,0:T(8,128)(2,1)}, u32[]{:S(2)}) copy-start(bf16[64,4096]{1,0:T(8,128)(2,1)} %param.16) | copy-start | bytes 1572868
  10.0 11.4 %copy-start.17 = (f32[64,512]{1,0:T(8,128)}, f32[64,512]{1,0:T(8,128)S(1)}, u32[]{:S(2)}) copy-start(f32[64,512]{1,0:T(8,128)S(1)} %copy.47) | copy-start | bytes 393220
  21.4 25.5 %all-to-all-start.1 = ((bf16[16,32,768]{2,1,0:T(8,128)(2,1)}), bf16[16,32,768]{2,1,0:T(8,128)(2,1)S(1)}, u32[]{:S(2)}, u32[]{:S(2)}) async-start(bf16[16,32,768]{2,1,0:T(8,128)(2,1)} %bitcast.8), calls=%async_computation.1 | async-start | bytes 1572864 | tf_op jit(solution)/shard_map/all_to_all | solution.py:304
  36.7 22.7 %collective-permute-start = (bf16[16,32,768]{2,1,0:T(8,128)(2,1)S(1)}, bf16[16,32,768]{2,1,0:T(8,128)(2,1)}, u32[]{:S(2)}, u32[]{:S(2)}) collective-permute-start(bf16[16,32,768]{2,1,0:T(8,128)(2,1)S(1)} %all-to-all-done), channel_id=1, source_target_pairs={{0,16},{16,32},{32,48},{48,0},{1,17},{17,33},{33,49},{49,1},{2,18}... | collective-permute-start | bytes 2359304 | tf_op jit(solution)/shard_map/ppermute | solution.py:62
  38.4 21.0 %collective-permute-start.1 = (bf16[16,32,768]{2,1,0:T(8,128)(2,1)S(1)}, bf16[16,32,768]{2,1,0:T(8,128)(2,1)}, u32[]{:S(2)}, u32[]{:S(2)}) collective-permute-start(bf16[16,32,768]{2,1,0:T(8,128)(2,1)S(1)} %all-to-all-done), channel_id=1, source_target_pairs={{0,48},{16,0},{32,16},{48,32},{1,49},{17,1},{33,17},{49,33},{2,50}... | collective-permute-start | bytes 2359304 | tf_op jit(solution)/shard_map/ppermute | solution.py:63
  47.0 18.3 %all-to-all-start.3 = ((bf16[16,32,768]{2,1,0:T(8,128)(2,1)}), bf16[16,32,768]{2,1,0:T(8,128)(2,1)S(1)}, u32[]{:S(2)}, u32[]{:S(2)}) async-start(bf16[16,32,768]{2,1,0:T(8,128)(2,1)} %param.28), calls=%async_computation.3 | async-start | bytes 1572864 | tf_op jit(solution)/shard_map/all_to_all | solution.py:304
  65.2 81.5 %all-to-all-start.2 = ((bf16[16,32,4096]{2,1,0:T(8,128)(2,1)}), bf16[16,32,4096]{2,1,0:T(8,128)(2,1)}, u32[]{:S(2)}, u32[]{:S(2)}) async-start(bf16[16,32,4096]{2,1,0:T(8,128)(2,1)} %bitcast.94), calls=%async_computation.2 | async-start | bytes 8388608 | tf_op jit(solution)/shard_map/all_to_all | solution.py:338
  70.3 7.4 %collective-permute-start.3 = (bf16[16,32,768]{2,1,0:T(8,128)(2,1)S(1)}, bf16[16,32,768]{2,1,0:T(8,128)(2,1)S(1)}, u32[]{:S(2)}, u32[]{:S(2)}) collective-permute-start(bf16[16,32,768]{2,1,0:T(8,128)(2,1)S(1)} %all-to-all-done), channel_id=1, source_target_pairs={{0,1},{1,0},{2,3},{3,2},{4,5},{5,4},{6,7},{7,6},{8,9},{9,8},{10,11... | collective-permute-start | bytes 2359304 | tf_op jit(solution)/shard_map/ppermute | solution.py:74
  73.7 19.2 %collective-permute-start.8 = (bf16[16,32,768]{2,1,0:T(8,128)(2,1)S(1)}, bf16[16,32,768]{2,1,0:T(8,128)(2,1)S(1)}, u32[]{:S(2)}, u32[]{:S(2)}) collective-permute-start(bf16[16,32,768]{2,1,0:T(8,128)(2,1)S(1)} %all-to-all-done.3), channel_id=1, source_target_pairs={{0,48},{16,0},{32,16},{48,32},{1,49},{17,1},{33,17},{49,33},{2,50}... | collective-permute-start | bytes 2359304 | tf_op jit(solution)/shard_map/ppermute | solution.py:63
  75.1 20.1 %collective-permute-start.14 = (bf16[16,32,768]{2,1,0:T(8,128)(2,1)S(1)}, bf16[16,32,768]{2,1,0:T(8,128)(2,1)}, u32[]{:S(2)}, u32[]{:S(2)}) collective-permute-start(bf16[16,32,768]{2,1,0:T(8,128)(2,1)S(1)} %all-to-all-done.1), channel_id=1, source_target_pairs={{0,16},{16,32},{32,48},{48,0},{1,17},{17,33},{33,49},{49,1},{2,18}... | collective-permute-start | bytes 2359304 | tf_op jit(solution)/shard_map/ppermute | solution.py:62
  75.1 34.6 %collective-permute-start.15 = (bf16[16,32,768]{2,1,0:T(8,128)(2,1)S(1)}, bf16[16,32,768]{2,1,0:T(8,128)(2,1)}, u32[]{:S(2)}, u32[]{:S(2)}) collective-permute-start(bf16[16,32,768]{2,1,0:T(8,128)(2,1)S(1)} %all-to-all-done.1), channel_id=1, source_target_pairs={{0,48},{16,0},{32,16},{48,32},{1,49},{17,1},{33,17},{49,33},{2,50}... | collective-permute-start | bytes 2359304 | tf_op jit(solution)/shard_map/ppermute | solution.py:63
  77.7 36.6 %collective-permute-start.7 = (bf16[16,32,768]{2,1,0:T(8,128)(2,1)S(1)}, bf16[16,32,768]{2,1,0:T(8,128)(2,1)S(1)}, u32[]{:S(2)}, u32[]{:S(2)}) collective-permute-start(bf16[16,32,768]{2,1,0:T(8,128)(2,1)S(1)} %all-to-all-done.3), channel_id=1, source_target_pairs={{0,16},{16,32},{32,48},{48,0},{1,17},{17,33},{33,49},{49,1},{2,18}... | collective-permute-start | bytes 2359304 | tf_op jit(solution)/shard_map/ppermute | solution.py:62
  78.6 35.8 %collective-permute-start.10 = (bf16[16,32,768]{2,1,0:T(8,128)(2,1)S(1)}, bf16[16,32,768]{2,1,0:T(8,128)(2,1)S(1)}, u32[]{:S(2)}, u32[]{:S(2)}) collective-permute-start(bf16[16,32,768]{2,1,0:T(8,128)(2,1)S(1)} %all-to-all-done.3), channel_id=1, source_target_pairs={{0,1},{1,0},{2,3},{3,2},{4,5},{5,4},{6,7},{7,6},{8,9},{9,8},{10,11... | collective-permute-start | bytes 2359304 | tf_op jit(solution)/shard_map/ppermute | solution.py:74
  92.9 48.4 %copy-start.3 = (bf16[16,32,768]{2,1,0:T(8,128)(2,1)}, bf16[16,32,768]{2,1,0:T(8,128)(2,1)S(1)}, u32[]{:S(2)}) copy-start(bf16[16,32,768]{2,1,0:T(8,128)(2,1)S(1)} %collective-permute-done.8) | copy-start | bytes 2359300
  92.9 46.5 %collective-permute-start.2 = (bf16[16,32,768]{2,1,0:T(8,128)(2,1)}, bf16[16,32,768]{2,1,0:T(8,128)(2,1)}, u32[]{:S(2)}, u32[]{:S(2)}) collective-permute-start(bf16[16,32,768]{2,1,0:T(8,128)(2,1)} %collective-permute-done), channel_id=1, source_target_pairs={{0,16},{16,32},{32,48},{48,0},{1,17},{17,33},{33,49},{49,1},{2,18}... | collective-permute-start | bytes 2359304 | tf_op jit(solution)/shard_map/ppermute | solution.py:65
  95.2 44.7 %collective-permute-start.4 = (bf16[16,32,768]{2,1,0:T(8,128)(2,1)}, bf16[16,32,768]{2,1,0:T(8,128)(2,1)S(1)}, u32[]{:S(2)}, u32[]{:S(2)}) collective-permute-start(bf16[16,32,768]{2,1,0:T(8,128)(2,1)} %collective-permute-done), channel_id=1, source_target_pairs={{0,1},{1,0},{2,3},{3,2},{4,5},{5,4},{6,7},{7,6},{8,9},{9,8},{10,11... | collective-permute-start | bytes 2359304 | tf_op jit(solution)/shard_map/ppermute | solution.py:74
  109.7 31.1 %collective-permute-start.9 = (bf16[16,32,768]{2,1,0:T(8,128)(2,1)S(1)}, bf16[16,32,768]{2,1,0:T(8,128)(2,1)}, u32[]{:S(2)}, u32[]{:S(2)}) collective-permute-start(bf16[16,32,768]{2,1,0:T(8,128)(2,1)S(1)} %collective-permute-done.8), channel_id=1, source_target_pairs={{0,48},{16,0},{32,16},{48,32},{1,49},{17,1},{33,17},{49,33},{2,50}... | collective-permute-start | bytes 2359304 | tf_op jit(solution)/shard_map/ppermute | solution.py:67
  114.4 22.9 %collective-permute-start.16 = (bf16[8,32,768]{2,1,0:T(8,128)(2,1)S(1)}, bf16[8,32,768]{2,1,0:T(8,128)(2,1)}, u32[]{:S(2)}, u32[]{:S(2)}) collective-permute-start(bf16[8,32,768]{2,1,0:T(8,128)(2,1)S(1)} %slice.8), channel_id=1, source_target_pairs={{0,16},{16,32},{32,48},{48,0},{1,17},{17,33},{33,49},{49,1},{2,18}... | collective-permute-start | bytes 1179656 | tf_op jit(solution)/shard_map/ppermute | solution.py:70
  115.3 23.1 %collective-permute-start.17 = (bf16[8,32,768]{2,1,0:T(8,128)(2,1)S(1)}, bf16[8,32,768]{2,1,0:T(8,128)(2,1)}, u32[]{:S(2)}, u32[]{:S(2)}) collective-permute-start(bf16[8,32,768]{2,1,0:T(8,128)(2,1)S(1)} %slice.9), channel_id=1, source_target_pairs={{0,48},{16,0},{32,16},{48,32},{1,49},{17,1},{33,17},{49,33},{2,50}... | collective-permute-start | bytes 1179656 | tf_op jit(solution)/shard_map/ppermute | solution.py:71
  137.3 4.0 %collective-permute-start.5 = (bf16[16,32,768]{2,1,0:T(8,128)(2,1)}, bf16[16,32,768]{2,1,0:T(8,128)(2,1)S(1)}, u32[]{:S(2)}, u32[]{:S(2)}) collective-permute-start(bf16[16,32,768]{2,1,0:T(8,128)(2,1)} %collective-permute-done.1), channel_id=1, source_target_pairs={{0,1},{1,0},{2,3},{3,2},{4,5},{5,4},{6,7},{7,6},{8,9},{9,8},{10,11... | collective-permute-start | bytes 2359304 | tf_op jit(solution)/shard_map/ppermute | solution.py:74
  138.5 4.1 %collective-permute-start.11 = (bf16[16,32,768]{2,1,0:T(8,128)(2,1)S(1)}, bf16[16,32,768]{2,1,0:T(8,128)(2,1)S(1)}, u32[]{:S(2)}, u32[]{:S(2)}) collective-permute-start(bf16[16,32,768]{2,1,0:T(8,128)(2,1)S(1)} %collective-permute-done.7), channel_id=1, source_target_pairs={{0,1},{1,0},{2,3},{3,2},{4,5},{5,4},{6,7},{7,6},{8,9},{9,8},{10,11... | collective-permute-start | bytes 2359304 | tf_op jit(solution)/shard_map/ppermute | solution.py:74
  139.4 4.2 %collective-permute-start.12 = (bf16[16,32,768]{2,1,0:T(8,128)(2,1)S(1)}, bf16[16,32,768]{2,1,0:T(8,128)(2,1)S(1)}, u32[]{:S(2)}, u32[]{:S(2)}) collective-permute-start(bf16[16,32,768]{2,1,0:T(8,128)(2,1)S(1)} %collective-permute-done.8), channel_id=1, source_target_pairs={{0,1},{1,0},{2,3},{3,2},{4,5},{5,4},{6,7},{7,6},{8,9},{9,8},{10,11... | collective-permute-start | bytes 2359304 | tf_op jit(solution)/shard_map/ppermute | solution.py:74
  140.8 4.2 %collective-permute-start.6 = (bf16[16,32,768]{2,1,0:T(8,128)(2,1)}, bf16[16,32,768]{2,1,0:T(8,128)(2,1)}, u32[]{:S(2)}, u32[]{:S(2)}) collective-permute-start(bf16[16,32,768]{2,1,0:T(8,128)(2,1)} %collective-permute-done.2), channel_id=1, source_target_pairs={{0,1},{1,0},{2,3},{3,2},{4,5},{5,4},{6,7},{7,6},{8,9},{9,8},{10,11... | collective-permute-start | bytes 2359304 | tf_op jit(solution)/shard_map/ppermute | solution.py:74
  140.8 5.5 %collective-permute-start.13 = (bf16[16,32,768]{2,1,0:T(8,128)(2,1)}, bf16[16,32,768]{2,1,0:T(8,128)(2,1)}, u32[]{:S(2)}, u32[]{:S(2)}) collective-permute-start(bf16[16,32,768]{2,1,0:T(8,128)(2,1)} %collective-permute-done.9), channel_id=1, source_target_pairs={{0,1},{1,0},{2,3},{3,2},{4,5},{5,4},{6,7},{7,6},{8,9},{9,8},{10,11... | collective-permute-start | bytes 2359304 | tf_op jit(solution)/shard_map/ppermute | solution.py:74
  142.2 25.0 %collective-permute-start.18 = (bf16[16,32,768]{2,1,0:T(8,128)(2,1)S(1)}, bf16[16,32,768]{2,1,0:T(8,128)(2,1)}, u32[]{:S(2)}, u32[]{:S(2)}) collective-permute-start(bf16[16,32,768]{2,1,0:T(8,128)(2,1)S(1)} %all-to-all-done.1), channel_id=1, source_target_pairs={{0,1},{1,0},{2,3},{3,2},{4,5},{5,4},{6,7},{7,6},{8,9},{9,8},{10,11... | collective-permute-start | bytes 2359304 | tf_op jit(solution)/shard_map/ppermute | solution.py:74
  143.5 23.7 %collective-permute-start.19 = (bf16[16,32,768]{2,1,0:T(8,128)(2,1)}, bf16[16,32,768]{2,1,0:T(8,128)(2,1)}, u32[]{:S(2)}, u32[]{:S(2)}) collective-permute-start(bf16[16,32,768]{2,1,0:T(8,128)(2,1)} %collective-permute-done.14), channel_id=1, source_target_pairs={{0,1},{1,0},{2,3},{3,2},{4,5},{5,4},{6,7},{7,6},{8,9},{9,8},{10,11... | collective-permute-start | bytes 2359304 | tf_op jit(solution)/shard_map/ppermute | solution.py:74
  144.5 22.7 %collective-permute-start.20 = (bf16[16,32,768]{2,1,0:T(8,128)(2,1)}, bf16[16,32,768]{2,1,0:T(8,128)(2,1)}, u32[]{:S(2)}, u32[]{:S(2)}) collective-permute-start(bf16[16,32,768]{2,1,0:T(8,128)(2,1)} %collective-permute-done.15), channel_id=1, source_target_pairs={{0,1},{1,0},{2,3},{3,2},{4,5},{5,4},{6,7},{7,6},{8,9},{9,8},{10,11... | collective-permute-start | bytes 2359304 | tf_op jit(solution)/shard_map/ppermute | solution.py:74
  144.9 22.3 %collective-permute-start.21 = (bf16[8,32,768]{2,1,0:T(8,128)(2,1)}, bf16[8,32,768]{2,1,0:T(8,128)(2,1)}, u32[]{:S(2)}, u32[]{:S(2)}) collective-permute-start(bf16[8,32,768]{2,1,0:T(8,128)(2,1)} %collective-permute-done.16), channel_id=1, source_target_pairs={{0,1},{1,0},{2,3},{3,2},{4,5},{5,4},{6,7},{7,6},{8,9},{9,8},{10,11... | collective-permute-start | bytes 1179656 | tf_op jit(solution)/shard_map/ppermute | solution.py:74
  146.3 20.9 %collective-permute-start.22 = (bf16[8,32,768]{2,1,0:T(8,128)(2,1)}, bf16[8,32,768]{2,1,0:T(8,128)(2,1)}, u32[]{:S(2)}, u32[]{:S(2)}) collective-permute-start(bf16[8,32,768]{2,1,0:T(8,128)(2,1)} %collective-permute-done.17), channel_id=1, source_target_pairs={{0,1},{1,0},{2,3},{3,2},{4,5},{5,4},{6,7},{7,6},{8,9},{9,8},{10,11... | collective-permute-start | bytes 1179656 | tf_op jit(solution)/shard_map/ppermute | solution.py:74
  178.4 73.4 %all-to-all-start.4 = ((bf16[16,32,4096]{2,1,0:T(8,128)(2,1)}), bf16[16,32,4096]{2,1,0:T(8,128)(2,1)}, u32[]{:S(2)}, u32[]{:S(2)}) async-start(bf16[16,32,4096]{2,1,0:T(8,128)(2,1)} %bitcast.82), calls=%async_computation.4 | async-start | bytes 8388608 | tf_op jit(solution)/shard_map/all_to_all | solution.py:348
  (22 other events, 69.5 us)

commit v3 on v2

--- a/solution.py
+++ b/solution.py
@@ -1,4 +1,3 @@
-import functools
 import math
 
 import jax
@@ -24,58 +23,132 @@
 MIB = 1024 * 1024
 
 
-def attend_rows(queries, key_cache, value_cache, new_keys, new_values, cache_lengths):
-    row_total = queries.shape[0]
-    context = key_cache.shape[1]
-    per_group = QHEADS // KVHEADS
-    query_parts = queries.reshape(row_total, KVHEADS, per_group, HDIM)
-    key_parts = key_cache.reshape(row_total, context, KVHEADS, HDIM)
-    value_parts = value_cache.reshape(row_total, context, KVHEADS, HDIM)
-    fresh_key = new_keys.reshape(row_total, KVHEADS, HDIM)
-    fresh_value = new_values.astype(jnp.float32).reshape(row_total, KVHEADS, HDIM)
+def attend_kernel(
+    lengths_ref,
+    q_ref,
+    k_ref,
+    v_ref,
+    nk_ref,
+    nv_ref,
+    hidden_ref,
+    gain_ref,
+    pick_ref,
+    middle_ref,
+    outgoing_ref,
+    mixed_ref,
+):
+    step = pl.program_id(0)
+    block, context, _ = k_ref.shape
     scaling = 1.0 / math.sqrt(HDIM)
-    cached = (
-        jnp.einsum("nkgd,nckd->nkgc", query_parts, key_parts, preferred_element_type=jnp.float32)
-        * scaling
+    first = lax.broadcasted_iota(jnp.int32, (QHEADS, HDIM), 0) < QHEADS // KVHEADS
+    position = lax.broadcasted_iota(jnp.int32, (QHEADS, context), 1)
+    all_scores = []
+    all_own = []
+    for i in range(block):
+        q = q_ref[i]
+        none = jnp.zeros_like(q)
+        wide = jnp.concatenate([jnp.where(first, q, none), jnp.where(first, none, q)], axis=1)
+        scores = lax.dot_general(
+            wide, k_ref[i], (((1,), (1,)), ((), ())), preferred_element_type=jnp.float32
+        )
+        all_scores.append(
+            jnp.where(position < lengths_ref[step * block + i], scores * scaling, -jnp.inf)
+        )
+        fresh = nk_ref[i : i + 1, :].astype(jnp.float32)
+        all_own.append(jnp.sum(wide.astype(jnp.float32) * fresh, axis=1, keepdims=True) * scaling)
+    scores = jnp.concatenate(all_scores, axis=0)
+    own = jnp.concatenate(all_own, axis=0)
+    highest = jnp.maximum(jnp.max(scores, axis=1, keepdims=True), own)
+    powers = jnp.exp(scores - highest)
+    own_power = jnp.exp(own - highest)
+    inverse = 1.0 / (jnp.sum(powers, axis=1, keepdims=True) + own_power)
+    probs = (powers * inverse).astype(jnp.bfloat16)
+    own_prob = (own_power * inverse).astype(jnp.bfloat16).astype(jnp.float32)
+    for i in range(block):
+        span = slice(i * QHEADS, (i + 1) * QHEADS)
+        mixed = jnp.dot(probs[span], v_ref[i], preferred_element_type=jnp.float32)
+        mixed = mixed + own_prob[span] * nv_ref[i : i + 1, :].astype(jnp.float32)
+        at = pl.multiple_of((step * block + i) * QHEADS, QHEADS)
+        mixed_ref[pl.ds(at, QHEADS), :] = jnp.where(first, mixed[:, :HDIM], mixed[:, HDIM:])
+
+    @pl.when(step == pl.num_programs(0) - 1)
+    def _():
+        rows, width = middle_ref.shape
+        squares = jnp.zeros((rows, HDIM), jnp.float32)
+        for head in range(QHEADS):
+            cols = slice(head * HDIM, (head + 1) * HDIM)
+            middle = hidden_ref[:, cols].astype(jnp.float32) + mixed_ref[
+                pl.ds(head, rows, stride=QHEADS), :
+            ]
+            middle_ref[:, cols] = middle
+            squares = squares + middle * middle
+        scale = lax.rsqrt(jnp.sum(squares, axis=1, keepdims=True) / width + 1e-06)
+        part = 512
+        for at in range(0, width, part):
+            cols = slice(at, at + part)
+            normed = (middle_ref[:, cols] * scale * gain_ref[:, cols]).astype(jnp.bfloat16)
+            outgoing_ref[:, cols] = jnp.dot(
+                pick_ref[...], normed, preferred_element_type=jnp.float32
+            ).astype(jnp.bfloat16)
+
+
+def attend_call(lengths, queries, keys, values, new_keys, new_values, hidden_states, gain, pick):
+    rows, width = hidden_states.shape
+    context, features = keys.shape[1:]
+    slots = pick.shape[0]
+    block = 8
+    whole = lambda shape: pl.BlockSpec(shape, lambda i: (0,) * len(shape))
+    return pl.pallas_call(
+        attend_kernel,
+        grid=(rows // block,),
+        out_shape=(
+            jax.ShapeDtypeStruct((rows, width), jnp.float32),
+            jax.ShapeDtypeStruct((slots, width), jnp.bfloat16),
+        ),
+        in_specs=[
+            pl.BlockSpec(memory_space=pltpu.SMEM),
+            pl.BlockSpec((block, QHEADS, HDIM), lambda i: (i, 0, 0)),
+            pl.BlockSpec((block, context, features), lambda i: (i, 0, 0)),
+            pl.BlockSpec((block, context, features), lambda i: (i, 0, 0)),
+            pl.BlockSpec((block, features), lambda i: (i, 0)),
+            pl.BlockSpec((block, features), lambda i: (i, 0)),
+            whole((rows, width)),
+            whole((1, width)),
+            whole((slots, rows)),
+        ],
+        out_specs=(whole((rows, width)), whole((slots, width))),
+        scratch_shapes=[pltpu.VMEM((rows * QHEADS, HDIM), jnp.float32)],
+        compiler_params=pltpu.CompilerParams(vmem_limit_bytes=40 * MIB),
+        cost_estimate=pl.CostEstimate(
+            flops=2 * rows * 2 * QHEADS * context * features,
+            bytes_accessed=64 * MIB,
+            transcendentals=rows * QHEADS * context,
+        ),
+        name="attend",
+    )(
+        lengths,
+        queries.reshape(rows, QHEADS, HDIM),
+        keys,
+        values,
+        new_keys,
+        new_values,
+        hidden_states,
+        gain.reshape(1, width),
+        pick,
     )
-    usable = jnp.arange(context)[None, :] < cache_lengths[:, None]
-    cached = jnp.where(usable[:, None, None, :], cached, -jnp.inf)
-    own_score = (
-        jnp.einsum("nkgd,nkd->nkg", query_parts, fresh_key, preferred_element_type=jnp.float32)
-        * scaling
-    )
-    highest = jnp.maximum(jnp.max(cached, axis=-1), own_score)
-    cached_exp = jnp.exp(cached - highest[..., None])
-    own_exp = jnp.exp(own_score - highest)
-    totals = jnp.sum(cached_exp, axis=-1) + own_exp
-    cached_prob = (cached_exp / totals[..., None]).astype(jnp.bfloat16)
-    own_prob = (own_exp / totals).astype(jnp.bfloat16).astype(jnp.float32)
-    mixture = jnp.einsum(
-        "nkgc,nckd->nkgd", cached_prob, value_parts, preferred_element_type=jnp.float32
-    )
-    mixture = mixture + own_prob[..., None] * fresh_value[:, :, None, :]
-    return mixture.reshape(row_total, QHEADS * HDIM)
-
-
-def spread_piece(piece, way):
+
+
+def spread_piece(piece):
     half = piece.shape[0] // 2
     prev = lax.ppermute(piece, "z", ZUP)
     succ = lax.ppermute(piece, "z", ZDOWN)
-    if way > 0:
-        far = [lax.ppermute(prev, "z", ZUP)]
-    elif way < 0:
-        far = [lax.ppermute(succ, "z", ZDOWN)]
-    else:
-        far = [
-            lax.ppermute(prev[:half], "z", ZUP),
-            lax.ppermute(succ[half:], "z", ZDOWN),
-        ]
+    far = [lax.ppermute(prev[:half], "z", ZUP), lax.ppermute(succ[half:], "z", ZDOWN)]
     mine = [piece, prev, succ] + far
     other = [lax.ppermute(part, "core", SWAP) for part in mine]
-    return [part.reshape(-1, 8, 32, part.shape[-1]) for part in mine + other]
-
-
-def place_copies(place_ref, parts, scratch, sem):
+    return [part.reshape((-1, 8) + part.shape[1:]) for part in mine + other]
+
+
+def place_copies(place_ref, parts, scratch, sem, kind=None):
     z = place_ref[0]
     core = place_ref[1]
     count = len(parts) // 2
@@ -86,18 +159,18 @@
         zz = lax.rem(z + (0, RING - 1, 1, 2, 2)[which], RING)
         for lo in range(part.shape[0]):
             low = lo if which != 4 else 1
-            copies.append(pltpu.make_async_copy(part.at[lo], scratch.at[low, zz, :, c], sem))
+            source = part.at[lo] if kind is None else part.at[lo, :, kind]
+            copies.append(pltpu.make_async_copy(source, scratch.at[low, zz, :, c], sem))
     return copies
 
 
-def hidden_kernel(gate_count, place_ref, rows_any, *refs):
-    gate_parts = refs[:gate_count]
-    up_parts = refs[gate_count:-6]
+def hidden_kernel(place_ref, rows_any, *refs):
+    parts = refs[:-6]
     out_ref, rows_ref, gate_ref, up_ref, acc_ref, sem = refs[-6:]
     rows_copy = pltpu.make_async_copy(rows_any, rows_ref, sem.at[2])
     rows_copy.start()
-    gate_copies = place_copies(place_ref, gate_parts, gate_ref, sem.at[0])
-    up_copies = place_copies(place_ref, up_parts, up_ref, sem.at[1])
+    gate_copies = place_copies(place_ref, parts, gate_ref, sem.at[0], 0)
+    up_copies = place_copies(place_ref, parts, up_ref, sem.at[1], 1)
     for copy in gate_copies + up_copies:
         copy.start()
     rows_copy.wait()
@@ -125,16 +198,16 @@
         out_ref[:, cols] = (acc_ref[:, cols] * u).astype(out_ref.dtype)
 
 
-def hidden_call(place, rows, gate_parts, up_parts):
+def hidden_call(place, rows, parts):
     count, depth = rows.shape
-    width = gate_parts[0].shape[-1]
+    width = parts[0].shape[-1]
     hbm = pl.BlockSpec(memory_space=pl.ANY)
     weight = pltpu.VMEM((2, RING, 8, 2, 32, width), jnp.bfloat16)
     return pl.pallas_call(
-        functools.partial(hidden_kernel, len(gate_parts)),
+        hidden_kernel,
         out_shape=jax.ShapeDtypeStruct((count, width), jnp.bfloat16),
         in_specs=[pl.BlockSpec(memory_space=pltpu.SMEM)]
-        + [hbm] * (1 + len(gate_parts) + len(up_parts)),
+        + [hbm] * (1 + len(parts)),
         out_specs=pl.BlockSpec(memory_space=pltpu.VMEM),
         scratch_shapes=[
             pltpu.VMEM((count, depth), jnp.bfloat16),
@@ -143,14 +216,14 @@
             pltpu.VMEM((count, width), jnp.float32),
             pltpu.SemaphoreType.DMA((3,)),
         ],
-        compiler_params=pltpu.CompilerParams(vmem_limit_bytes=24 * MIB),
+        compiler_params=pltpu.CompilerParams(vmem_limit_bytes=56 * MIB),
         cost_estimate=pl.CostEstimate(
             flops=4 * count * depth * width,
             bytes_accessed=4 * depth * width + 2 * count * depth,
             transcendentals=count * width,
         ),
         name="hidden",
-    )(place, rows, *gate_parts, *up_parts)
+    )(place, rows, *parts)
 
 
 def project_kernel(place_ref, hidden_ref, *refs):
@@ -195,7 +268,7 @@
             pltpu.SemaphoreType.DMA,
             pltpu.SemaphoreType.DMA((2 * RING,)),
         ],
-        compiler_params=pltpu.CompilerParams(vmem_limit_bytes=18 * MIB),
+        compiler_params=pltpu.CompilerParams(vmem_limit_bytes=56 * MIB),
         cost_estimate=pl.CostEstimate(
             flops=2 * count * depth * width,
             bytes_accessed=2 * depth * width + 2 * count * depth,
@@ -205,12 +278,12 @@
     )(place, hidden, *parts)
 
 
-def combine_kernel(high_ref, low_ref, picked_ref, middle_ref, back_ref, layer_ref, parcel_ref, rows_ref):
+def combine_kernel(weighs_ref, picked_ref, middle_ref, back_ref, layer_ref, parcel_ref, rows_ref):
     step = pl.program_id(0)
     back = back_ref[...]
-    routed = jnp.dot(high_ref[...], back, preferred_element_type=jnp.float32) + jnp.dot(
-        low_ref[...], back, preferred_element_type=jnp.float32
-    )
+    rows = layer_ref.shape[0]
+    routed = jnp.dot(weighs_ref[...], back, preferred_element_type=jnp.float32)
+    routed = routed[:rows] + routed[rows:]
     layer = (middle_ref[...] + routed).astype(jnp.bfloat16)
     layer_ref[...] = layer
     lines = picked_ref.shape[0]
@@ -226,7 +299,7 @@
         parcel_ref[...] = rows_ref[...].reshape(parcel_ref.shape).astype(parcel_ref.dtype)
 
 
-def combine_call(high, low, picked, middle, back):
+def combine_call(weighs, picked, middle, back):
     rows, width = middle.shape
     slots = back.shape[0]
     learners = picked.shape[0]
@@ -241,8 +314,7 @@
             jax.ShapeDtypeStruct((learners, LINES, LINE), jnp.bfloat16),
         ),
         in_specs=[
-            whole((rows, slots)),
-            whole((rows, slots)),
+            whole((2 * rows, slots)),
             whole((learners, rows)),
             column(rows),
             column(slots),
@@ -251,7 +323,7 @@
         scratch_shapes=[pltpu.VMEM((learners * LINES, LINE), jnp.float32)],
         compiler_params=pltpu.CompilerParams(vmem_limit_bytes=16 * MIB),
         name="combine",
-    )(high, low, picked, middle, back)
+    )(weighs, picked, middle, back)
 
 
 def unpack_kernel(lines_ref, out_ref, rows_ref):
@@ -302,18 +374,10 @@
     place = jnp.stack([lax.axis_index("z"), lax.axis_index("core")]).astype(jnp.int32)
 
     to_chip = lambda part: lax.all_to_all(part, PLANE, split_axis=0, concat_axis=0, tiled=True)
-    gate = to_chip(gate_weight)
-    up = to_chip(up_weight)
+    pair = to_chip(jnp.stack([gate_weight, up_weight], axis=1))
     down = to_chip(jnp.swapaxes(down_weight, 1, 2))
-    gate_parts = spread_piece(gate, 1)
-    up_parts = spread_piece(up, -1)
-    down_parts = spread_piece(down, 0)
-
-    queries, _ = lax.optimization_barrier((queries, gate))
-    attended = attend_rows(queries, key_cache, value_cache, new_keys, new_values, cache_lengths)
-    middle = hidden_states.astype(jnp.float32) + attended
-    spread = jnp.mean(middle * middle, axis=-1, keepdims=True)
-    normed = (middle * lax.rsqrt(spread + 1e-06) * norm_gain).astype(jnp.bfloat16)
+    pair_parts = spread_piece(pair)
+    down_parts = spread_piece(down)
 
     expert_range = jnp.arange(experts, dtype=jnp.int32)
     hit_table = expert_ids[:, :, None] == expert_range[None, None, :]
@@ -326,15 +390,34 @@
     )
     slot_range = jnp.arange(capacity, dtype=jnp.int32)
     chosen = matched[:, :, None] & (slot_rank[:, :, None] == slot_range[None, None, :])
-    pick = chosen.reshape(row_count, slots).astype(jnp.bfloat16)
     weigh = jnp.where(chosen, slot_gate[:, :, None], 0.0).reshape(row_count, slots)
     weigh_high = weigh.astype(jnp.bfloat16)
     weigh_low = (weigh - weigh_high.astype(jnp.float32)).astype(jnp.bfloat16)
-
-    outgoing = lax.dot_general(
-        pick, normed, (((0,), (0,)), ((), ())), preferred_element_type=jnp.float32
-    ).astype(jnp.bfloat16)
-    outgoing, _, _, _ = lax.optimization_barrier((outgoing, gate_parts[1], gate_parts[2], down))
+    weighs = jnp.concatenate([weigh_high, weigh_low], axis=0)
+    turned = matched.T[:, None, :] & (slot_rank.T[:, None, :] == slot_range[None, :, None])
+    pick = turned.reshape(slots, row_count).astype(jnp.bfloat16)
+
+    finished_rows = finished > 0
+    same_target = (learner_ids[:, None] == learner_ids[None, :]) & finished_rows[None, :] & earlier
+    learner_rank = jnp.sum(same_target.astype(jnp.int32), axis=1)
+    slot_of_row = learner_ids + learner_rank
+    slot_span = jnp.arange(learners, dtype=jnp.int32)
+    picked = finished_rows[None, :] & (slot_of_row[None, :] == slot_span[:, None])
+    picked = picked.astype(jnp.bfloat16)
+
+    queries, weighs, picked, place = lax.optimization_barrier((queries, weighs, picked, place))
+    middle, outgoing = attend_call(
+        cache_lengths,
+        queries,
+        key_cache,
+        value_cache,
+        new_keys,
+        new_values,
+        hidden_states,
+        norm_gain,
+        pick,
+    )
+    outgoing, _, _ = lax.optimization_barrier((outgoing, pair, down))
     received = lax.all_to_all(
         outgoing.reshape(experts, capacity, model_width),
         PLANE,
@@ -343,7 +426,7 @@
         tiled=True,
     ).reshape(slots, model_width)
 
-    hidden = hidden_call(place, received, gate_parts, up_parts)
+    hidden = hidden_call(place, received, pair_parts)
     expert_out = project_call(place, hidden, down_parts)
     returned = lax.all_to_all(
         expert_out.reshape(experts, capacity, model_width),
@@ -353,15 +436,7 @@
         tiled=True,
     ).reshape(slots, model_width)
 
-    finished_rows = finished > 0
-    same_target = (learner_ids[:, None] == learner_ids[None, :]) & finished_rows[None, :] & earlier
-    learner_rank = jnp.sum(same_target.astype(jnp.int32), axis=1)
-    slot_of_row = learner_ids + learner_rank
-    slot_span = jnp.arange(learners, dtype=jnp.int32)
-    picked = finished_rows[None, :] & (slot_of_row[None, :] == slot_span[:, None])
-    layer_out, parcel = combine_call(
-        weigh_high, weigh_low, picked.astype(jnp.bfloat16), middle, returned
-    )
+    layer_out, parcel = combine_call(weighs, picked, middle, returned)
     arrived = lax.all_to_all(parcel, AXES, split_axis=0, concat_axis=0, tiled=True)
     return (layer_out, unpack_call(arrived))
 

time: 292 us -> 254 us (0.87)
  waiting for transfers between devices: 130 us -> 76.1 us
  blocking collectives: 28.1 us -> 81.1 us
  matrix products: 17.3 us -> 0 us
  local copies, waits for them, and re-layouts: 20.6 us -> 7.59 us
  starting transfers between devices: 54.2 us -> 41.2 us
  Pallas kernels: 31.3 us -> 42.6 us
  other arithmetic: 7.76 us -> 3.58 us
    all_to_all x1 -> x0, waiting for transfers between devices: 66.2 us -> none  [shards(): lax.all_to_all(expert_out.reshape(experts, capacity, model_width), PLANE,...]
    all_to_all x0 -> x1, blocking collectives: none -> 56.9 us  [shards(): lax.all_to_all(expert_out.reshape(experts, capacity, model_width), PLANE,...]
    ppermute x3 -> x2, waiting for transfers between devices: 2.28 us -> 46.3 us  [spread_piece(): prev = lax.ppermute(piece, 'z', ZUP)]
    ppermute x3 -> x2, waiting for transfers between devices: 26 us -> 0.01 us  [spread_piece(): succ = lax.ppermute(piece, 'z', ZDOWN)]
    dot_general x4 -> x0, matrix products: 17.3 us -> none  [the longest x1 7.09 us: attend_rows(): jnp.einsum('nkgd,nckd->nkgc', query_parts, key_parts, preferred_element_t...]
    pallas_call x1 -> x2, Pallas kernels: 11.4 us -> 26.1 us  [the longest x1 13.2 us: hidden_call(): pl.pallas_call(hidden_kernel, out_shape=jax.ShapeDtypeStruct((count, widt...]
    unnamed x53 -> x51, local copies, waits for them, and re-layouts: 17.4 us -> 5.64 us
    all_to_all x1 -> x0, starting transfers between devices: 6.88 us -> none  [shards(): lax.all_to_all(expert_out.reshape(experts, capacity, model_width), PLANE,...]
  transfers between devices with their start and end apart: 28 -> 21, of which waited for: 8 -> 5; matrix products, arithmetic and copies ran while one was open for 10% -> 2% of each run, Pallas kernels for 4% -> 10%
where the time goes in v3:
time: 254 us; the launch traced here: 253 us
  blocking collectives  81.1 us (32%)
  waiting for transfers between devices  76.1 us (30%)
  Pallas kernels  42.6 us (17%)
  starting transfers between devices  41.2 us (16%)
  local copies, waits for them, and re-layouts  7.59 us (3%)
  other arithmetic  3.58 us (1%)
    all_to_all x1, blocking collectives, shards(): lax.all_to_all(expert_out.reshape(experts, capacity, model_width), PLANE,...  56.9 us
    ppermute x2, waiting for transfers between devices, spread_piece(): prev = lax.ppermute(piece, 'z', ZUP)  46.3 us
    all_to_all x1, blocking collectives, shards(): lax.all_to_all(parcel, AXES, split_axis=0, concat_axis=0, tiled=True)  24.2 us
    ppermute x2, waiting for transfers between devices, spread_piece(): lax.ppermute(prev[:half], 'z', ZUP)  14.3 us
    all_to_all x2, waiting for transfers between devices, shards(): lax.all_to_all(part, PLANE, split_axis=0, concat_axis=0, tiled=True)  14.1 us
    pallas_call x1, Pallas kernels, hidden_call(): pl.pallas_call(hidden_kernel, out_shape=jax.ShapeDtypeStruct((count, widt...  13.2 us
    pallas_call x1, Pallas kernels, attend_call(): pl.pallas_call(attend_kernel, grid=(rows // block,), out_shape=(jax.Shape...  12.9 us
    all_to_all x2, starting transfers between devices, shards(): lax.all_to_all(part, PLANE, split_axis=0, concat_axis=0, tiled=True)  12.4 us
  transfers between devices with their start and end apart: 21, of which 5 were waited for; matrix products, arithmetic and copies ran while one was open for 2% of the time, Pallas kernels for 10%

profile of v3, /device:TPU:1, one launch (start us, length us, event | category | flops | bytes accessed | tf_op | source)
XLA Modules:
  0.0 253.4 jit_solution(13425444118588515682)
XLA Ops:
  0.7 7.7 %all-to-all-start.1 = ((bf16[16,32,768]{2,1,0:T(8,128)(2,1)}), bf16[16,32,768]{2,1,0:T(8,128)(2,1)S(1)}, u32[]{:S(2)}, u32[]{:S(2)}) async-start(bf16[16,32,768]{2,1,0:T(8,128)(2,1)} %bitcast.52), calls=%async_computation.1 | async-start | bytes 1572864 | tf_op jit(solution)/shard_map/all_to_all | solution.py:376
  8.5 1.3 pad_maximum_fusion
  9.8 11.6 %all-to-all-done.1 = bf16[16,32,768]{2,1,0:T(8,128)(2,1)S(1)} async-done(((bf16[16,32,768]{2,1,0:T(8,128)(2,1)}), bf16[16,32,768]{2,1,0:T(8,128)(2,1)S(1)}, u32[]{:S(2)}, u32[]{:S(2)}) %all-to-all-start.1) | async-done | bytes 786464 | tf_op jit(solution)/shard_map/all_to_all | solution.py:376
  21.5 4.7 %all-to-all-start = ((bf16[16,2,32,768]{3,2,1,0:T(8,128)(2,1)}), bf16[16,2,32,768]{3,2,1,0:T(8,128)(2,1)}, u32[]{:S(2)}, u32[]{:S(2)}) async-start(bf16[16,2,32,768]{3,2,1,0:T(8,128)(2,1)} %pad_maximum_fusion), calls=%async_computation | async-start | bytes 3145728 | tf_op jit(solution)/shard_map/all_to_all | solution.py:376
  26.6 1.2 select_reduce_fusion
  28.3 0.6 pad_add_fusion.place_ref
  29.4 12.9 %attend.1 = (f32[64,4096]{1,0:T(8,128)S(1)}, bf16[512,4096]{1,0:T(8,128)(2,1)S(1)}) custom-call(s32[64]{0:T(128)S(1)} %copy-done.5, bf16[64,32,128]{2,1,0:T(8,128)(2,1)S(1)} %bitcast.47, bf16[64,256,256]{2,1,0:T(8,128)(2,1)} %k_ref.1, bf16[64,256,256]{2,1,0:T(8,128)(2,1)} %v_ref.1, bf16[64,256]{1,0:T(8,128)(2,1)S(1)} %copy-done.2, ...), custom_call_target="tpu_custom_call" | custom-call | flops 536870912 | bytes 67108864 | tf_op jit(solution)/shard_map/attend/pallas_call | solution.py:101
  42.3 2.0 copy-done
  44.3 2.5 all-to-all-done
  46.8 6.5 %all-to-all-start.2 = ((bf16[16,32,4096]{2,1,0:T(8,128)(2,1)}), bf16[16,32,4096]{2,1,0:T(8,128)(2,1)}, u32[]{:S(2)}, u32[]{:S(2)}) async-start(bf16[16,32,4096]{2,1,0:T(8,128)(2,1)} %bitcast.46), calls=%async_computation.2 | async-start | bytes 8388608 | tf_op jit(solution)/shard_map/all_to_all | solution.py:421
  53.3 1.7 collective-permute-start
  55.0 2.2 collective-permute-start.1
  57.2 2.7 %collective-permute-start.10 = (bf16[16,32,768]{2,1,0:T(8,128)(2,1)S(1)}, bf16[16,32,768]{2,1,0:T(8,128)(2,1)}, u32[]{:S(2)}, u32[]{:S(2)}) collective-permute-start(bf16[16,32,768]{2,1,0:T(8,128)(2,1)S(1)} %all-to-all-done.1), channel_id=1, source_target_pairs={{0,48},{16,0},{32,16},{48,32},{1,49},{17,1},{33,17},{49,33},{2,50}... | collective-permute-start | bytes 2359304 | tf_op jit(solution)/shard_map/ppermute | solution.py:144
  59.9 46.3 %collective-permute-done.9 = bf16[16,32,768]{2,1,0:T(8,128)(2,1)S(1)} collective-permute-done((bf16[16,32,768]{2,1,0:T(8,128)(2,1)S(1)}, bf16[16,32,768]{2,1,0:T(8,128)(2,1)S(1)}, u32[]{:S(2)}, u32[]{:S(2)}) %collective-permute-start.9) | collective-permute-done | bytes 786464 | tf_op jit(solution)/shard_map/ppermute | solution.py:143
  106.3 1.2 slice.19
  107.5 2.6 %collective-permute-start.12 = (bf16[8,32,768]{2,1,0:T(8,128)(2,1)S(1)}, bf16[8,32,768]{2,1,0:T(8,128)(2,1)}, u32[]{:S(2)}, u32[]{:S(2)}) collective-permute-start(bf16[8,32,768]{2,1,0:T(8,128)(2,1)S(1)} %slice.19), channel_id=1, source_target_pairs={{0,48},{16,0},{32,16},{48,32},{1,49},{17,1},{33,17},{49,33},{2,50}... | collective-permute-start | bytes 1179656 | tf_op jit(solution)/shard_map/ppermute | solution.py:145
  110.0 4.0 %collective-permute-start.4 = (bf16[16,2,32,768]{3,2,1,0:T(8,128)(2,1)}, bf16[16,2,32,768]{3,2,1,0:T(8,128)(2,1)S(1)}, u32[]{:S(2)}, u32[]{:S(2)}) collective-permute-start(bf16[16,2,32,768]{3,2,1,0:T(8,128)(2,1)} %all-to-all-done), channel_id=1, source_target_pairs={{0,1},{1,0},{2,3},{3,2},{4,5},{5,4},{6,7},{7,6},{8,9},{9,8},{10,11... | collective-permute-start | bytes 4718600 | tf_op jit(solution)/shard_map/ppermute | solution.py:147
  114.6 0.5 copy-done.10
  115.1 0.6 copy-done.11
  115.8 2.7 %collective-permute-start.3 = (bf16[8,2,32,768]{3,2,1,0:T(8,128)(2,1)S(1)}, bf16[8,2,32,768]{3,2,1,0:T(8,128)(2,1)S(1)}, u32[]{:S(2)}, u32[]{:S(2)}) collective-permute-start(bf16[8,2,32,768]{3,2,1,0:T(8,128)(2,1)S(1)} %slice.17), channel_id=1, source_target_pairs={{0,48},{16,0},{32,16},{48,32},{1,49},{17,1},{33,17},{49,33},{2,50}... | collective-permute-start | bytes 2359304 | tf_op jit(solution)/shard_map/ppermute | solution.py:145
  118.4 14.3 %collective-permute-done.2 = bf16[8,2,32,768]{3,2,1,0:T(8,128)(2,1)S(1)} collective-permute-done((bf16[8,2,32,768]{3,2,1,0:T(8,128)(2,1)S(1)}, bf16[8,2,32,768]{3,2,1,0:T(8,128)(2,1)S(1)}, u32[]{:S(2)}, u32[]{:S(2)}) %collective-permute-start.2) | collective-permute-done | bytes 786464 | tf_op jit(solution)/shard_map/ppermute | solution.py:145
  132.7 4.2 %collective-permute-start.7 = (bf16[8,2,32,768]{3,2,1,0:T(8,128)(2,1)S(1)}, bf16[8,2,32,768]{3,2,1,0:T(8,128)(2,1)S(1)}, u32[]{:S(2)}, u32[]{:S(2)}) collective-permute-start(bf16[8,2,32,768]{3,2,1,0:T(8,128)(2,1)S(1)} %collective-permute-done.2), channel_id=1, source_target_pairs={{0,1},{1,0},{2,3},{3,2},{4,5},{5,4},{6,7},{7,6},{8,9},{9,8},{10,11... | collective-permute-start | bytes 2359304 | tf_op jit(solution)/shard_map/ppermute | solution.py:147
  137.7 0.6 copy-done.16
  138.8 0.6 copy-done.18
  139.7 1.3 collective-permute-done.8
  141.1 1.0 copy-done.22
  142.4 13.2 %hidden.1.hidden_ref = bf16[512,768]{1,0:T(8,128)(2,1)} custom-call(s32[2]{0:T(128)} %pad_add_fusion.place_ref, bf16[512,4096]{1,0:T(8,128)(2,1)} %bitcast.14.rows_any, bf16[2,8,2,32,768]{4,3,2,1,0:T(8,128)(2,1)} %bitcast.15.refs_0_, bf16[2,8,2,32,768]{4,3,2,1,0:T(8,128)(2,1)} %bitcast.57, bf16[2,8,2,32,768]{4,3,2,1,0:T(8,128)(2,1)} %bitcast.58, ...), custom_call_target="tpu_custom_call" | custom-call | flops 6442450944 | bytes 16777216 | tf_op jit(solution)/shard_map/hidden/pallas_call | solution.py:206
  155.7 8.3 %project.1 = bf16[512,4096]{1,0:T(8,128)(2,1)} custom-call(s32[2]{0:T(128)} %pad_add_fusion.place_ref, bf16[512,768]{1,0:T(8,128)(2,1)} %hidden.1.hidden_ref, bf16[2,8,32,768]{3,2,1,0:T(8,128)(2,1)} %bitcast.53, bf16[2,8,32,768]{3,2,1,0:T(8,128)(2,1)} %bitcast.61, bf16[2,8,32,768]{3,2,1,0:T(8,128)(2,1)} %bitcast.27.refs_2_, ...), custom_call_target="tpu_custom_call" | custom-call | flops 3221225472 | bytes 10485760 | tf_op jit(solution)/shard_map/project/pallas_call | solution.py:256
  164.0 56.9 %all_to_all.25 = bf16[16,32,4096]{2,1,0:T(8,128)(2,1)S(1)} all-to-all(bf16[16,32,4096]{2,1,0:T(8,128)(2,1)} %bitcast.49), channel_id=1, replica_groups=mesh['ylo'=2,'z'=4,'x'=4,'yhi'=2,'core'=2] {'ylo','x','yhi'}, dimensions={0} | all-to-all | bytes 8388608 | tf_op jit(solution)/shard_map/all_to_all | solution.py:431
  221.0 5.4 %combine.1 = (bf16[64,4096]{1,0:T(8,128)(2,1)}, bf16[128,32,128]{2,1,0:T(8,128)(2,1)S(1)}) custom-call(bf16[128,512]{1,0:T(8,128)(2,1)S(1)} %pad_maximum_fusion.1.weighs_ref, bf16[128,64]{1,0:T(8,128)(2,1)S(1)} %fusion.4.picked_ref, f32[64,4096]{1,0:T(8,128)S(1)} %get-tuple-element.14.middle_ref, bf16[512,4096]{1,0:T(8,128)(2,1)S(1)} %bitcast.45), custom_call_target="tpu_custom_call" | custom-call | tf_op jit(solution)/shard_map/combine/pallas_call | solution.py:309
  226.4 24.2 %all_to_all.26.lines_ref = bf16[128,32,128]{2,1,0:T(8,128)(2,1)S(1)} all-to-all(bf16[128,32,128]{2,1,0:T(8,128)(2,1)S(1)} %get-tuple-element.19), channel_id=1, replica_groups=mesh['ylo'=2,'z'=4,'x'=4,'yhi'=2,'core'=2] {'ylo','z','x','yhi','core'}, dimensions={0} | all-to-all | bytes 2097152 | tf_op jit(solution)/shard_map/all_to_all | solution.py:440
  250.6 2.8 %unpack.1 = bf16[128,4096]{1,0:T(8,128)(2,1)} custom-call(bf16[128,32,128]{2,1,0:T(8,128)(2,1)S(1)} %all_to_all.26.lines_ref), custom_call_target="tpu_custom_call" | custom-call | tf_op jit(solution)/shard_map/unpack/pallas_call | solution.py:341
  (96 shorter events, 4.1 us)
Async XLA Ops:
  0.6 7.8 %copy-start.13 = (s32[64,8]{0,1:T(8,128)S(1)}, s32[64,8]{0,1:T(8,128)}, u32[]{:S(2)}) copy-start(s32[64,8]{0,1:T(8,128)} %param.23) | copy-start | bytes 6148
  0.6 7.8 %copy-start.14 = (f32[64,8]{0,1:T(8,128)S(1)}, f32[64,8]{0,1:T(8,128)}, u32[]{:S(2)}) copy-start(f32[64,8]{0,1:T(8,128)} %param.24) | copy-start | bytes 6148
  0.7 7.8 %copy-start.7 = (bf16[16,32,768]{2,1,0:T(8,128)(2,1)S(1)}, bf16[16,32,768]{2,1,0:T(8,128)(2,1)}, u32[]{:S(2)}) copy-start(bf16[16,32,768]{2,1,0:T(8,128)(2,1)} %param.28) | copy-start | bytes 2359300
  0.7 7.8 %copy-start.8 = (bf16[16,32,768]{2,1,0:T(8,128)(2,1)S(1)}, bf16[16,32,768]{2,1,0:T(8,128)(2,1)}, u32[]{:S(2)}) copy-start(bf16[16,32,768]{2,1,0:T(8,128)(2,1)} %param.27) | copy-start | bytes 2359300
  0.7 20.8 %all-to-all-start.1 = ((bf16[16,32,768]{2,1,0:T(8,128)(2,1)}), bf16[16,32,768]{2,1,0:T(8,128)(2,1)S(1)}, u32[]{:S(2)}, u32[]{:S(2)}) async-start(bf16[16,32,768]{2,1,0:T(8,128)(2,1)} %bitcast.52), calls=%async_computation.1 | async-start | bytes 1572864 | tf_op jit(solution)/shard_map/all_to_all | solution.py:376
  21.5 115.6 %copy-start.6 = (bf16[16,32,768]{2,1,0:T(8,128)(2,1)}, bf16[16,32,768]{2,1,0:T(8,128)(2,1)S(1)}, u32[]{:S(2)}) copy-start(bf16[16,32,768]{2,1,0:T(8,128)(2,1)S(1)} %all-to-all-done.1) | copy-start | bytes 2359300
  21.5 25.4 %all-to-all-start = ((bf16[16,2,32,768]{3,2,1,0:T(8,128)(2,1)}), bf16[16,2,32,768]{3,2,1,0:T(8,128)(2,1)}, u32[]{:S(2)}, u32[]{:S(2)}) async-start(bf16[16,2,32,768]{3,2,1,0:T(8,128)(2,1)} %pad_maximum_fusion), calls=%async_computation | async-start | bytes 3145728 | tf_op jit(solution)/shard_map/all_to_all | solution.py:376
  26.4 2.9 %copy-start.1 = (bf16[64,4096]{1,0:T(8,128)(2,1)S(1)}, bf16[64,4096]{1,0:T(8,128)(2,1)}, u32[]{:S(2)}) copy-start(bf16[64,4096]{1,0:T(8,128)(2,1)} %hidden_ref.1) | copy-start | bytes 1572868
  26.4 2.9 %copy-start.2 = (bf16[64,256]{1,0:T(8,128)(2,1)S(1)}, bf16[64,256]{1,0:T(8,128)(2,1)}, u32[]{:S(2)}) copy-start(bf16[64,256]{1,0:T(8,128)(2,1)} %nk_ref.1) | copy-start | bytes 98308
  46.8 95.6 %all-to-all-start.2 = ((bf16[16,32,4096]{2,1,0:T(8,128)(2,1)}), bf16[16,32,4096]{2,1,0:T(8,128)(2,1)}, u32[]{:S(2)}, u32[]{:S(2)}) async-start(bf16[16,32,4096]{2,1,0:T(8,128)(2,1)} %bitcast.46), calls=%async_computation.2 | async-start | bytes 8388608 | tf_op jit(solution)/shard_map/all_to_all | solution.py:421
  53.3 60.7 %collective-permute-start = (bf16[16,2,32,768]{3,2,1,0:T(8,128)(2,1)}, bf16[16,2,32,768]{3,2,1,0:T(8,128)(2,1)S(1)}, u32[]{:S(2)}, u32[]{:S(2)}) collective-permute-start(bf16[16,2,32,768]{3,2,1,0:T(8,128)(2,1)} %all-to-all-done), channel_id=1, source_target_pairs={{0,16},{16,32},{32,48},{48,0},{1,17},{17,33},{33,49},{49,1},{2,18}... | collective-permute-start | bytes 4718600 | tf_op jit(solution)/shard_map/ppermute | solution.py:143
  55.0 59.1 %collective-permute-start.1 = (bf16[16,2,32,768]{3,2,1,0:T(8,128)(2,1)}, bf16[16,2,32,768]{3,2,1,0:T(8,128)(2,1)S(1)}, u32[]{:S(2)}, u32[]{:S(2)}) collective-permute-start(bf16[16,2,32,768]{3,2,1,0:T(8,128)(2,1)} %all-to-all-done), channel_id=1, source_target_pairs={{0,48},{16,0},{32,16},{48,32},{1,49},{17,1},{33,17},{49,33},{2,50}... | collective-permute-start | bytes 4718600 | tf_op jit(solution)/shard_map/ppermute | solution.py:144
  57.2 48.9 %collective-permute-start.9 = (bf16[16,32,768]{2,1,0:T(8,128)(2,1)S(1)}, bf16[16,32,768]{2,1,0:T(8,128)(2,1)S(1)}, u32[]{:S(2)}, u32[]{:S(2)}) collective-permute-start(bf16[16,32,768]{2,1,0:T(8,128)(2,1)S(1)} %all-to-all-done.1), channel_id=1, source_target_pairs={{0,16},{16,32},{32,48},{48,0},{1,17},{17,33},{33,49},{49,1},{2,18}... | collective-permute-start | bytes 2359304 | tf_op jit(solution)/shard_map/ppermute | solution.py:143
  57.2 49.0 %collective-permute-start.10 = (bf16[16,32,768]{2,1,0:T(8,128)(2,1)S(1)}, bf16[16,32,768]{2,1,0:T(8,128)(2,1)}, u32[]{:S(2)}, u32[]{:S(2)}) collective-permute-start(bf16[16,32,768]{2,1,0:T(8,128)(2,1)S(1)} %all-to-all-done.1), channel_id=1, source_target_pairs={{0,48},{16,0},{32,16},{48,32},{1,49},{17,1},{33,17},{49,33},{2,50}... | collective-permute-start | bytes 2359304 | tf_op jit(solution)/shard_map/ppermute | solution.py:144
  106.2 31.4 %copy-start.12 = (bf16[16,32,768]{2,1,0:T(8,128)(2,1)}, bf16[16,32,768]{2,1,0:T(8,128)(2,1)S(1)}, u32[]{:S(2)}) copy-start(bf16[16,32,768]{2,1,0:T(8,128)(2,1)S(1)} %collective-permute-done.9) | copy-start | bytes 2359300
  106.2 9.6 %collective-permute-start.11 = (bf16[8,32,768]{2,1,0:T(8,128)(2,1)S(1)}, bf16[8,32,768]{2,1,0:T(8,128)(2,1)S(1)}, u32[]{:S(2)}, u32[]{:S(2)}) collective-permute-start(bf16[8,32,768]{2,1,0:T(8,128)(2,1)S(1)} %slice.18), channel_id=1, source_target_pairs={{0,16},{16,32},{32,48},{48,0},{1,17},{17,33},{33,49},{49,1},{2,18}... | collective-permute-start | bytes 1179656 | tf_op jit(solution)/shard_map/ppermute | solution.py:145
  107.5 8.3 %collective-permute-start.12 = (bf16[8,32,768]{2,1,0:T(8,128)(2,1)S(1)}, bf16[8,32,768]{2,1,0:T(8,128)(2,1)}, u32[]{:S(2)}, u32[]{:S(2)}) collective-permute-start(bf16[8,32,768]{2,1,0:T(8,128)(2,1)S(1)} %slice.19), channel_id=1, source_target_pairs={{0,48},{16,0},{32,16},{48,32},{1,49},{17,1},{33,17},{49,33},{2,50}... | collective-permute-start | bytes 1179656 | tf_op jit(solution)/shard_map/ppermute | solution.py:145
  110.0 27.0 %collective-permute-start.4 = (bf16[16,2,32,768]{3,2,1,0:T(8,128)(2,1)}, bf16[16,2,32,768]{3,2,1,0:T(8,128)(2,1)S(1)}, u32[]{:S(2)}, u32[]{:S(2)}) collective-permute-start(bf16[16,2,32,768]{3,2,1,0:T(8,128)(2,1)} %all-to-all-done), channel_id=1, source_target_pairs={{0,1},{1,0},{2,3},{3,2},{4,5},{5,4},{6,7},{7,6},{8,9},{9,8},{10,11... | collective-permute-start | bytes 4718600 | tf_op jit(solution)/shard_map/ppermute | solution.py:147
  114.0 23.5 %collective-permute-start.5 = (bf16[16,2,32,768]{3,2,1,0:T(8,128)(2,1)S(1)}, bf16[16,2,32,768]{3,2,1,0:T(8,128)(2,1)S(1)}, u32[]{:S(2)}, u32[]{:S(2)}) collective-permute-start(bf16[16,2,32,768]{3,2,1,0:T(8,128)(2,1)S(1)} %collective-permute-done), channel_id=1, source_target_pairs={{0,1},{1,0},{2,3},{3,2},{4,5},{5,4},{6,7},{7,6},{8,9},{9,8},{10,11... | collective-permute-start | bytes 4718600 | tf_op jit(solution)/shard_map/ppermute | solution.py:147
  114.1 23.6 %collective-permute-start.6 = (bf16[16,2,32,768]{3,2,1,0:T(8,128)(2,1)S(1)}, bf16[16,2,32,768]{3,2,1,0:T(8,128)(2,1)S(1)}, u32[]{:S(2)}, u32[]{:S(2)}) collective-permute-start(bf16[16,2,32,768]{3,2,1,0:T(8,128)(2,1)S(1)} %collective-permute-done.1), channel_id=1, source_target_pairs={{0,1},{1,0},{2,3},{3,2},{4,5},{5,4},{6,7},{7,6},{8,9},{9,8},{10,11... | collective-permute-start | bytes 4718600 | tf_op jit(solution)/shard_map/ppermute | solution.py:147
  115.7 39.9 %copy-start.23 = (bf16[8,32,768]{2,1,0:T(8,128)(2,1)}, bf16[8,32,768]{2,1,0:T(8,128)(2,1)S(1)}, u32[]{:S(2)}) copy-start(bf16[8,32,768]{2,1,0:T(8,128)(2,1)S(1)} %collective-permute-done.11) | copy-start | bytes 1179652
  115.8 17.0 %collective-permute-start.2 = (bf16[8,2,32,768]{3,2,1,0:T(8,128)(2,1)S(1)}, bf16[8,2,32,768]{3,2,1,0:T(8,128)(2,1)S(1)}, u32[]{:S(2)}, u32[]{:S(2)}) collective-permute-start(bf16[8,2,32,768]{3,2,1,0:T(8,128)(2,1)S(1)} %slice.16), channel_id=1, source_target_pairs={{0,16},{16,32},{32,48},{48,0},{1,17},{17,33},{33,49},{49,1},{2,18}... | collective-permute-start | bytes 2359304 | tf_op jit(solution)/shard_map/ppermute | solution.py:145
  115.8 21.2 %collective-permute-start.3 = (bf16[8,2,32,768]{3,2,1,0:T(8,128)(2,1)S(1)}, bf16[8,2,32,768]{3,2,1,0:T(8,128)(2,1)S(1)}, u32[]{:S(2)}, u32[]{:S(2)}) collective-permute-start(bf16[8,2,32,768]{3,2,1,0:T(8,128)(2,1)S(1)} %slice.17), channel_id=1, source_target_pairs={{0,48},{16,0},{32,16},{48,32},{1,49},{17,1},{33,17},{49,33},{2,50}... | collective-permute-start | bytes 2359304 | tf_op jit(solution)/shard_map/ppermute | solution.py:145
  132.7 7.0 %copy-start.19 = (bf16[8,2,32,768]{3,2,1,0:T(8,128)(2,1)}, bf16[8,2,32,768]{3,2,1,0:T(8,128)(2,1)S(1)}, u32[]{:S(2)}) copy-start(bf16[8,2,32,768]{3,2,1,0:T(8,128)(2,1)S(1)} %collective-permute-done.2) | copy-start | bytes 2359300
  132.7 6.1 %collective-permute-start.7 = (bf16[8,2,32,768]{3,2,1,0:T(8,128)(2,1)S(1)}, bf16[8,2,32,768]{3,2,1,0:T(8,128)(2,1)S(1)}, u32[]{:S(2)}, u32[]{:S(2)}) collective-permute-start(bf16[8,2,32,768]{3,2,1,0:T(8,128)(2,1)S(1)} %collective-permute-done.2), channel_id=1, source_target_pairs={{0,1},{1,0},{2,3},{3,2},{4,5},{5,4},{6,7},{7,6},{8,9},{9,8},{10,11... | collective-permute-start | bytes 2359304 | tf_op jit(solution)/shard_map/ppermute | solution.py:147
  136.9 4.2 %copy-start.20 = (bf16[8,2,32,768]{3,2,1,0:T(8,128)(2,1)}, bf16[8,2,32,768]{3,2,1,0:T(8,128)(2,1)S(1)}, u32[]{:S(2)}) copy-start(bf16[8,2,32,768]{3,2,1,0:T(8,128)(2,1)S(1)} %collective-permute-done.3) | copy-start | bytes 2359300
  136.9 4.2 %collective-permute-start.8 = (bf16[8,2,32,768]{3,2,1,0:T(8,128)(2,1)S(1)}, bf16[8,2,32,768]{3,2,1,0:T(8,128)(2,1)S(1)}, u32[]{:S(2)}, u32[]{:S(2)}) collective-permute-start(bf16[8,2,32,768]{3,2,1,0:T(8,128)(2,1)S(1)} %collective-permute-done.3), channel_id=1, source_target_pairs={{0,1},{1,0},{2,3},{3,2},{4,5},{5,4},{6,7},{7,6},{8,9},{9,8},{10,11... | collective-permute-start | bytes 2359304 | tf_op jit(solution)/shard_map/ppermute | solution.py:147
  137.0 18.7 %collective-permute-start.13 = (bf16[16,32,768]{2,1,0:T(8,128)(2,1)S(1)}, bf16[16,32,768]{2,1,0:T(8,128)(2,1)}, u32[]{:S(2)}, u32[]{:S(2)}) collective-permute-start(bf16[16,32,768]{2,1,0:T(8,128)(2,1)S(1)} %all-to-all-done.1), channel_id=1, source_target_pairs={{0,1},{1,0},{2,3},{3,2},{4,5},{5,4},{6,7},{7,6},{8,9},{9,8},{10,11... | collective-permute-start | bytes 2359304 | tf_op jit(solution)/shard_map/ppermute | solution.py:147
  137.5 18.2 %collective-permute-start.14 = (bf16[16,32,768]{2,1,0:T(8,128)(2,1)S(1)}, bf16[16,32,768]{2,1,0:T(8,128)(2,1)}, u32[]{:S(2)}, u32[]{:S(2)}) collective-permute-start(bf16[16,32,768]{2,1,0:T(8,128)(2,1)S(1)} %collective-permute-done.9), channel_id=1, source_target_pairs={{0,1},{1,0},{2,3},{3,2},{4,5},{5,4},{6,7},{7,6},{8,9},{9,8},{10,11... | collective-permute-start | bytes 2359304 | tf_op jit(solution)/shard_map/ppermute | solution.py:147
  138.3 17.4 %collective-permute-start.15 = (bf16[16,32,768]{2,1,0:T(8,128)(2,1)}, bf16[16,32,768]{2,1,0:T(8,128)(2,1)}, u32[]{:S(2)}, u32[]{:S(2)}) collective-permute-start(bf16[16,32,768]{2,1,0:T(8,128)(2,1)} %collective-permute-done.10), channel_id=1, source_target_pairs={{0,1},{1,0},{2,3},{3,2},{4,5},{5,4},{6,7},{7,6},{8,9},{9,8},{10,11... | collective-permute-start | bytes 2359304 | tf_op jit(solution)/shard_map/ppermute | solution.py:147
  139.4 16.3 %collective-permute-start.16 = (bf16[8,32,768]{2,1,0:T(8,128)(2,1)S(1)}, bf16[8,32,768]{2,1,0:T(8,128)(2,1)}, u32[]{:S(2)}, u32[]{:S(2)}) collective-permute-start(bf16[8,32,768]{2,1,0:T(8,128)(2,1)S(1)} %collective-permute-done.11), channel_id=1, source_target_pairs={{0,1},{1,0},{2,3},{3,2},{4,5},{5,4},{6,7},{7,6},{8,9},{9,8},{10,11... | collective-permute-start | bytes 1179656 | tf_op jit(solution)/shard_map/ppermute | solution.py:147
  142.1 13.7 %collective-permute-start.17 = (bf16[8,32,768]{2,1,0:T(8,128)(2,1)}, bf16[8,32,768]{2,1,0:T(8,128)(2,1)}, u32[]{:S(2)}, u32[]{:S(2)}) collective-permute-start(bf16[8,32,768]{2,1,0:T(8,128)(2,1)} %collective-permute-done.12), channel_id=1, source_target_pairs={{0,1},{1,0},{2,3},{3,2},{4,5},{5,4},{6,7},{7,6},{8,9},{9,8},{10,11... | collective-permute-start | bytes 1179656 | tf_op jit(solution)/shard_map/ppermute | solution.py:147
  (14 other events, 26.5 us)

commit v4 on v3

--- a/solution.py
+++ b/solution.py
@@ -18,6 +18,11 @@
 ZUP = [(i, (i + 1) % RING) for i in range(RING)]
 ZDOWN = [(i, (i - 1) % RING) for i in range(RING)]
 SWAP = [(0, 1), (1, 0)]
+STEPS = (0, RING - 1, 1, 2)
+NEAR_TAGS = ((0, 0), (1, 0), (2, 0))
+FAR_TAGS = ((3, 0), (3, 1))
+NEAR_PARTS = 2 * len(NEAR_TAGS)
+FAR_PARTS = 2 * len(FAR_TAGS)
 LINE = 128
 LINES = 32
 MIB = 1024 * 1024
@@ -142,140 +147,190 @@
     half = piece.shape[0] // 2
     prev = lax.ppermute(piece, "z", ZUP)
     succ = lax.ppermute(piece, "z", ZDOWN)
-    far = [lax.ppermute(prev[:half], "z", ZUP), lax.ppermute(succ[half:], "z", ZDOWN)]
-    mine = [piece, prev, succ] + far
-    other = [lax.ppermute(part, "core", SWAP) for part in mine]
-    return [part.reshape((-1, 8) + part.shape[1:]) for part in mine + other]
-
-
-def place_copies(place_ref, parts, scratch, sem, kind=None):
-    z = place_ref[0]
+    low_far = lax.ppermute(prev[:half], "z", ZUP)
+    high_far = lax.ppermute(succ[half:], "z", ZDOWN)
+    return [piece, prev, succ], [low_far, high_far]
+
+
+def with_other_core(mine):
+    parts = mine + [lax.ppermute(part, "core", SWAP) for part in mine]
+    return [part.reshape((-1, 8) + part.shape[1:]) for part in parts]
+
+
+def share_copies(place_ref, parts, tags, lo, target_of, sem, kind=None):
     core = place_ref[1]
-    count = len(parts) // 2
     copies = []
     for index, part in enumerate(parts):
-        which = index % count
-        c = core if index < count else 1 - core
-        zz = lax.rem(z + (0, RING - 1, 1, 2, 2)[which], RING)
-        for lo in range(part.shape[0]):
-            low = lo if which != 4 else 1
-            source = part.at[lo] if kind is None else part.at[lo, :, kind]
-            copies.append(pltpu.make_async_copy(source, scratch.at[low, zz, :, c], sem))
+        which, first = tags[index % len(tags)]
+        if not first <= lo < first + part.shape[0]:
+            continue
+        c = core if index < len(tags) else 1 - core
+        source = part.at[lo - first] if kind is None else part.at[lo - first, :, kind]
+        copies.append(pltpu.make_async_copy(source, target_of(which).at[:, c], sem))
     return copies
 
 
-def hidden_kernel(place_ref, rows_any, *refs):
-    parts = refs[:-6]
-    out_ref, rows_ref, gate_ref, up_ref, acc_ref, sem = refs[-6:]
-    rows_copy = pltpu.make_async_copy(rows_any, rows_ref, sem.at[2])
-    rows_copy.start()
-    gate_copies = place_copies(place_ref, parts, gate_ref, sem.at[0], 0)
-    up_copies = place_copies(place_ref, parts, up_ref, sem.at[1], 1)
-    for copy in gate_copies + up_copies:
+def share_columns(place_ref, lo, which):
+    z = lax.rem(place_ref[0] + STEPS[which], RING)
+    return pl.ds(pl.multiple_of(lo * 2048 + z * 512, 512), 512)
+
+
+def near_kernel(place_ref, rows_any, *refs):
+    gate_parts, up_parts = refs[:NEAR_PARTS], refs[NEAR_PARTS : 2 * NEAR_PARTS]
+    gate_out, up_out, rows_ref, gate_ref, up_ref, sem = refs[2 * NEAR_PARTS :]
+    width = gate_out.shape[1]
+    depth = rows_ref.shape[2]
+    step = 256
+    copies = []
+    for lo in range(2):
+        group = []
+        for which in range(3):
+            source = rows_any.at[:, share_columns(place_ref, lo, which)]
+            target = rows_ref.at[lo, :, which * 512 : (which + 1) * 512]
+            group.append(pltpu.make_async_copy(source, target, sem.at[lo]))
+        gate_of = lambda which, lo=lo: gate_ref.at[lo, which]
+        up_of = lambda which, lo=lo: up_ref.at[lo, which]
+        group += share_copies(place_ref, gate_parts, NEAR_TAGS, lo, gate_of, sem.at[lo])
+        group += share_copies(place_ref, up_parts, NEAR_TAGS, lo, up_of, sem.at[lo], 0)
+        for copy in group:
+            copy.start()
+        copies.append(group)
+    for lo in range(2):
+        for copy in copies[lo]:
+            copy.wait()
+
+        @pl.loop(0, width // step)
+        def _(i):
+            cols = pl.ds(pl.multiple_of(i * step, step), step)
+            gate = gate_ref[lo, :, :, :, :, cols].reshape(depth, step)
+            up = up_ref[lo, :, :, :, :, cols].reshape(depth, step)
+            g = jnp.dot(rows_ref[lo], gate, preferred_element_type=jnp.float32)
+            u = jnp.dot(rows_ref[lo], up, preferred_element_type=jnp.float32)
+            if lo == 0:
+                gate_out[:, cols] = g
+                up_out[:, cols] = u
+            else:
+                gate_out[:, cols] += g
+                up_out[:, cols] += u
+
+
+def near_call(place, rows, gate_parts, up_parts):
+    count, depth = rows.shape
+    width = gate_parts[0].shape[-1]
+    any_place = pl.BlockSpec(memory_space=pl.ANY)
+    vmem = pl.BlockSpec(memory_space=pltpu.VMEM)
+    weight = pltpu.VMEM((2, 3, 8, 2, 32, width), jnp.bfloat16)
+    total = jax.ShapeDtypeStruct((count, width), jnp.float32)
+    return pl.pallas_call(
+        near_kernel,
+        out_shape=(total, total),
+        in_specs=[pl.BlockSpec(memory_space=pltpu.SMEM)] + [any_place] * (1 + 2 * NEAR_PARTS),
+        out_specs=(vmem, vmem),
+        scratch_shapes=[
+            pltpu.VMEM((2, count, 3 * 512), jnp.bfloat16),
+            weight,
+            weight,
+            pltpu.SemaphoreType.DMA((2,)),
+        ],
+        compiler_params=pltpu.CompilerParams(vmem_limit_bytes=52 * MIB),
+        cost_estimate=pl.CostEstimate(
+            flops=3 * count * depth * width,
+            bytes_accessed=3 * depth * width + 2 * count * depth,
+            transcendentals=0,
+        ),
+        name="near",
+    )(place, rows, *gate_parts, *up_parts)
+
+
+def rest_kernel(place_ref, gate_sum, up_sum, rows_any, *refs):
+    gate_parts, up_parts = refs[:FAR_PARTS], refs[FAR_PARTS : 2 * FAR_PARTS]
+    near_parts = refs[2 * FAR_PARTS : 2 * FAR_PARTS + NEAR_PARTS]
+    out_any, rows_ref, gate_ref, up_ref, down_ref, hidden_ref, out_ref, sem, out_sem = refs[
+        2 * FAR_PARTS + NEAR_PARTS :
+    ]
+    width = gate_sum.shape[1]
+    step = 256
+    copies = []
+    for lo in range(2):
+        source = rows_any.at[:, share_columns(place_ref, lo, 3)]
+        target = rows_ref.at[:, lo * 512 : (lo + 1) * 512]
+        copies.append(pltpu.make_async_copy(source, target, sem.at[0]))
+        gate_of = lambda which, lo=lo: gate_ref.at[lo]
+        up_of = lambda which, lo=lo: up_ref.at[lo]
+        copies += share_copies(place_ref, gate_parts, FAR_TAGS, lo, gate_of, sem.at[0])
+        copies += share_copies(place_ref, up_parts, FAR_TAGS, lo, up_of, sem.at[0], 0)
+    down_copies = []
+    for lo in range(2):
+        down_of = lambda which, lo=lo: down_ref.at[lo, which]
+        group = share_copies(place_ref, near_parts, NEAR_TAGS, lo, down_of, sem.at[1 + lo], 1)
+        group += share_copies(place_ref, up_parts, FAR_TAGS, lo, down_of, sem.at[1 + lo], 1)
+        down_copies.append(group)
+    for copy in copies + down_copies[0] + down_copies[1]:
         copy.start()
-    rows_copy.wait()
-    for copy in gate_copies:
+    for copy in copies:
         copy.wait()
-    depth = rows_ref.shape[1]
-    width = out_ref.shape[1]
-    step = 256
 
     @pl.loop(0, width // step)
     def _(i):
         cols = pl.ds(pl.multiple_of(i * step, step), step)
-        gate = gate_ref[:, :, :, :, :, cols].reshape(depth, step)
-        g = jnp.dot(rows_ref[...], gate, preferred_element_type=jnp.float32)
-        acc_ref[:, cols] = g / (1.0 + jnp.exp(-g))
-
-    for copy in up_copies:
-        copy.wait()
-
-    @pl.loop(0, width // step)
-    def _(i):
-        cols = pl.ds(pl.multiple_of(i * step, step), step)
-        up = up_ref[:, :, :, :, :, cols].reshape(depth, step)
-        u = jnp.dot(rows_ref[...], up, preferred_element_type=jnp.float32)
-        out_ref[:, cols] = (acc_ref[:, cols] * u).astype(out_ref.dtype)
-
-
-def hidden_call(place, rows, parts):
+        rows = rows_ref[...]
+        gate = gate_ref[:, :, :, :, cols].reshape(1024, step)
+        up = up_ref[:, :, :, :, cols].reshape(1024, step)
+        g = gate_sum[:, cols] + jnp.dot(rows, gate, preferred_element_type=jnp.float32)
+        u = up_sum[:, cols] + jnp.dot(rows, up, preferred_element_type=jnp.float32)
+        hidden_ref[:, cols] = (g / (1.0 + jnp.exp(-g)) * u).astype(hidden_ref.dtype)
+
+    outs = []
+    for lo in range(2):
+        for copy in down_copies[lo]:
+            copy.wait()
+        for which in range(RING):
+            chunk = lo * RING + which
+            weight = down_ref[lo, which].reshape(512, width)
+            out_ref[chunk] = lax.dot_general(
+                hidden_ref[...],
+                weight,
+                (((1,), (1,)), ((), ())),
+                preferred_element_type=jnp.float32,
+            ).astype(out_ref.dtype)
+            target = out_any.at[:, share_columns(place_ref, lo, which)]
+            out = pltpu.make_async_copy(out_ref.at[chunk], target, out_sem.at[chunk])
+            out.start()
+            outs.append(out)
+    for out in outs:
+        out.wait()
+
+
+def rest_call(place, sums, rows, gate_parts, up_parts, near_parts):
     count, depth = rows.shape
-    width = parts[0].shape[-1]
-    hbm = pl.BlockSpec(memory_space=pl.ANY)
-    weight = pltpu.VMEM((2, RING, 8, 2, 32, width), jnp.bfloat16)
+    width = gate_parts[0].shape[-1]
+    any_place = pl.BlockSpec(memory_space=pl.ANY)
+    vmem = pl.BlockSpec(memory_space=pltpu.VMEM)
+    weight = pltpu.VMEM((2, 8, 2, 32, width), jnp.bfloat16)
     return pl.pallas_call(
-        hidden_kernel,
-        out_shape=jax.ShapeDtypeStruct((count, width), jnp.bfloat16),
-        in_specs=[pl.BlockSpec(memory_space=pltpu.SMEM)]
-        + [hbm] * (1 + len(parts)),
-        out_specs=pl.BlockSpec(memory_space=pltpu.VMEM),
+        rest_kernel,
+        out_shape=jax.ShapeDtypeStruct((count, depth), jnp.bfloat16),
+        in_specs=[pl.BlockSpec(memory_space=pltpu.SMEM), vmem, vmem]
+        + [any_place] * (1 + 2 * FAR_PARTS + NEAR_PARTS),
+        out_specs=any_place,
         scratch_shapes=[
-            pltpu.VMEM((count, depth), jnp.bfloat16),
+            pltpu.VMEM((count, 1024), jnp.bfloat16),
             weight,
             weight,
-            pltpu.VMEM((count, width), jnp.float32),
+            pltpu.VMEM((2, RING, 8, 2, 32, width), jnp.bfloat16),
+            pltpu.VMEM((count, width), jnp.bfloat16),
+            pltpu.VMEM((2 * RING, count, 512), jnp.bfloat16),
             pltpu.SemaphoreType.DMA((3,)),
+            pltpu.SemaphoreType.DMA((2 * RING,)),
         ],
-        compiler_params=pltpu.CompilerParams(vmem_limit_bytes=56 * MIB),
+        compiler_params=pltpu.CompilerParams(vmem_limit_bytes=52 * MIB),
         cost_estimate=pl.CostEstimate(
-            flops=4 * count * depth * width,
-            bytes_accessed=4 * depth * width + 2 * count * depth,
+            flops=3 * count * depth * width,
+            bytes_accessed=3 * depth * width + 2 * count * depth,
             transcendentals=count * width,
         ),
-        name="hidden",
-    )(place, rows, *parts)
-
-
-def project_kernel(place_ref, hidden_ref, *refs):
-    parts = refs[:-5]
-    out_any, scratch, out_ref, sem, out_sem = refs[-5:]
-    copies = place_copies(place_ref, parts, scratch, sem)
-    for copy in copies:
-        copy.start()
-    for copy in copies:
-        copy.wait()
-    hidden = hidden_ref[...]
-    outs = []
-    for chunk in range(2 * RING):
-        weight = scratch[chunk // RING, chunk % RING].reshape(512, hidden.shape[1])
-        cols = slice(chunk * 512, (chunk + 1) * 512)
-        out_ref[:, cols] = lax.dot_general(
-            hidden, weight, (((1,), (1,)), ((), ())), preferred_element_type=jnp.float32
-        ).astype(out_ref.dtype)
-        out = pltpu.make_async_copy(out_ref.at[:, cols], out_any.at[:, cols], out_sem.at[chunk])
-        out.start()
-        outs.append(out)
-    for out in outs:
-        out.wait()
-
-
-def project_call(place, hidden, parts):
-    count, width = hidden.shape
-    depth = 4096
-    hbm = pl.BlockSpec(memory_space=pl.ANY)
-    return pl.pallas_call(
-        project_kernel,
-        out_shape=jax.ShapeDtypeStruct((count, depth), jnp.bfloat16),
-        in_specs=[
-            pl.BlockSpec(memory_space=pltpu.SMEM),
-            pl.BlockSpec(memory_space=pltpu.VMEM),
-        ]
-        + [hbm] * len(parts),
-        out_specs=hbm,
-        scratch_shapes=[
-            pltpu.VMEM((2, RING, 8, 2, 32, width), jnp.bfloat16),
-            pltpu.VMEM((count, depth), jnp.bfloat16),
-            pltpu.SemaphoreType.DMA,
-            pltpu.SemaphoreType.DMA((2 * RING,)),
-        ],
-        compiler_params=pltpu.CompilerParams(vmem_limit_bytes=56 * MIB),
-        cost_estimate=pl.CostEstimate(
-            flops=2 * count * depth * width,
-            bytes_accessed=2 * depth * width + 2 * count * depth,
-            transcendentals=0,
-        ),
-        name="project",
-    )(place, hidden, *parts)
+        name="rest",
+    )(place, *sums, rows, *gate_parts, *up_parts, *near_parts)
 
 
 def combine_kernel(weighs_ref, picked_ref, middle_ref, back_ref, layer_ref, parcel_ref, rows_ref):
@@ -374,10 +429,11 @@
     place = jnp.stack([lax.axis_index("z"), lax.axis_index("core")]).astype(jnp.int32)
 
     to_chip = lambda part: lax.all_to_all(part, PLANE, split_axis=0, concat_axis=0, tiled=True)
-    pair = to_chip(jnp.stack([gate_weight, up_weight], axis=1))
-    down = to_chip(jnp.swapaxes(down_weight, 1, 2))
-    pair_parts = spread_piece(pair)
-    down_parts = spread_piece(down)
+    gate = to_chip(gate_weight)
+    pair = jnp.stack([up_weight, jnp.swapaxes(down_weight, 1, 2)], axis=1)
+    pair, queries, gate = lax.optimization_barrier((pair, queries, gate))
+    pair = to_chip(pair)
+    gate_near, gate_far = spread_piece(gate)
 
     expert_range = jnp.arange(experts, dtype=jnp.int32)
     hit_table = expert_ids[:, :, None] == expert_range[None, None, :]
@@ -417,7 +473,8 @@
         norm_gain,
         pick,
     )
-    outgoing, _, _ = lax.optimization_barrier((outgoing, pair, down))
+    pair, outgoing, _, _ = lax.optimization_barrier((pair, outgoing, gate_near[1], gate_near[2]))
+    pair_near, pair_far = spread_piece(pair)
     received = lax.all_to_all(
         outgoing.reshape(experts, capacity, model_width),
         PLANE,
@@ -426,8 +483,12 @@
         tiled=True,
     ).reshape(slots, model_width)
 
-    hidden = hidden_call(place, received, pair_parts)
-    expert_out = project_call(place, hidden, down_parts)
+    pair_near = with_other_core(pair_near)
+    sums = near_call(place, received, with_other_core(gate_near), pair_near)
+    gate_far = with_other_core(gate_far)
+    low_far, high_far, *sums = lax.optimization_barrier((*pair_far, *sums))
+    pair_far = with_other_core([low_far, high_far])
+    expert_out = rest_call(place, sums, received, gate_far, pair_far, pair_near)
     returned = lax.all_to_all(
         expert_out.reshape(experts, capacity, model_width),
         PLANE,

time: 254 us -> 236 us (0.929)
  waiting for transfers between devices: 76.1 us -> 47.9 us
  starting transfers between devices: 41.2 us -> 49.4 us
  local copies, waits for them, and re-layouts: 7.59 us -> 10.7 us
    ppermute x2, waiting for transfers between devices: 46.3 us -> 1.82 us  [spread_piece(): prev = lax.ppermute(piece, 'z', ZUP)]
    ppermute x2, waiting for transfers between devices: 0.01 us -> 25.9 us  [spread_piece(): succ = lax.ppermute(piece, 'z', ZDOWN)]
    ppermute x14, starting transfers between devices: 15.7 us -> 25.2 us  [the longest x10 20.3 us: with_other_core(): parts = mine + [lax.ppermute(part, 'core', SWAP) for part in mine]]
    ppermute x14, waiting for transfers between devices: 15.7 us -> 6.37 us  [the longest x10 3.59 us: with_other_core(): parts = mine + [lax.ppermute(part, 'core', SWAP) for part in mine]]
    slice x4, local copies, waits for them, and re-layouts: 1.32 us -> 4.8 us  [the longest x2 3.1 us: spread_piece(): high_far = lax.ppermute(succ[half:], 'z', ZDOWN)]
    unnamed x51 -> x45, local copies, waits for them, and re-layouts: 5.64 us -> 5.26 us
  transfers between devices with their start and end apart: 21 -> 21, of which waited for: 5 -> 9; matrix products, arithmetic and copies ran while one was open for 2% -> 4% of each run, Pallas kernels for 10% -> 10%
where the time goes in v4:
time: 236 us; the launch traced here: 235 us
  blocking collectives  80.4 us (34%)
  starting transfers between devices  49.4 us (21%)
  waiting for transfers between devices  47.9 us (20%)
  Pallas kernels  42.4 us (18%)
  local copies, waits for them, and re-layouts  10.7 us (5%)
  other arithmetic  3.06 us (1%)
    all_to_all x1, blocking collectives, shards(): lax.all_to_all(expert_out.reshape(experts, capacity, model_width), PLANE,...  56.2 us
    ppermute x2, waiting for transfers between devices, spread_piece(): succ = lax.ppermute(piece, 'z', ZDOWN)  25.9 us
    all_to_all x1, blocking collectives, shards(): lax.all_to_all(parcel, AXES, split_axis=0, concat_axis=0, tiled=True)  24.3 us
    ppermute x10, starting transfers between devices, with_other_core(): parts = mine + [lax.ppermute(part, 'core', SWAP) for part in mine]  20.3 us
    pallas_call x1, Pallas kernels, attend_call(): pl.pallas_call(attend_kernel, grid=(rows // block,), out_shape=(jax.Shape...  12.9 us
    all_to_all x2, starting transfers between devices, shards(): lax.all_to_all(part, PLANE, split_axis=0, concat_axis=0, tiled=True)  12.4 us
    all_to_all x2, waiting for transfers between devices, shards(): lax.all_to_all(part, PLANE, split_axis=0, concat_axis=0, tiled=True)  11.6 us
    pallas_call x1, Pallas kernels, near_call(): pl.pallas_call(near_kernel, out_shape=(total, total), in_specs=[pl.BlockS...  10.7 us
  transfers between devices with their start and end apart: 21, of which 9 were waited for; matrix products, arithmetic and copies ran while one was open for 4% of the time, Pallas kernels for 10%

profile of v4, /device:TPU:1, one launch (start us, length us, event | category | flops | bytes accessed | tf_op | source)
XLA Modules:
  0.0 235.0 jit_solution(9825093749679973145)
XLA Ops:
  0.7 7.7 %all-to-all-start = ((bf16[16,32,768]{2,1,0:T(8,128)(2,1)}), bf16[16,32,768]{2,1,0:T(8,128)(2,1)S(1)}, u32[]{:S(2)}, u32[]{:S(2)}) async-start(bf16[16,32,768]{2,1,0:T(8,128)(2,1)} %param.27), calls=%async_computation | async-start | bytes 1572864 | tf_op jit(solution)/shard_map/all_to_all | solution.py:431
  8.5 1.3 pad_maximum_fusion
  9.8 11.6 %all-to-all-done = bf16[16,32,768]{2,1,0:T(8,128)(2,1)S(1)} async-done(((bf16[16,32,768]{2,1,0:T(8,128)(2,1)}), bf16[16,32,768]{2,1,0:T(8,128)(2,1)S(1)}, u32[]{:S(2)}, u32[]{:S(2)}) %all-to-all-start) | async-done | bytes 786464 | tf_op jit(solution)/shard_map/all_to_all | solution.py:431
  21.4 4.7 %all-to-all-start.1 = ((bf16[16,2,32,768]{3,2,1,0:T(8,128)(2,1)}), bf16[16,2,32,768]{3,2,1,0:T(8,128)(2,1)}, u32[]{:S(2)}, u32[]{:S(2)}) async-start(bf16[16,2,32,768]{3,2,1,0:T(8,128)(2,1)} %pad_maximum_fusion), calls=%async_computation.1 | async-start | bytes 3145728 | tf_op jit(solution)/shard_map/all_to_all | solution.py:431
  26.2 1.2 select_reduce_fusion
  28.1 3.8 %collective-permute-start.1 = (bf16[16,32,768]{2,1,0:T(8,128)(2,1)S(1)}, bf16[16,32,768]{2,1,0:T(8,128)(2,1)}, u32[]{:S(2)}, u32[]{:S(2)}) collective-permute-start(bf16[16,32,768]{2,1,0:T(8,128)(2,1)S(1)} %all-to-all-done), channel_id=1, source_target_pairs={{0,48},{16,0},{32,16},{48,32},{1,49},{17,1},{33,17},{49,33},{2,50}... | collective-permute-start | bytes 2359304 | tf_op jit(solution)/shard_map/ppermute | solution.py:149
  32.7 12.9 %attend.1 = (f32[64,4096]{1,0:T(8,128)S(1)}, bf16[512,4096]{1,0:T(8,128)(2,1)S(1)}) custom-call(s32[64]{0:T(128)S(1)} %copy-done.5, bf16[64,32,128]{2,1,0:T(8,128)(2,1)S(1)} %bitcast.49, bf16[64,256,256]{2,1,0:T(8,128)(2,1)} %k_ref.1, bf16[64,256,256]{2,1,0:T(8,128)(2,1)} %v_ref.1, bf16[64,256]{1,0:T(8,128)(2,1)S(1)} %copy-done.2, ...), custom_call_target="tpu_custom_call" | custom-call | flops 536870912 | bytes 67108864 | tf_op jit(solution)/shard_map/attend/pallas_call | solution.py:106
  45.6 2.0 copy-done
  47.6 1.8 collective-permute-done
  49.4 6.5 %all-to-all-start.2 = ((bf16[16,32,4096]{2,1,0:T(8,128)(2,1)}), bf16[16,32,4096]{2,1,0:T(8,128)(2,1)}, u32[]{:S(2)}, u32[]{:S(2)}) async-start(bf16[16,32,4096]{2,1,0:T(8,128)(2,1)} %bitcast.47), calls=%async_computation.2 | async-start | bytes 8388608 | tf_op jit(solution)/shard_map/all_to_all | solution.py:478
  55.9 1.2 collective-permute-start.4
  57.5 4.7 %collective-permute-start.6 = (bf16[16,32,768]{2,1,0:T(8,128)(2,1)S(1)}, bf16[16,32,768]{2,1,0:T(8,128)(2,1)S(1)}, u32[]{:S(2)}, u32[]{:S(2)}) collective-permute-start(bf16[16,32,768]{2,1,0:T(8,128)(2,1)S(1)} %all-to-all-done), channel_id=1, source_target_pairs={{0,1},{1,0},{2,3},{3,2},{4,5},{5,4},{6,7},{7,6},{8,9},{9,8},{10,11... | collective-permute-start | bytes 2359304 | tf_op jit(solution)/shard_map/ppermute | solution.py:156
  62.2 25.9 %collective-permute-done.4 = bf16[16,2,32,768]{3,2,1,0:T(8,128)(2,1)S(1)} collective-permute-done((bf16[16,2,32,768]{3,2,1,0:T(8,128)(2,1)}, bf16[16,2,32,768]{3,2,1,0:T(8,128)(2,1)S(1)}, u32[]{:S(2)}, u32[]{:S(2)}) %collective-permute-start.4) | collective-permute-done | bytes 1572896 | tf_op jit(solution)/shard_map/ppermute | solution.py:149
  88.1 4.9 %collective-permute-start.11 = (bf16[16,2,32,768]{3,2,1,0:T(8,128)(2,1)S(1)}, bf16[16,2,32,768]{3,2,1,0:T(8,128)(2,1)S(1)}, u32[]{:S(2)}, u32[]{:S(2)}) collective-permute-start(bf16[16,2,32,768]{3,2,1,0:T(8,128)(2,1)S(1)} %collective-permute-done.4), channel_id=1, source_target_pairs={{0,1},{1,0},{2,3},{3,2},{4,5},{5,4},{6,7},{7,6},{8,9},{9,8},{10,11... | collective-permute-start | bytes 4718600 | tf_op jit(solution)/shard_map/ppermute | solution.py:156
  93.0 2.3 collective-permute-start.10
  98.7 2.0 collective-permute-done.8
  100.7 2.4 %collective-permute-start.5 = (bf16[8,2,32,768]{3,2,1,0:T(8,128)(2,1)}, bf16[8,2,32,768]{3,2,1,0:T(8,128)(2,1)}, u32[]{:S(2)}, u32[]{:S(2)}) collective-permute-start(bf16[8,2,32,768]{3,2,1,0:T(8,128)(2,1)} %slice.17), channel_id=1, source_target_pairs={{0,48},{16,0},{32,16},{48,32},{1,49},{17,1},{33,17},{49,33},{2,50}... | collective-permute-start | bytes 2359304 | tf_op jit(solution)/shard_map/ppermute | solution.py:151
  103.1 2.1 slice.19
  106.0 2.4 %collective-permute-start.13 = (bf16[8,32,768]{2,1,0:T(8,128)(2,1)}, bf16[8,32,768]{2,1,0:T(8,128)(2,1)S(1)}, u32[]{:S(2)}, u32[]{:S(2)}) collective-permute-start(bf16[8,32,768]{2,1,0:T(8,128)(2,1)} %slice.19), channel_id=1, source_target_pairs={{0,48},{16,0},{32,16},{48,32},{1,49},{17,1},{33,17},{49,33},{2,50}... | collective-permute-start | bytes 1179656 | tf_op jit(solution)/shard_map/ppermute | solution.py:151
  108.5 1.1 copy-done.9
  109.5 2.2 all-to-all-done.2
  111.7 10.7 %near.1 = (f32[512,768]{1,0:T(8,128)}, f32[512,768]{1,0:T(8,128)}) custom-call(s32[2]{0:T(128)S(1)} %pad_add_fusion.place_ref, bf16[512,4096]{1,0:T(8,128)(2,1)} %bitcast.14.rows_any, bf16[2,8,32,768]{3,2,1,0:T(8,128)(2,1)S(1)} %bitcast.48, bf16[2,8,32,768]{3,2,1,0:T(8,128)(2,1)S(1)} %bitcast.50, bf16[2,8,32,768]{3,2,1,0:T(8,128)(2,1)} %bitcast.17.refs_2_, ...), custom_call_target="tpu_custom_call" | custom-call | flops 4831838208 | bytes 13631488 | tf_op jit(solution)/shard_map/near/pallas_call | solution.py:224
  123.1 4.9 %collective-permute-start.16 = (bf16[8,2,32,768]{3,2,1,0:T(8,128)(2,1)}, bf16[8,2,32,768]{3,2,1,0:T(8,128)(2,1)S(1)}, u32[]{:S(2)}, u32[]{:S(2)}) collective-permute-start(bf16[8,2,32,768]{3,2,1,0:T(8,128)(2,1)} %collective-permute-done.3), channel_id=1, source_target_pairs={{0,1},{1,0},{2,3},{3,2},{4,5},{5,4},{6,7},{7,6},{8,9},{9,8},{10,11... | collective-permute-start | bytes 2359304 | tf_op jit(solution)/shard_map/ppermute | solution.py:156
  128.5 1.1 collective-permute-start.15
  129.6 1.9 collective-permute-done.12
  131.5 1.5 collective-permute-start.14
  133.0 1.6 collective-permute-done.14
  135.7 10.6 %rest.1 = bf16[512,4096]{1,0:T(8,128)(2,1)} custom-call(s32[2]{0:T(128)S(1)} %pad_add_fusion.place_ref, f32[512,768]{1,0:T(8,128)} %get-tuple-element.34.gate_sum, f32[512,768]{1,0:T(8,128)} %get-tuple-element.35.up_sum, bf16[512,4096]{1,0:T(8,128)(2,1)} %bitcast.14.rows_any, bf16[1,8,32,768]{3,2,1,0:T(8,128)(2,1)} %bitcast.27.refs_0_, ...), custom_call_target="tpu_custom_call" | custom-call | flops 4831838208 | bytes 13631488 | tf_op jit(solution)/shard_map/rest/pallas_call | solution.py:310
  146.4 56.2 %all_to_all.25 = bf16[16,32,4096]{2,1,0:T(8,128)(2,1)S(1)} all-to-all(bf16[16,32,4096]{2,1,0:T(8,128)(2,1)} %bitcast.55), channel_id=1, replica_groups=mesh['ylo'=2,'z'=4,'x'=4,'yhi'=2,'core'=2] {'ylo','x','yhi'}, dimensions={0} | all-to-all | bytes 8388608 | tf_op jit(solution)/shard_map/all_to_all | solution.py:492
  202.5 5.4 %combine.1 = (bf16[64,4096]{1,0:T(8,128)(2,1)}, bf16[128,32,128]{2,1,0:T(8,128)(2,1)S(1)}) custom-call(bf16[128,512]{1,0:T(8,128)(2,1)S(1)} %pad_maximum_fusion.1.weighs_ref, bf16[128,64]{1,0:T(8,128)(2,1)S(1)} %fusion.4.picked_ref, f32[64,4096]{1,0:T(8,128)S(1)} %get-tuple-element.25.middle_ref, bf16[512,4096]{1,0:T(8,128)(2,1)S(1)} %bitcast.46), custom_call_target="tpu_custom_call" | custom-call | tf_op jit(solution)/shard_map/combine/pallas_call | solution.py:364
  207.9 24.3 %all_to_all.26.lines_ref = bf16[128,32,128]{2,1,0:T(8,128)(2,1)S(1)} all-to-all(bf16[128,32,128]{2,1,0:T(8,128)(2,1)S(1)} %get-tuple-element.39), channel_id=1, replica_groups=mesh['ylo'=2,'z'=4,'x'=4,'yhi'=2,'core'=2] {'ylo','z','x','yhi','core'}, dimensions={0} | all-to-all | bytes 2097152 | tf_op jit(solution)/shard_map/all_to_all | solution.py:501
  232.2 2.8 %unpack.1 = bf16[128,4096]{1,0:T(8,128)(2,1)} custom-call(bf16[128,32,128]{2,1,0:T(8,128)(2,1)S(1)} %all_to_all.26.lines_ref), custom_call_target="tpu_custom_call" | custom-call | tf_op jit(solution)/shard_map/unpack/pallas_call | solution.py:396
  (90 shorter events, 8.2 us)
Async XLA Ops:
  0.6 7.8 %copy-start.18 = (s32[64,8]{0,1:T(8,128)S(1)}, s32[64,8]{0,1:T(8,128)}, u32[]{:S(2)}) copy-start(s32[64,8]{0,1:T(8,128)} %param.23) | copy-start | bytes 6148
  0.6 7.8 %copy-start.12 = (bf16[16,768,32]{1,2,0:T(8,128)(2,1)S(1)}, bf16[16,768,32]{1,2,0:T(8,128)(2,1)}, u32[]{:S(2)}) copy-start(bf16[16,768,32]{1,2,0:T(8,128)(2,1)} %param.29) | copy-start | bytes 2359300
  0.7 7.8 %copy-start.13 = (bf16[16,32,768]{2,1,0:T(8,128)(2,1)S(1)}, bf16[16,32,768]{2,1,0:T(8,128)(2,1)}, u32[]{:S(2)}) copy-start(bf16[16,32,768]{2,1,0:T(8,128)(2,1)} %param.28) | copy-start | bytes 2359300
  0.7 20.8 %all-to-all-start = ((bf16[16,32,768]{2,1,0:T(8,128)(2,1)}), bf16[16,32,768]{2,1,0:T(8,128)(2,1)S(1)}, u32[]{:S(2)}, u32[]{:S(2)}) async-start(bf16[16,32,768]{2,1,0:T(8,128)(2,1)} %param.27), calls=%async_computation | async-start | bytes 1572864 | tf_op jit(solution)/shard_map/all_to_all | solution.py:431
  9.8 18.0 %copy-start.19 = (f32[64,8]{0,1:T(8,128)S(1)}, f32[64,8]{0,1:T(8,128)}, u32[]{:S(2)}) copy-start(f32[64,8]{0,1:T(8,128)} %param.24) | copy-start | bytes 6148
  21.4 28.0 %all-to-all-start.1 = ((bf16[16,2,32,768]{3,2,1,0:T(8,128)(2,1)}), bf16[16,2,32,768]{3,2,1,0:T(8,128)(2,1)}, u32[]{:S(2)}, u32[]{:S(2)}) async-start(bf16[16,2,32,768]{3,2,1,0:T(8,128)(2,1)} %pad_maximum_fusion), calls=%async_computation.1 | async-start | bytes 3145728 | tf_op jit(solution)/shard_map/all_to_all | solution.py:431
  26.2 5.8 %copy-start.20 = (s32[64]{0:T(128)S(1)}, s32[64]{0:T(128)}, u32[]{:S(2)}) copy-start(s32[64]{0:T(128)} %param.26) | copy-start | bytes 772
  26.2 6.4 %copy-start.17 = (bf16[64,4096]{1,0:T(8,128)(2,1)S(1)}, bf16[64,4096]{1,0:T(8,128)(2,1)}, u32[]{:S(2)}) copy-start(bf16[64,4096]{1,0:T(8,128)(2,1)} %param.16) | copy-start | bytes 1572868
  27.8 4.8 %copy-start.1 = (bf16[64,4096]{1,0:T(8,128)(2,1)S(1)}, bf16[64,4096]{1,0:T(8,128)(2,1)}, u32[]{:S(2)}) copy-start(bf16[64,4096]{1,0:T(8,128)(2,1)} %hidden_ref.1) | copy-start | bytes 1572868
  28.1 19.5 %collective-permute-start.1 = (bf16[16,32,768]{2,1,0:T(8,128)(2,1)S(1)}, bf16[16,32,768]{2,1,0:T(8,128)(2,1)}, u32[]{:S(2)}, u32[]{:S(2)}) collective-permute-start(bf16[16,32,768]{2,1,0:T(8,128)(2,1)S(1)} %all-to-all-done), channel_id=1, source_target_pairs={{0,48},{16,0},{32,16},{48,32},{1,49},{17,1},{33,17},{49,33},{2,50}... | collective-permute-start | bytes 2359304 | tf_op jit(solution)/shard_map/ppermute | solution.py:149
  31.9 17.5 %collective-permute-start = (bf16[16,32,768]{2,1,0:T(8,128)(2,1)S(1)}, bf16[16,32,768]{2,1,0:T(8,128)(2,1)S(1)}, u32[]{:S(2)}, u32[]{:S(2)}) collective-permute-start(bf16[16,32,768]{2,1,0:T(8,128)(2,1)S(1)} %all-to-all-done), channel_id=1, source_target_pairs={{0,16},{16,32},{32,48},{48,0},{1,17},{17,33},{33,49},{49,1},{2,18}... | collective-permute-start | bytes 2359304 | tf_op jit(solution)/shard_map/ppermute | solution.py:148
  49.4 62.3 %all-to-all-start.2 = ((bf16[16,32,4096]{2,1,0:T(8,128)(2,1)}), bf16[16,32,4096]{2,1,0:T(8,128)(2,1)}, u32[]{:S(2)}, u32[]{:S(2)}) async-start(bf16[16,32,4096]{2,1,0:T(8,128)(2,1)} %bitcast.47), calls=%async_computation.2 | async-start | bytes 8388608 | tf_op jit(solution)/shard_map/all_to_all | solution.py:478
  55.9 32.1 %collective-permute-start.4 = (bf16[16,2,32,768]{3,2,1,0:T(8,128)(2,1)}, bf16[16,2,32,768]{3,2,1,0:T(8,128)(2,1)S(1)}, u32[]{:S(2)}, u32[]{:S(2)}) collective-permute-start(bf16[16,2,32,768]{3,2,1,0:T(8,128)(2,1)} %all-to-all-done.1), channel_id=1, source_target_pairs={{0,48},{16,0},{32,16},{48,32},{1,49},{17,1},{33,17},{49,33},{2,50}... | collective-permute-start | bytes 4718600 | tf_op jit(solution)/shard_map/ppermute | solution.py:149
  57.1 35.9 %collective-permute-start.2 = (bf16[16,2,32,768]{3,2,1,0:T(8,128)(2,1)}, bf16[16,2,32,768]{3,2,1,0:T(8,128)(2,1)S(1)}, u32[]{:S(2)}, u32[]{:S(2)}) collective-permute-start(bf16[16,2,32,768]{3,2,1,0:T(8,128)(2,1)} %all-to-all-done.1), channel_id=1, source_target_pairs={{0,16},{16,32},{32,48},{48,0},{1,17},{17,33},{33,49},{49,1},{2,18}... | collective-permute-start | bytes 4718600 | tf_op jit(solution)/shard_map/ppermute | solution.py:148
  57.5 37.9 %collective-permute-start.6 = (bf16[16,32,768]{2,1,0:T(8,128)(2,1)S(1)}, bf16[16,32,768]{2,1,0:T(8,128)(2,1)S(1)}, u32[]{:S(2)}, u32[]{:S(2)}) collective-permute-start(bf16[16,32,768]{2,1,0:T(8,128)(2,1)S(1)} %all-to-all-done), channel_id=1, source_target_pairs={{0,1},{1,0},{2,3},{3,2},{4,5},{5,4},{6,7},{7,6},{8,9},{9,8},{10,11... | collective-permute-start | bytes 2359304 | tf_op jit(solution)/shard_map/ppermute | solution.py:156
  62.2 43.8 %collective-permute-start.9 = (bf16[16,2,32,768]{3,2,1,0:T(8,128)(2,1)}, bf16[16,2,32,768]{3,2,1,0:T(8,128)(2,1)S(1)}, u32[]{:S(2)}, u32[]{:S(2)}) collective-permute-start(bf16[16,2,32,768]{3,2,1,0:T(8,128)(2,1)} %all-to-all-done.1), channel_id=1, source_target_pairs={{0,1},{1,0},{2,3},{3,2},{4,5},{5,4},{6,7},{7,6},{8,9},{9,8},{10,11... | collective-permute-start | bytes 4718600 | tf_op jit(solution)/shard_map/ppermute | solution.py:156
  88.1 10.6 %copy-start.6 = (bf16[16,2,32,768]{3,2,1,0:T(8,128)(2,1)}, bf16[16,2,32,768]{3,2,1,0:T(8,128)(2,1)S(1)}, u32[]{:S(2)}) copy-start(bf16[16,2,32,768]{3,2,1,0:T(8,128)(2,1)S(1)} %collective-permute-done.4) | copy-start | bytes 4718596
  88.1 20.3 %collective-permute-start.11 = (bf16[16,2,32,768]{3,2,1,0:T(8,128)(2,1)S(1)}, bf16[16,2,32,768]{3,2,1,0:T(8,128)(2,1)S(1)}, u32[]{:S(2)}, u32[]{:S(2)}) collective-permute-start(bf16[16,2,32,768]{3,2,1,0:T(8,128)(2,1)S(1)} %collective-permute-done.4), channel_id=1, source_target_pairs={{0,1},{1,0},{2,3},{3,2},{4,5},{5,4},{6,7},{7,6},{8,9},{9,8},{10,11... | collective-permute-start | bytes 4718600 | tf_op jit(solution)/shard_map/ppermute | solution.py:156
  93.0 5.7 %copy-start.7 = (bf16[16,2,32,768]{3,2,1,0:T(8,128)(2,1)}, bf16[16,2,32,768]{3,2,1,0:T(8,128)(2,1)S(1)}, u32[]{:S(2)}) copy-start(bf16[16,2,32,768]{3,2,1,0:T(8,128)(2,1)S(1)} %collective-permute-done.2) | copy-start | bytes 4718596
  93.0 16.5 %collective-permute-start.10 = (bf16[16,2,32,768]{3,2,1,0:T(8,128)(2,1)S(1)}, bf16[16,2,32,768]{3,2,1,0:T(8,128)(2,1)}, u32[]{:S(2)}, u32[]{:S(2)}) collective-permute-start(bf16[16,2,32,768]{3,2,1,0:T(8,128)(2,1)S(1)} %collective-permute-done.2), channel_id=1, source_target_pairs={{0,1},{1,0},{2,3},{3,2},{4,5},{5,4},{6,7},{7,6},{8,9},{9,8},{10,11... | collective-permute-start | bytes 4718600 | tf_op jit(solution)/shard_map/ppermute | solution.py:156
  95.4 5.4 %collective-permute-start.8 = (bf16[16,32,768]{2,1,0:T(8,128)(2,1)}, bf16[16,32,768]{2,1,0:T(8,128)(2,1)S(1)}, u32[]{:S(2)}, u32[]{:S(2)}) collective-permute-start(bf16[16,32,768]{2,1,0:T(8,128)(2,1)} %collective-permute-done.1), channel_id=1, source_target_pairs={{0,1},{1,0},{2,3},{3,2},{4,5},{5,4},{6,7},{7,6},{8,9},{9,8},{10,11... | collective-permute-start | bytes 2359304 | tf_op jit(solution)/shard_map/ppermute | solution.py:156
  96.3 6.9 %collective-permute-start.7 = (bf16[16,32,768]{2,1,0:T(8,128)(2,1)S(1)}, bf16[16,32,768]{2,1,0:T(8,128)(2,1)S(1)}, u32[]{:S(2)}, u32[]{:S(2)}) collective-permute-start(bf16[16,32,768]{2,1,0:T(8,128)(2,1)S(1)} %collective-permute-done), channel_id=1, source_target_pairs={{0,1},{1,0},{2,3},{3,2},{4,5},{5,4},{6,7},{7,6},{8,9},{9,8},{10,11... | collective-permute-start | bytes 2359304 | tf_op jit(solution)/shard_map/ppermute | solution.py:156
  100.7 7.7 %copy-start.15 = (bf16[16,32,768]{2,1,0:T(8,128)(2,1)}, bf16[16,32,768]{2,1,0:T(8,128)(2,1)S(1)}, u32[]{:S(2)}) copy-start(bf16[16,32,768]{2,1,0:T(8,128)(2,1)S(1)} %collective-permute-done.8) | copy-start | bytes 2359300
  100.7 21.6 %collective-permute-start.5 = (bf16[8,2,32,768]{3,2,1,0:T(8,128)(2,1)}, bf16[8,2,32,768]{3,2,1,0:T(8,128)(2,1)}, u32[]{:S(2)}, u32[]{:S(2)}) collective-permute-start(bf16[8,2,32,768]{3,2,1,0:T(8,128)(2,1)} %slice.17), channel_id=1, source_target_pairs={{0,48},{16,0},{32,16},{48,32},{1,49},{17,1},{33,17},{49,33},{2,50}... | collective-permute-start | bytes 2359304 | tf_op jit(solution)/shard_map/ppermute | solution.py:151
  103.1 5.4 %copy-start.16 = (bf16[16,32,768]{2,1,0:T(8,128)(2,1)}, bf16[16,32,768]{2,1,0:T(8,128)(2,1)S(1)}, u32[]{:S(2)}) copy-start(bf16[16,32,768]{2,1,0:T(8,128)(2,1)S(1)} %collective-permute-done.7) | copy-start | bytes 2359300
  103.1 20.0 %collective-permute-start.3 = (bf16[8,2,32,768]{3,2,1,0:T(8,128)(2,1)}, bf16[8,2,32,768]{3,2,1,0:T(8,128)(2,1)}, u32[]{:S(2)}, u32[]{:S(2)}) collective-permute-start(bf16[8,2,32,768]{3,2,1,0:T(8,128)(2,1)} %slice.16), channel_id=1, source_target_pairs={{0,16},{16,32},{32,48},{48,0},{1,17},{17,33},{33,49},{49,1},{2,18}... | collective-permute-start | bytes 2359304 | tf_op jit(solution)/shard_map/ppermute | solution.py:150
  106.0 22.5 %collective-permute-start.13 = (bf16[8,32,768]{2,1,0:T(8,128)(2,1)}, bf16[8,32,768]{2,1,0:T(8,128)(2,1)S(1)}, u32[]{:S(2)}, u32[]{:S(2)}) collective-permute-start(bf16[8,32,768]{2,1,0:T(8,128)(2,1)} %slice.19), channel_id=1, source_target_pairs={{0,48},{16,0},{32,16},{48,32},{1,49},{17,1},{33,17},{49,33},{2,50}... | collective-permute-start | bytes 1179656 | tf_op jit(solution)/shard_map/ppermute | solution.py:151
  108.4 23.1 %collective-permute-start.12 = (bf16[8,32,768]{2,1,0:T(8,128)(2,1)}, bf16[8,32,768]{2,1,0:T(8,128)(2,1)}, u32[]{:S(2)}, u32[]{:S(2)}) collective-permute-start(bf16[8,32,768]{2,1,0:T(8,128)(2,1)} %slice.18), channel_id=1, source_target_pairs={{0,16},{16,32},{32,48},{48,0},{1,17},{17,33},{33,49},{49,1},{2,18}... | collective-permute-start | bytes 1179656 | tf_op jit(solution)/shard_map/ppermute | solution.py:150
  123.1 11.5 %collective-permute-start.16 = (bf16[8,2,32,768]{3,2,1,0:T(8,128)(2,1)}, bf16[8,2,32,768]{3,2,1,0:T(8,128)(2,1)S(1)}, u32[]{:S(2)}, u32[]{:S(2)}) collective-permute-start(bf16[8,2,32,768]{3,2,1,0:T(8,128)(2,1)} %collective-permute-done.3), channel_id=1, source_target_pairs={{0,1},{1,0},{2,3},{3,2},{4,5},{5,4},{6,7},{7,6},{8,9},{9,8},{10,11... | collective-permute-start | bytes 2359304 | tf_op jit(solution)/shard_map/ppermute | solution.py:156
  128.0 6.6 %collective-permute-start.17 = (bf16[8,2,32,768]{3,2,1,0:T(8,128)(2,1)}, bf16[8,2,32,768]{3,2,1,0:T(8,128)(2,1)S(1)}, u32[]{:S(2)}, u32[]{:S(2)}) collective-permute-start(bf16[8,2,32,768]{3,2,1,0:T(8,128)(2,1)} %collective-permute-done.5), channel_id=1, source_target_pairs={{0,1},{1,0},{2,3},{3,2},{4,5},{5,4},{6,7},{7,6},{8,9},{9,8},{10,11... | collective-permute-start | bytes 2359304 | tf_op jit(solution)/shard_map/ppermute | solution.py:156
  128.5 4.6 %collective-permute-start.15 = (bf16[8,32,768]{2,1,0:T(8,128)(2,1)S(1)}, bf16[8,32,768]{2,1,0:T(8,128)(2,1)S(1)}, u32[]{:S(2)}, u32[]{:S(2)}) collective-permute-start(bf16[8,32,768]{2,1,0:T(8,128)(2,1)S(1)} %collective-permute-done.13), channel_id=1, source_target_pairs={{0,1},{1,0},{2,3},{3,2},{4,5},{5,4},{6,7},{7,6},{8,9},{9,8},{10,11... | collective-permute-start | bytes 1179656 | tf_op jit(solution)/shard_map/ppermute | solution.py:156
  131.5 3.1 %collective-permute-start.14 = (bf16[8,32,768]{2,1,0:T(8,128)(2,1)}, bf16[8,32,768]{2,1,0:T(8,128)(2,1)S(1)}, u32[]{:S(2)}, u32[]{:S(2)}) collective-permute-start(bf16[8,32,768]{2,1,0:T(8,128)(2,1)} %collective-permute-done.12), channel_id=1, source_target_pairs={{0,1},{1,0},{2,3},{3,2},{4,5},{5,4},{6,7},{7,6},{8,9},{9,8},{10,11... | collective-permute-start | bytes 1179656 | tf_op jit(solution)/shard_map/ppermute | solution.py:156
  (11 other events, 29.6 us)

commit v5 on v4

--- a/solution.py
+++ b/solution.py
@@ -358,7 +358,7 @@
     rows, width = middle.shape
     slots = back.shape[0]
     learners = picked.shape[0]
-    step = 512
+    step = 1024
     whole = lambda shape: pl.BlockSpec(shape, lambda i: (0,) * len(shape))
     column = lambda count: pl.BlockSpec((count, step), lambda i: (0, i))
     return pl.pallas_call(
@@ -392,13 +392,14 @@
 
 def unpack_call(lines):
     count = lines.shape[0]
-    vmem = pl.BlockSpec(memory_space=pltpu.VMEM)
+    block = count // 4
     return pl.pallas_call(
         unpack_kernel,
+        grid=(4,),
         out_shape=jax.ShapeDtypeStruct((count, LINES * LINE), jnp.bfloat16),
-        in_specs=[vmem],
-        out_specs=vmem,
-        scratch_shapes=[pltpu.VMEM((count * LINES, LINE), jnp.float32)],
+        in_specs=[pl.BlockSpec((block, LINES, LINE), lambda i: (i, 0, 0))],
+        out_specs=pl.BlockSpec((block, LINES * LINE), lambda i: (i, 0)),
+        scratch_shapes=[pltpu.VMEM((block * LINES, LINE), jnp.float32)],
         compiler_params=pltpu.CompilerParams(vmem_limit_bytes=16 * MIB),
         name="unpack",
     )(lines)

time: 236 us -> 234 us (level)
  no operation moved by 1% of the time
where the time goes in v5:
time: 234 us; the launch traced here: 233 us
  blocking collectives  80.4 us (34%)
  starting transfers between devices  49.4 us (21%)
  waiting for transfers between devices  47.9 us (20%)
  Pallas kernels  40.6 us (17%)
  local copies, waits for them, and re-layouts  10.7 us (5%)
  other arithmetic  3.06 us (1%)
    all_to_all x1, blocking collectives, shards(): lax.all_to_all(expert_out.reshape(experts, capacity, model_width), PLANE,...  56.2 us
    ppermute x2, waiting for transfers between devices, spread_piece(): succ = lax.ppermute(piece, 'z', ZDOWN)  25.9 us
    all_to_all x1, blocking collectives, shards(): lax.all_to_all(parcel, AXES, split_axis=0, concat_axis=0, tiled=True)  24.3 us
    ppermute x10, starting transfers between devices, with_other_core(): parts = mine + [lax.ppermute(part, 'core', SWAP) for part in mine]  20.3 us
    pallas_call x1, Pallas kernels, attend_call(): pl.pallas_call(attend_kernel, grid=(rows // block,), out_shape=(jax.Shape...  12.9 us
    all_to_all x2, starting transfers between devices, shards(): lax.all_to_all(part, PLANE, split_axis=0, concat_axis=0, tiled=True)  12.4 us
    all_to_all x2, waiting for transfers between devices, shards(): lax.all_to_all(part, PLANE, split_axis=0, concat_axis=0, tiled=True)  11.6 us
    pallas_call x1, Pallas kernels, near_call(): pl.pallas_call(near_kernel, out_shape=(total, total), in_specs=[pl.BlockS...  10.7 us
  transfers between devices with their start and end apart: 21, of which 9 were waited for; matrix products, arithmetic and copies ran while one was open for 4% of the time, Pallas kernels for 10%

profile of v5, /device:TPU:1, one launch (start us, length us, event | category | flops | bytes accessed | tf_op | source)
XLA Modules:
  0.0 233.2 jit_solution(6719396550003854854)
XLA Ops:
  0.7 7.7 %all-to-all-start = ((bf16[16,32,768]{2,1,0:T(8,128)(2,1)}), bf16[16,32,768]{2,1,0:T(8,128)(2,1)S(1)}, u32[]{:S(2)}, u32[]{:S(2)}) async-start(bf16[16,32,768]{2,1,0:T(8,128)(2,1)} %param.27), calls=%async_computation | async-start | bytes 1572864 | tf_op jit(solution)/shard_map/all_to_all | solution.py:432
  8.5 1.3 pad_maximum_fusion
  9.8 11.6 %all-to-all-done = bf16[16,32,768]{2,1,0:T(8,128)(2,1)S(1)} async-done(((bf16[16,32,768]{2,1,0:T(8,128)(2,1)}), bf16[16,32,768]{2,1,0:T(8,128)(2,1)S(1)}, u32[]{:S(2)}, u32[]{:S(2)}) %all-to-all-start) | async-done | bytes 786464 | tf_op jit(solution)/shard_map/all_to_all | solution.py:432
  21.4 4.7 %all-to-all-start.1 = ((bf16[16,2,32,768]{3,2,1,0:T(8,128)(2,1)}), bf16[16,2,32,768]{3,2,1,0:T(8,128)(2,1)}, u32[]{:S(2)}, u32[]{:S(2)}) async-start(bf16[16,2,32,768]{3,2,1,0:T(8,128)(2,1)} %pad_maximum_fusion), calls=%async_computation.1 | async-start | bytes 3145728 | tf_op jit(solution)/shard_map/all_to_all | solution.py:432
  26.2 1.2 select_reduce_fusion
  28.1 3.8 %collective-permute-start.1 = (bf16[16,32,768]{2,1,0:T(8,128)(2,1)S(1)}, bf16[16,32,768]{2,1,0:T(8,128)(2,1)}, u32[]{:S(2)}, u32[]{:S(2)}) collective-permute-start(bf16[16,32,768]{2,1,0:T(8,128)(2,1)S(1)} %all-to-all-done), channel_id=1, source_target_pairs={{0,48},{16,0},{32,16},{48,32},{1,49},{17,1},{33,17},{49,33},{2,50}... | collective-permute-start | bytes 2359304 | tf_op jit(solution)/shard_map/ppermute | solution.py:149
  32.7 12.9 %attend.1 = (f32[64,4096]{1,0:T(8,128)S(1)}, bf16[512,4096]{1,0:T(8,128)(2,1)S(1)}) custom-call(s32[64]{0:T(128)S(1)} %copy-done.5, bf16[64,32,128]{2,1,0:T(8,128)(2,1)S(1)} %bitcast.49, bf16[64,256,256]{2,1,0:T(8,128)(2,1)} %k_ref.1, bf16[64,256,256]{2,1,0:T(8,128)(2,1)} %v_ref.1, bf16[64,256]{1,0:T(8,128)(2,1)S(1)} %copy-done.2, ...), custom_call_target="tpu_custom_call" | custom-call | flops 536870912 | bytes 67108864 | tf_op jit(solution)/shard_map/attend/pallas_call | solution.py:106
  45.6 2.0 copy-done
  47.6 1.8 collective-permute-done
  49.4 6.5 %all-to-all-start.2 = ((bf16[16,32,4096]{2,1,0:T(8,128)(2,1)}), bf16[16,32,4096]{2,1,0:T(8,128)(2,1)}, u32[]{:S(2)}, u32[]{:S(2)}) async-start(bf16[16,32,4096]{2,1,0:T(8,128)(2,1)} %bitcast.47), calls=%async_computation.2 | async-start | bytes 8388608 | tf_op jit(solution)/shard_map/all_to_all | solution.py:479
  55.9 1.2 collective-permute-start.4
  57.5 4.7 %collective-permute-start.6 = (bf16[16,32,768]{2,1,0:T(8,128)(2,1)S(1)}, bf16[16,32,768]{2,1,0:T(8,128)(2,1)S(1)}, u32[]{:S(2)}, u32[]{:S(2)}) collective-permute-start(bf16[16,32,768]{2,1,0:T(8,128)(2,1)S(1)} %all-to-all-done), channel_id=1, source_target_pairs={{0,1},{1,0},{2,3},{3,2},{4,5},{5,4},{6,7},{7,6},{8,9},{9,8},{10,11... | collective-permute-start | bytes 2359304 | tf_op jit(solution)/shard_map/ppermute | solution.py:156
  62.2 25.9 %collective-permute-done.4 = bf16[16,2,32,768]{3,2,1,0:T(8,128)(2,1)S(1)} collective-permute-done((bf16[16,2,32,768]{3,2,1,0:T(8,128)(2,1)}, bf16[16,2,32,768]{3,2,1,0:T(8,128)(2,1)S(1)}, u32[]{:S(2)}, u32[]{:S(2)}) %collective-permute-start.4) | collective-permute-done | bytes 1572896 | tf_op jit(solution)/shard_map/ppermute | solution.py:149
  88.1 4.9 %collective-permute-start.11 = (bf16[16,2,32,768]{3,2,1,0:T(8,128)(2,1)S(1)}, bf16[16,2,32,768]{3,2,1,0:T(8,128)(2,1)S(1)}, u32[]{:S(2)}, u32[]{:S(2)}) collective-permute-start(bf16[16,2,32,768]{3,2,1,0:T(8,128)(2,1)S(1)} %collective-permute-done.4), channel_id=1, source_target_pairs={{0,1},{1,0},{2,3},{3,2},{4,5},{5,4},{6,7},{7,6},{8,9},{9,8},{10,11... | collective-permute-start | bytes 4718600 | tf_op jit(solution)/shard_map/ppermute | solution.py:156
  93.0 2.3 %collective-permute-start.10 = (bf16[16,2,32,768]{3,2,1,0:T(8,128)(2,1)S(1)}, bf16[16,2,32,768]{3,2,1,0:T(8,128)(2,1)}, u32[]{:S(2)}, u32[]{:S(2)}) collective-permute-start(bf16[16,2,32,768]{3,2,1,0:T(8,128)(2,1)S(1)} %collective-permute-done.2), channel_id=1, source_target_pairs={{0,1},{1,0},{2,3},{3,2},{4,5},{5,4},{6,7},{7,6},{8,9},{9,8},{10,11... | collective-permute-start | bytes 4718600 | tf_op jit(solution)/shard_map/ppermute | solution.py:156
  98.7 2.0 collective-permute-done.8
  100.7 2.4 %collective-permute-start.5 = (bf16[8,2,32,768]{3,2,1,0:T(8,128)(2,1)}, bf16[8,2,32,768]{3,2,1,0:T(8,128)(2,1)}, u32[]{:S(2)}, u32[]{:S(2)}) collective-permute-start(bf16[8,2,32,768]{3,2,1,0:T(8,128)(2,1)} %slice.17), channel_id=1, source_target_pairs={{0,48},{16,0},{32,16},{48,32},{1,49},{17,1},{33,17},{49,33},{2,50}... | collective-permute-start | bytes 2359304 | tf_op jit(solution)/shard_map/ppermute | solution.py:151
  103.1 2.1 slice.19
  106.0 2.4 %collective-permute-start.13 = (bf16[8,32,768]{2,1,0:T(8,128)(2,1)}, bf16[8,32,768]{2,1,0:T(8,128)(2,1)S(1)}, u32[]{:S(2)}, u32[]{:S(2)}) collective-permute-start(bf16[8,32,768]{2,1,0:T(8,128)(2,1)} %slice.19), channel_id=1, source_target_pairs={{0,48},{16,0},{32,16},{48,32},{1,49},{17,1},{33,17},{49,33},{2,50}... | collective-permute-start | bytes 1179656 | tf_op jit(solution)/shard_map/ppermute | solution.py:151
  108.5 1.1 copy-done.9
  109.5 2.2 all-to-all-done.2
  111.7 10.7 %near.1 = (f32[512,768]{1,0:T(8,128)}, f32[512,768]{1,0:T(8,128)}) custom-call(s32[2]{0:T(128)S(1)} %pad_add_fusion.place_ref, bf16[512,4096]{1,0:T(8,128)(2,1)} %bitcast.14.rows_any, bf16[2,8,32,768]{3,2,1,0:T(8,128)(2,1)S(1)} %bitcast.48, bf16[2,8,32,768]{3,2,1,0:T(8,128)(2,1)S(1)} %bitcast.50, bf16[2,8,32,768]{3,2,1,0:T(8,128)(2,1)} %bitcast.17.refs_2_, ...), custom_call_target="tpu_custom_call" | custom-call | flops 4831838208 | bytes 13631488 | tf_op jit(solution)/shard_map/near/pallas_call | solution.py:224
  123.1 4.9 %collective-permute-start.16 = (bf16[8,2,32,768]{3,2,1,0:T(8,128)(2,1)}, bf16[8,2,32,768]{3,2,1,0:T(8,128)(2,1)S(1)}, u32[]{:S(2)}, u32[]{:S(2)}) collective-permute-start(bf16[8,2,32,768]{3,2,1,0:T(8,128)(2,1)} %collective-permute-done.3), channel_id=1, source_target_pairs={{0,1},{1,0},{2,3},{3,2},{4,5},{5,4},{6,7},{7,6},{8,9},{9,8},{10,11... | collective-permute-start | bytes 2359304 | tf_op jit(solution)/shard_map/ppermute | solution.py:156
  128.5 1.1 collective-permute-start.15
  129.6 1.9 collective-permute-done.12
  131.5 1.5 collective-permute-start.14
  133.0 1.6 collective-permute-done.14
  135.7 10.6 %rest.1 = bf16[512,4096]{1,0:T(8,128)(2,1)} custom-call(s32[2]{0:T(128)S(1)} %pad_add_fusion.place_ref, f32[512,768]{1,0:T(8,128)} %get-tuple-element.34.gate_sum, f32[512,768]{1,0:T(8,128)} %get-tuple-element.35.up_sum, bf16[512,4096]{1,0:T(8,128)(2,1)} %bitcast.14.rows_any, bf16[1,8,32,768]{3,2,1,0:T(8,128)(2,1)} %bitcast.27.refs_0_, ...), custom_call_target="tpu_custom_call" | custom-call | flops 4831838208 | bytes 13631488 | tf_op jit(solution)/shard_map/rest/pallas_call | solution.py:310
  146.4 56.2 %all_to_all.25 = bf16[16,32,4096]{2,1,0:T(8,128)(2,1)S(1)} all-to-all(bf16[16,32,4096]{2,1,0:T(8,128)(2,1)} %bitcast.55), channel_id=1, replica_groups=mesh['ylo'=2,'z'=4,'x'=4,'yhi'=2,'core'=2] {'ylo','x','yhi'}, dimensions={0} | all-to-all | bytes 8388608 | tf_op jit(solution)/shard_map/all_to_all | solution.py:493
  202.5 3.9 %combine.1 = (bf16[64,4096]{1,0:T(8,128)(2,1)}, bf16[128,32,128]{2,1,0:T(8,128)(2,1)S(1)}) custom-call(bf16[128,512]{1,0:T(8,128)(2,1)S(1)} %pad_maximum_fusion.1.weighs_ref, bf16[128,64]{1,0:T(8,128)(2,1)S(1)} %fusion.4.picked_ref, f32[64,4096]{1,0:T(8,128)S(1)} %get-tuple-element.25.middle_ref, bf16[512,4096]{1,0:T(8,128)(2,1)S(1)} %bitcast.46), custom_call_target="tpu_custom_call" | custom-call | tf_op jit(solution)/shard_map/combine/pallas_call | solution.py:364
  206.5 24.3 %all_to_all.26.lines_ref = bf16[128,32,128]{2,1,0:T(8,128)(2,1)S(1)} all-to-all(bf16[128,32,128]{2,1,0:T(8,128)(2,1)S(1)} %get-tuple-element.39), channel_id=1, replica_groups=mesh['ylo'=2,'z'=4,'x'=4,'yhi'=2,'core'=2] {'ylo','z','x','yhi','core'}, dimensions={0} | all-to-all | bytes 2097152 | tf_op jit(solution)/shard_map/all_to_all | solution.py:502
  230.7 2.5 %unpack.1 = bf16[128,4096]{1,0:T(8,128)(2,1)} custom-call(bf16[128,32,128]{2,1,0:T(8,128)(2,1)S(1)} %all_to_all.26.lines_ref), custom_call_target="tpu_custom_call" | custom-call | tf_op jit(solution)/shard_map/unpack/pallas_call | solution.py:396
  (90 shorter events, 8.2 us)
Async XLA Ops:
  0.6 7.8 %copy-start.18 = (s32[64,8]{0,1:T(8,128)S(1)}, s32[64,8]{0,1:T(8,128)}, u32[]{:S(2)}) copy-start(s32[64,8]{0,1:T(8,128)} %param.23) | copy-start | bytes 6148
  0.6 7.8 %copy-start.12 = (bf16[16,768,32]{1,2,0:T(8,128)(2,1)S(1)}, bf16[16,768,32]{1,2,0:T(8,128)(2,1)}, u32[]{:S(2)}) copy-start(bf16[16,768,32]{1,2,0:T(8,128)(2,1)} %param.29) | copy-start | bytes 2359300
  0.7 7.8 %copy-start.13 = (bf16[16,32,768]{2,1,0:T(8,128)(2,1)S(1)}, bf16[16,32,768]{2,1,0:T(8,128)(2,1)}, u32[]{:S(2)}) copy-start(bf16[16,32,768]{2,1,0:T(8,128)(2,1)} %param.28) | copy-start | bytes 2359300
  0.7 20.8 %all-to-all-start = ((bf16[16,32,768]{2,1,0:T(8,128)(2,1)}), bf16[16,32,768]{2,1,0:T(8,128)(2,1)S(1)}, u32[]{:S(2)}, u32[]{:S(2)}) async-start(bf16[16,32,768]{2,1,0:T(8,128)(2,1)} %param.27), calls=%async_computation | async-start | bytes 1572864 | tf_op jit(solution)/shard_map/all_to_all | solution.py:432
  9.8 18.0 %copy-start.19 = (f32[64,8]{0,1:T(8,128)S(1)}, f32[64,8]{0,1:T(8,128)}, u32[]{:S(2)}) copy-start(f32[64,8]{0,1:T(8,128)} %param.24) | copy-start | bytes 6148
  21.4 28.0 %all-to-all-start.1 = ((bf16[16,2,32,768]{3,2,1,0:T(8,128)(2,1)}), bf16[16,2,32,768]{3,2,1,0:T(8,128)(2,1)}, u32[]{:S(2)}, u32[]{:S(2)}) async-start(bf16[16,2,32,768]{3,2,1,0:T(8,128)(2,1)} %pad_maximum_fusion), calls=%async_computation.1 | async-start | bytes 3145728 | tf_op jit(solution)/shard_map/all_to_all | solution.py:432
  26.2 5.8 %copy-start.20 = (s32[64]{0:T(128)S(1)}, s32[64]{0:T(128)}, u32[]{:S(2)}) copy-start(s32[64]{0:T(128)} %param.26) | copy-start | bytes 772
  26.2 6.4 %copy-start.17 = (bf16[64,4096]{1,0:T(8,128)(2,1)S(1)}, bf16[64,4096]{1,0:T(8,128)(2,1)}, u32[]{:S(2)}) copy-start(bf16[64,4096]{1,0:T(8,128)(2,1)} %param.16) | copy-start | bytes 1572868
  27.8 4.8 %copy-start.1 = (bf16[64,4096]{1,0:T(8,128)(2,1)S(1)}, bf16[64,4096]{1,0:T(8,128)(2,1)}, u32[]{:S(2)}) copy-start(bf16[64,4096]{1,0:T(8,128)(2,1)} %hidden_ref.1) | copy-start | bytes 1572868
  28.1 19.5 %collective-permute-start.1 = (bf16[16,32,768]{2,1,0:T(8,128)(2,1)S(1)}, bf16[16,32,768]{2,1,0:T(8,128)(2,1)}, u32[]{:S(2)}, u32[]{:S(2)}) collective-permute-start(bf16[16,32,768]{2,1,0:T(8,128)(2,1)S(1)} %all-to-all-done), channel_id=1, source_target_pairs={{0,48},{16,0},{32,16},{48,32},{1,49},{17,1},{33,17},{49,33},{2,50}... | collective-permute-start | bytes 2359304 | tf_op jit(solution)/shard_map/ppermute | solution.py:149
  31.9 17.5 %collective-permute-start = (bf16[16,32,768]{2,1,0:T(8,128)(2,1)S(1)}, bf16[16,32,768]{2,1,0:T(8,128)(2,1)S(1)}, u32[]{:S(2)}, u32[]{:S(2)}) collective-permute-start(bf16[16,32,768]{2,1,0:T(8,128)(2,1)S(1)} %all-to-all-done), channel_id=1, source_target_pairs={{0,16},{16,32},{32,48},{48,0},{1,17},{17,33},{33,49},{49,1},{2,18}... | collective-permute-start | bytes 2359304 | tf_op jit(solution)/shard_map/ppermute | solution.py:148
  49.4 62.3 %all-to-all-start.2 = ((bf16[16,32,4096]{2,1,0:T(8,128)(2,1)}), bf16[16,32,4096]{2,1,0:T(8,128)(2,1)}, u32[]{:S(2)}, u32[]{:S(2)}) async-start(bf16[16,32,4096]{2,1,0:T(8,128)(2,1)} %bitcast.47), calls=%async_computation.2 | async-start | bytes 8388608 | tf_op jit(solution)/shard_map/all_to_all | solution.py:479
  55.9 32.1 %collective-permute-start.4 = (bf16[16,2,32,768]{3,2,1,0:T(8,128)(2,1)}, bf16[16,2,32,768]{3,2,1,0:T(8,128)(2,1)S(1)}, u32[]{:S(2)}, u32[]{:S(2)}) collective-permute-start(bf16[16,2,32,768]{3,2,1,0:T(8,128)(2,1)} %all-to-all-done.1), channel_id=1, source_target_pairs={{0,48},{16,0},{32,16},{48,32},{1,49},{17,1},{33,17},{49,33},{2,50}... | collective-permute-start | bytes 4718600 | tf_op jit(solution)/shard_map/ppermute | solution.py:149
  57.1 35.9 %collective-permute-start.2 = (bf16[16,2,32,768]{3,2,1,0:T(8,128)(2,1)}, bf16[16,2,32,768]{3,2,1,0:T(8,128)(2,1)S(1)}, u32[]{:S(2)}, u32[]{:S(2)}) collective-permute-start(bf16[16,2,32,768]{3,2,1,0:T(8,128)(2,1)} %all-to-all-done.1), channel_id=1, source_target_pairs={{0,16},{16,32},{32,48},{48,0},{1,17},{17,33},{33,49},{49,1},{2,18}... | collective-permute-start | bytes 4718600 | tf_op jit(solution)/shard_map/ppermute | solution.py:148
  57.5 37.9 %collective-permute-start.6 = (bf16[16,32,768]{2,1,0:T(8,128)(2,1)S(1)}, bf16[16,32,768]{2,1,0:T(8,128)(2,1)S(1)}, u32[]{:S(2)}, u32[]{:S(2)}) collective-permute-start(bf16[16,32,768]{2,1,0:T(8,128)(2,1)S(1)} %all-to-all-done), channel_id=1, source_target_pairs={{0,1},{1,0},{2,3},{3,2},{4,5},{5,4},{6,7},{7,6},{8,9},{9,8},{10,11... | collective-permute-start | bytes 2359304 | tf_op jit(solution)/shard_map/ppermute | solution.py:156
  62.2 43.8 %collective-permute-start.9 = (bf16[16,2,32,768]{3,2,1,0:T(8,128)(2,1)}, bf16[16,2,32,768]{3,2,1,0:T(8,128)(2,1)S(1)}, u32[]{:S(2)}, u32[]{:S(2)}) collective-permute-start(bf16[16,2,32,768]{3,2,1,0:T(8,128)(2,1)} %all-to-all-done.1), channel_id=1, source_target_pairs={{0,1},{1,0},{2,3},{3,2},{4,5},{5,4},{6,7},{7,6},{8,9},{9,8},{10,11... | collective-permute-start | bytes 4718600 | tf_op jit(solution)/shard_map/ppermute | solution.py:156
  88.1 10.6 %copy-start.6 = (bf16[16,2,32,768]{3,2,1,0:T(8,128)(2,1)}, bf16[16,2,32,768]{3,2,1,0:T(8,128)(2,1)S(1)}, u32[]{:S(2)}) copy-start(bf16[16,2,32,768]{3,2,1,0:T(8,128)(2,1)S(1)} %collective-permute-done.4) | copy-start | bytes 4718596
  88.1 20.3 %collective-permute-start.11 = (bf16[16,2,32,768]{3,2,1,0:T(8,128)(2,1)S(1)}, bf16[16,2,32,768]{3,2,1,0:T(8,128)(2,1)S(1)}, u32[]{:S(2)}, u32[]{:S(2)}) collective-permute-start(bf16[16,2,32,768]{3,2,1,0:T(8,128)(2,1)S(1)} %collective-permute-done.4), channel_id=1, source_target_pairs={{0,1},{1,0},{2,3},{3,2},{4,5},{5,4},{6,7},{7,6},{8,9},{9,8},{10,11... | collective-permute-start | bytes 4718600 | tf_op jit(solution)/shard_map/ppermute | solution.py:156
  93.0 5.7 %copy-start.7 = (bf16[16,2,32,768]{3,2,1,0:T(8,128)(2,1)}, bf16[16,2,32,768]{3,2,1,0:T(8,128)(2,1)S(1)}, u32[]{:S(2)}) copy-start(bf16[16,2,32,768]{3,2,1,0:T(8,128)(2,1)S(1)} %collective-permute-done.2) | copy-start | bytes 4718596
  93.0 16.5 %collective-permute-start.10 = (bf16[16,2,32,768]{3,2,1,0:T(8,128)(2,1)S(1)}, bf16[16,2,32,768]{3,2,1,0:T(8,128)(2,1)}, u32[]{:S(2)}, u32[]{:S(2)}) collective-permute-start(bf16[16,2,32,768]{3,2,1,0:T(8,128)(2,1)S(1)} %collective-permute-done.2), channel_id=1, source_target_pairs={{0,1},{1,0},{2,3},{3,2},{4,5},{5,4},{6,7},{7,6},{8,9},{9,8},{10,11... | collective-permute-start | bytes 4718600 | tf_op jit(solution)/shard_map/ppermute | solution.py:156
  95.4 5.4 %collective-permute-start.8 = (bf16[16,32,768]{2,1,0:T(8,128)(2,1)}, bf16[16,32,768]{2,1,0:T(8,128)(2,1)S(1)}, u32[]{:S(2)}, u32[]{:S(2)}) collective-permute-start(bf16[16,32,768]{2,1,0:T(8,128)(2,1)} %collective-permute-done.1), channel_id=1, source_target_pairs={{0,1},{1,0},{2,3},{3,2},{4,5},{5,4},{6,7},{7,6},{8,9},{9,8},{10,11... | collective-permute-start | bytes 2359304 | tf_op jit(solution)/shard_map/ppermute | solution.py:156
  96.3 6.9 %collective-permute-start.7 = (bf16[16,32,768]{2,1,0:T(8,128)(2,1)S(1)}, bf16[16,32,768]{2,1,0:T(8,128)(2,1)S(1)}, u32[]{:S(2)}, u32[]{:S(2)}) collective-permute-start(bf16[16,32,768]{2,1,0:T(8,128)(2,1)S(1)} %collective-permute-done), channel_id=1, source_target_pairs={{0,1},{1,0},{2,3},{3,2},{4,5},{5,4},{6,7},{7,6},{8,9},{9,8},{10,11... | collective-permute-start | bytes 2359304 | tf_op jit(solution)/shard_map/ppermute | solution.py:156
  100.7 7.7 %copy-start.15 = (bf16[16,32,768]{2,1,0:T(8,128)(2,1)}, bf16[16,32,768]{2,1,0:T(8,128)(2,1)S(1)}, u32[]{:S(2)}) copy-start(bf16[16,32,768]{2,1,0:T(8,128)(2,1)S(1)} %collective-permute-done.8) | copy-start | bytes 2359300
  100.7 21.6 %collective-permute-start.5 = (bf16[8,2,32,768]{3,2,1,0:T(8,128)(2,1)}, bf16[8,2,32,768]{3,2,1,0:T(8,128)(2,1)}, u32[]{:S(2)}, u32[]{:S(2)}) collective-permute-start(bf16[8,2,32,768]{3,2,1,0:T(8,128)(2,1)} %slice.17), channel_id=1, source_target_pairs={{0,48},{16,0},{32,16},{48,32},{1,49},{17,1},{33,17},{49,33},{2,50}... | collective-permute-start | bytes 2359304 | tf_op jit(solution)/shard_map/ppermute | solution.py:151
  103.1 5.4 %copy-start.16 = (bf16[16,32,768]{2,1,0:T(8,128)(2,1)}, bf16[16,32,768]{2,1,0:T(8,128)(2,1)S(1)}, u32[]{:S(2)}) copy-start(bf16[16,32,768]{2,1,0:T(8,128)(2,1)S(1)} %collective-permute-done.7) | copy-start | bytes 2359300
  103.1 20.0 %collective-permute-start.3 = (bf16[8,2,32,768]{3,2,1,0:T(8,128)(2,1)}, bf16[8,2,32,768]{3,2,1,0:T(8,128)(2,1)}, u32[]{:S(2)}, u32[]{:S(2)}) collective-permute-start(bf16[8,2,32,768]{3,2,1,0:T(8,128)(2,1)} %slice.16), channel_id=1, source_target_pairs={{0,16},{16,32},{32,48},{48,0},{1,17},{17,33},{33,49},{49,1},{2,18}... | collective-permute-start | bytes 2359304 | tf_op jit(solution)/shard_map/ppermute | solution.py:150
  106.0 22.5 %collective-permute-start.13 = (bf16[8,32,768]{2,1,0:T(8,128)(2,1)}, bf16[8,32,768]{2,1,0:T(8,128)(2,1)S(1)}, u32[]{:S(2)}, u32[]{:S(2)}) collective-permute-start(bf16[8,32,768]{2,1,0:T(8,128)(2,1)} %slice.19), channel_id=1, source_target_pairs={{0,48},{16,0},{32,16},{48,32},{1,49},{17,1},{33,17},{49,33},{2,50}... | collective-permute-start | bytes 1179656 | tf_op jit(solution)/shard_map/ppermute | solution.py:151
  108.4 23.1 %collective-permute-start.12 = (bf16[8,32,768]{2,1,0:T(8,128)(2,1)}, bf16[8,32,768]{2,1,0:T(8,128)(2,1)}, u32[]{:S(2)}, u32[]{:S(2)}) collective-permute-start(bf16[8,32,768]{2,1,0:T(8,128)(2,1)} %slice.18), channel_id=1, source_target_pairs={{0,16},{16,32},{32,48},{48,0},{1,17},{17,33},{33,49},{49,1},{2,18}... | collective-permute-start | bytes 1179656 | tf_op jit(solution)/shard_map/ppermute | solution.py:150
  123.1 11.5 %collective-permute-start.16 = (bf16[8,2,32,768]{3,2,1,0:T(8,128)(2,1)}, bf16[8,2,32,768]{3,2,1,0:T(8,128)(2,1)S(1)}, u32[]{:S(2)}, u32[]{:S(2)}) collective-permute-start(bf16[8,2,32,768]{3,2,1,0:T(8,128)(2,1)} %collective-permute-done.3), channel_id=1, source_target_pairs={{0,1},{1,0},{2,3},{3,2},{4,5},{5,4},{6,7},{7,6},{8,9},{9,8},{10,11... | collective-permute-start | bytes 2359304 | tf_op jit(solution)/shard_map/ppermute | solution.py:156
  128.0 6.6 %collective-permute-start.17 = (bf16[8,2,32,768]{3,2,1,0:T(8,128)(2,1)}, bf16[8,2,32,768]{3,2,1,0:T(8,128)(2,1)S(1)}, u32[]{:S(2)}, u32[]{:S(2)}) collective-permute-start(bf16[8,2,32,768]{3,2,1,0:T(8,128)(2,1)} %collective-permute-done.5), channel_id=1, source_target_pairs={{0,1},{1,0},{2,3},{3,2},{4,5},{5,4},{6,7},{7,6},{8,9},{9,8},{10,11... | collective-permute-start | bytes 2359304 | tf_op jit(solution)/shard_map/ppermute | solution.py:156
  128.5 4.6 %collective-permute-start.15 = (bf16[8,32,768]{2,1,0:T(8,128)(2,1)S(1)}, bf16[8,32,768]{2,1,0:T(8,128)(2,1)S(1)}, u32[]{:S(2)}, u32[]{:S(2)}) collective-permute-start(bf16[8,32,768]{2,1,0:T(8,128)(2,1)S(1)} %collective-permute-done.13), channel_id=1, source_target_pairs={{0,1},{1,0},{2,3},{3,2},{4,5},{5,4},{6,7},{7,6},{8,9},{9,8},{10,11... | collective-permute-start | bytes 1179656 | tf_op jit(solution)/shard_map/ppermute | solution.py:156
  131.5 3.1 %collective-permute-start.14 = (bf16[8,32,768]{2,1,0:T(8,128)(2,1)}, bf16[8,32,768]{2,1,0:T(8,128)(2,1)S(1)}, u32[]{:S(2)}, u32[]{:S(2)}) collective-permute-start(bf16[8,32,768]{2,1,0:T(8,128)(2,1)} %collective-permute-done.12), channel_id=1, source_target_pairs={{0,1},{1,0},{2,3},{3,2},{4,5},{5,4},{6,7},{7,6},{8,9},{9,8},{10,11... | collective-permute-start | bytes 1179656 | tf_op jit(solution)/shard_map/ppermute | solution.py:156
  (11 other events, 29.6 us)

commit v6 on v5

--- a/solution.py
+++ b/solution.py
@@ -432,9 +432,6 @@
     to_chip = lambda part: lax.all_to_all(part, PLANE, split_axis=0, concat_axis=0, tiled=True)
     gate = to_chip(gate_weight)
     pair = jnp.stack([up_weight, jnp.swapaxes(down_weight, 1, 2)], axis=1)
-    pair, queries, gate = lax.optimization_barrier((pair, queries, gate))
-    pair = to_chip(pair)
-    gate_near, gate_far = spread_piece(gate)
 
     expert_range = jnp.arange(experts, dtype=jnp.int32)
     hit_table = expert_ids[:, :, None] == expert_range[None, None, :]
@@ -462,7 +459,11 @@
     picked = finished_rows[None, :] & (slot_of_row[None, :] == slot_span[:, None])
     picked = picked.astype(jnp.bfloat16)
 
-    queries, weighs, picked, place = lax.optimization_barrier((queries, weighs, picked, place))
+    pair, queries, gate, weighs, pick, picked, place = lax.optimization_barrier(
+        (pair, queries, gate, weighs, pick, picked, place)
+    )
+    pair = to_chip(pair)
+    gate_near, gate_far = spread_piece(gate)
     middle, outgoing = attend_call(
         cache_lengths,
         queries,

time: 234 us -> 234 us (level)
    ppermute x10, starting transfers between devices: 20.3 us -> 16.6 us  [with_other_core(): parts = mine + [lax.ppermute(part, 'core', SWAP) for part in mine]]
    all_to_all x2, waiting for transfers between devices: 11.6 us -> 8 us  [shards(): lax.all_to_all(part, PLANE, split_axis=0, concat_axis=0, tiled=True)]
    unnamed x45 -> x47, local copies, waits for them, and re-layouts: 5.26 us -> 6.08 us
where the time goes in v6:
time: 234 us; the launch traced here: 233 us
  blocking collectives  80.4 us (34%)
  waiting for transfers between devices  49.3 us (21%)
  starting transfers between devices  47.4 us (20%)
  Pallas kernels  40.7 us (17%)
  local copies, waits for them, and re-layouts  10.2 us (4%)
  other arithmetic  4.17 us (2%)
    all_to_all x1, blocking collectives, shards(): lax.all_to_all(expert_out.reshape(experts, capacity, model_width), PLANE,...  56.2 us
    ppermute x2, waiting for transfers between devices, spread_piece(): succ = lax.ppermute(piece, 'z', ZDOWN)  28 us
    all_to_all x1, blocking collectives, shards(): lax.all_to_all(parcel, AXES, split_axis=0, concat_axis=0, tiled=True)  24.2 us
    ppermute x10, starting transfers between devices, with_other_core(): parts = mine + [lax.ppermute(part, 'core', SWAP) for part in mine]  16.6 us
    pallas_call x1, Pallas kernels, attend_call(): pl.pallas_call(attend_kernel, grid=(rows // block,), out_shape=(jax.Shape...  12.9 us
    all_to_all x2, starting transfers between devices, shards(): lax.all_to_all(part, PLANE, split_axis=0, concat_axis=0, tiled=True)  12.4 us
    pallas_call x1, Pallas kernels, near_call(): pl.pallas_call(near_kernel, out_shape=(total, total), in_specs=[pl.BlockS...  10.7 us
    pallas_call x1, Pallas kernels, rest_call(): pl.pallas_call(rest_kernel, out_shape=jax.ShapeDtypeStruct((count, depth)...  10.6 us
  transfers between devices with their start and end apart: 21, of which 9 were waited for; matrix products, arithmetic and copies ran while one was open for 4% of the time, Pallas kernels for 10%

profile of v6, /device:TPU:1, one launch (start us, length us, event | category | flops | bytes accessed | tf_op | source)
XLA Modules:
  0.0 233.3 jit_solution(5121480061621331040)
XLA Ops:
  0.7 7.7 %all-to-all-start = ((bf16[16,32,768]{2,1,0:T(8,128)(2,1)}), bf16[16,32,768]{2,1,0:T(8,128)(2,1)S(1)}, u32[]{:S(2)}, u32[]{:S(2)}) async-start(bf16[16,32,768]{2,1,0:T(8,128)(2,1)} %param.27), calls=%async_computation | async-start | bytes 1572864 | tf_op jit(solution)/shard_map/all_to_all | solution.py:432
  8.6 1.2 select_reduce_fusion
  10.9 2.4 %pad_maximum_fusion = bf16[16,2,32,768]{3,2,1,0:T(8,128)(2,1)} fusion(bf16[16,1,32,768]{3,2,1,0:T(8,128)(2,1)S(1)} %bitcast.69, bf16[16,1,32,768]{3,2,1,0:T(8,128)(2,1)} %bitcast.70), kind=kLoop, calls=%fused_computation | loop fusion | flops 786432 | bytes 3145728 | tf_op jit(solution)/shard_map/stack | solution.py:434
  13.5 8.0 %all-to-all-done = bf16[16,32,768]{2,1,0:T(8,128)(2,1)S(1)} async-done(((bf16[16,32,768]{2,1,0:T(8,128)(2,1)}), bf16[16,32,768]{2,1,0:T(8,128)(2,1)S(1)}, u32[]{:S(2)}, u32[]{:S(2)}) %all-to-all-start) | async-done | bytes 786464 | tf_op jit(solution)/shard_map/all_to_all | solution.py:432
  21.5 4.7 %all-to-all-start.1 = ((bf16[16,2,32,768]{3,2,1,0:T(8,128)(2,1)}), bf16[16,2,32,768]{3,2,1,0:T(8,128)(2,1)}, u32[]{:S(2)}, u32[]{:S(2)}) async-start(bf16[16,2,32,768]{3,2,1,0:T(8,128)(2,1)} %pad_maximum_fusion), calls=%async_computation.1 | async-start | bytes 3145728 | tf_op jit(solution)/shard_map/all_to_all | solution.py:432
  26.2 3.8 %collective-permute-start.1 = (bf16[16,32,768]{2,1,0:T(8,128)(2,1)S(1)}, bf16[16,32,768]{2,1,0:T(8,128)(2,1)S(1)}, u32[]{:S(2)}, u32[]{:S(2)}) collective-permute-start(bf16[16,32,768]{2,1,0:T(8,128)(2,1)S(1)} %all-to-all-done), channel_id=1, source_target_pairs={{0,48},{16,0},{32,16},{48,32},{1,49},{17,1},{33,17},{49,33},{2,50}... | collective-permute-start | bytes 2359304 | tf_op jit(solution)/shard_map/ppermute | solution.py:149
  30.1 12.9 %attend.1 = (f32[64,4096]{1,0:T(8,128)S(1)}, bf16[512,4096]{1,0:T(8,128)(2,1)S(1)}) custom-call(s32[64]{0:T(128)S(1)} %copy-done.5, bf16[64,32,128]{2,1,0:T(8,128)(2,1)S(1)} %bitcast.49, bf16[64,256,256]{2,1,0:T(8,128)(2,1)} %k_ref.1, bf16[64,256,256]{2,1,0:T(8,128)(2,1)} %v_ref.1, bf16[64,256]{1,0:T(8,128)(2,1)S(1)} %copy-done.2, ...), custom_call_target="tpu_custom_call" | custom-call | flops 536870912 | bytes 67108864 | tf_op jit(solution)/shard_map/attend/pallas_call | solution.py:106
  43.1 1.9 copy-done
  45.9 1.7 collective-permute-done
  47.6 6.3 %all-to-all-start.2 = ((bf16[16,32,4096]{2,1,0:T(8,128)(2,1)}), bf16[16,32,4096]{2,1,0:T(8,128)(2,1)}, u32[]{:S(2)}, u32[]{:S(2)}) async-start(bf16[16,32,4096]{2,1,0:T(8,128)(2,1)} %bitcast.47), calls=%async_computation.2 | async-start | bytes 8388608 | tf_op jit(solution)/shard_map/all_to_all | solution.py:480
  53.9 3.2 %collective-permute-start.4 = (bf16[16,2,32,768]{3,2,1,0:T(8,128)(2,1)}, bf16[16,2,32,768]{3,2,1,0:T(8,128)(2,1)S(1)}, u32[]{:S(2)}, u32[]{:S(2)}) collective-permute-start(bf16[16,2,32,768]{3,2,1,0:T(8,128)(2,1)} %all-to-all-done.1), channel_id=1, source_target_pairs={{0,48},{16,0},{32,16},{48,32},{1,49},{17,1},{33,17},{49,33},{2,50}... | collective-permute-start | bytes 4718600 | tf_op jit(solution)/shard_map/ppermute | solution.py:149
  57.2 3.1 %collective-permute-start.6 = (bf16[16,32,768]{2,1,0:T(8,128)(2,1)S(1)}, bf16[16,32,768]{2,1,0:T(8,128)(2,1)S(1)}, u32[]{:S(2)}, u32[]{:S(2)}) collective-permute-start(bf16[16,32,768]{2,1,0:T(8,128)(2,1)S(1)} %all-to-all-done), channel_id=1, source_target_pairs={{0,1},{1,0},{2,3},{3,2},{4,5},{5,4},{6,7},{7,6},{8,9},{9,8},{10,11... | collective-permute-start | bytes 2359304 | tf_op jit(solution)/shard_map/ppermute | solution.py:156
  60.3 28.0 %collective-permute-done.4 = bf16[16,2,32,768]{3,2,1,0:T(8,128)(2,1)S(1)} collective-permute-done((bf16[16,2,32,768]{3,2,1,0:T(8,128)(2,1)}, bf16[16,2,32,768]{3,2,1,0:T(8,128)(2,1)S(1)}, u32[]{:S(2)}, u32[]{:S(2)}) %collective-permute-start.4) | collective-permute-done | bytes 1572896 | tf_op jit(solution)/shard_map/ppermute | solution.py:149
  88.3 3.8 %collective-permute-start.11 = (bf16[16,2,32,768]{3,2,1,0:T(8,128)(2,1)S(1)}, bf16[16,2,32,768]{3,2,1,0:T(8,128)(2,1)S(1)}, u32[]{:S(2)}, u32[]{:S(2)}) collective-permute-start(bf16[16,2,32,768]{3,2,1,0:T(8,128)(2,1)S(1)} %collective-permute-done.4), channel_id=1, source_target_pairs={{0,1},{1,0},{2,3},{3,2},{4,5},{5,4},{6,7},{7,6},{8,9},{9,8},{10,11... | collective-permute-start | bytes 4718600 | tf_op jit(solution)/shard_map/ppermute | solution.py:156
  92.1 3.3 %collective-permute-start.10 = (bf16[16,2,32,768]{3,2,1,0:T(8,128)(2,1)S(1)}, bf16[16,2,32,768]{3,2,1,0:T(8,128)(2,1)}, u32[]{:S(2)}, u32[]{:S(2)}) collective-permute-start(bf16[16,2,32,768]{3,2,1,0:T(8,128)(2,1)S(1)} %collective-permute-done.2), channel_id=1, source_target_pairs={{0,1},{1,0},{2,3},{3,2},{4,5},{5,4},{6,7},{7,6},{8,9},{9,8},{10,11... | collective-permute-start | bytes 4718600 | tf_op jit(solution)/shard_map/ppermute | solution.py:156
  98.7 2.0 collective-permute-done.8
  100.8 2.4 %collective-permute-start.5 = (bf16[8,2,32,768]{3,2,1,0:T(8,128)(2,1)}, bf16[8,2,32,768]{3,2,1,0:T(8,128)(2,1)}, u32[]{:S(2)}, u32[]{:S(2)}) collective-permute-start(bf16[8,2,32,768]{3,2,1,0:T(8,128)(2,1)} %slice.17), channel_id=1, source_target_pairs={{0,48},{16,0},{32,16},{48,32},{1,49},{17,1},{33,17},{49,33},{2,50}... | collective-permute-start | bytes 2359304 | tf_op jit(solution)/shard_map/ppermute | solution.py:151
  104.8 2.6 %collective-permute-start.13 = (bf16[8,32,768]{2,1,0:T(8,128)(2,1)}, bf16[8,32,768]{2,1,0:T(8,128)(2,1)S(1)}, u32[]{:S(2)}, u32[]{:S(2)}) collective-permute-start(bf16[8,32,768]{2,1,0:T(8,128)(2,1)} %slice.19), channel_id=1, source_target_pairs={{0,48},{16,0},{32,16},{48,32},{1,49},{17,1},{33,17},{49,33},{2,50}... | collective-permute-start | bytes 1179656 | tf_op jit(solution)/shard_map/ppermute | solution.py:151
  108.6 1.1 all-to-all-done.2
  109.7 10.7 %near.1 = (f32[512,768]{1,0:T(8,128)}, f32[512,768]{1,0:T(8,128)}) custom-call(s32[2]{0:T(128)S(1)} %pad_add_fusion.place_ref, bf16[512,4096]{1,0:T(8,128)(2,1)} %bitcast.14.rows_any, bf16[2,8,32,768]{3,2,1,0:T(8,128)(2,1)S(1)} %bitcast.48, bf16[2,8,32,768]{3,2,1,0:T(8,128)(2,1)S(1)} %bitcast.50, bf16[2,8,32,768]{3,2,1,0:T(8,128)(2,1)} %bitcast.64, ...), custom_call_target="tpu_custom_call" | custom-call | flops 4831838208 | bytes 13631488 | tf_op jit(solution)/shard_map/near/pallas_call | solution.py:224
  120.4 2.7 %collective-permute-done.3 = bf16[8,2,32,768]{3,2,1,0:T(8,128)(2,1)} collective-permute-done((bf16[8,2,32,768]{3,2,1,0:T(8,128)(2,1)}, bf16[8,2,32,768]{3,2,1,0:T(8,128)(2,1)}, u32[]{:S(2)}, u32[]{:S(2)}) %collective-permute-start.3) | collective-permute-done | bytes 786464 | tf_op jit(solution)/shard_map/ppermute | solution.py:150
  123.1 2.9 %collective-permute-start.16 = (bf16[8,2,32,768]{3,2,1,0:T(8,128)(2,1)}, bf16[8,2,32,768]{3,2,1,0:T(8,128)(2,1)S(1)}, u32[]{:S(2)}, u32[]{:S(2)}) collective-permute-start(bf16[8,2,32,768]{3,2,1,0:T(8,128)(2,1)} %collective-permute-done.3), channel_id=1, source_target_pairs={{0,1},{1,0},{2,3},{3,2},{4,5},{5,4},{6,7},{7,6},{8,9},{9,8},{10,11... | collective-permute-start | bytes 2359304 | tf_op jit(solution)/shard_map/ppermute | solution.py:156
  126.3 2.2 collective-permute-done.13
  128.5 1.1 collective-permute-start.15
  129.6 1.9 collective-permute-done.12
  131.5 1.5 collective-permute-start.14
  133.1 1.6 collective-permute-done.14
  135.8 10.6 %rest.1 = bf16[512,4096]{1,0:T(8,128)(2,1)} custom-call(s32[2]{0:T(128)S(1)} %pad_add_fusion.place_ref, f32[512,768]{1,0:T(8,128)} %get-tuple-element.34.gate_sum, f32[512,768]{1,0:T(8,128)} %get-tuple-element.35.up_sum, bf16[512,4096]{1,0:T(8,128)(2,1)} %bitcast.14.rows_any, bf16[1,8,32,768]{3,2,1,0:T(8,128)(2,1)} %bitcast.27.refs_0_, ...), custom_call_target="tpu_custom_call" | custom-call | flops 4831838208 | bytes 13631488 | tf_op jit(solution)/shard_map/rest/pallas_call | solution.py:310
  146.4 56.2 %all_to_all.25 = bf16[16,32,4096]{2,1,0:T(8,128)(2,1)S(1)} all-to-all(bf16[16,32,4096]{2,1,0:T(8,128)(2,1)} %bitcast.55), channel_id=1, replica_groups=mesh['ylo'=2,'z'=4,'x'=4,'yhi'=2,'core'=2] {'ylo','x','yhi'}, dimensions={0} | all-to-all | bytes 8388608 | tf_op jit(solution)/shard_map/all_to_all | solution.py:494
  202.6 4.0 %combine.1 = (bf16[64,4096]{1,0:T(8,128)(2,1)}, bf16[128,32,128]{2,1,0:T(8,128)(2,1)S(1)}) custom-call(bf16[128,512]{1,0:T(8,128)(2,1)S(1)} %pad_maximum_fusion.1.weighs_ref, bf16[128,64]{1,0:T(8,128)(2,1)S(1)} %fusion.4.picked_ref, f32[64,4096]{1,0:T(8,128)S(1)} %get-tuple-element.25.middle_ref, bf16[512,4096]{1,0:T(8,128)(2,1)S(1)} %bitcast.46), custom_call_target="tpu_custom_call" | custom-call | tf_op jit(solution)/shard_map/combine/pallas_call | solution.py:364
  206.6 24.2 %all_to_all.26.lines_ref = bf16[128,32,128]{2,1,0:T(8,128)(2,1)S(1)} all-to-all(bf16[128,32,128]{2,1,0:T(8,128)(2,1)S(1)} %get-tuple-element.39), channel_id=1, replica_groups=mesh['ylo'=2,'z'=4,'x'=4,'yhi'=2,'core'=2] {'ylo','z','x','yhi','core'}, dimensions={0} | all-to-all | bytes 2097152 | tf_op jit(solution)/shard_map/all_to_all | solution.py:503
  230.8 2.5 %unpack.1 = bf16[128,4096]{1,0:T(8,128)(2,1)} custom-call(bf16[128,32,128]{2,1,0:T(8,128)(2,1)S(1)} %all_to_all.26.lines_ref), custom_call_target="tpu_custom_call" | custom-call | tf_op jit(solution)/shard_map/unpack/pallas_call | solution.py:396
  (92 shorter events, 9.8 us)
Async XLA Ops:
  0.6 7.8 %copy-start.19 = (s32[64,8]{0,1:T(8,128)S(1)}, s32[64,8]{0,1:T(8,128)}, u32[]{:S(2)}) copy-start(s32[64,8]{0,1:T(8,128)} %param.23) | copy-start | bytes 6148
  0.7 7.9 %copy-start.20 = (f32[64,8]{0,1:T(8,128)S(1)}, f32[64,8]{0,1:T(8,128)}, u32[]{:S(2)}) copy-start(f32[64,8]{0,1:T(8,128)} %param.24) | copy-start | bytes 6148
  0.7 9.7 %copy-start.21 = (s32[64]{0:T(128)S(1)}, s32[64]{0:T(128)}, u32[]{:S(2)}) copy-start(s32[64]{0:T(128)} %param.26) | copy-start | bytes 772
  0.7 20.8 %all-to-all-start = ((bf16[16,32,768]{2,1,0:T(8,128)(2,1)}), bf16[16,32,768]{2,1,0:T(8,128)(2,1)S(1)}, u32[]{:S(2)}, u32[]{:S(2)}) async-start(bf16[16,32,768]{2,1,0:T(8,128)(2,1)} %param.27), calls=%async_computation | async-start | bytes 1572864 | tf_op jit(solution)/shard_map/all_to_all | solution.py:432
  13.4 16.6 %copy-start.18 = (bf16[64,4096]{1,0:T(8,128)(2,1)S(1)}, bf16[64,4096]{1,0:T(8,128)(2,1)}, u32[]{:S(2)}) copy-start(bf16[64,4096]{1,0:T(8,128)(2,1)} %param.16) | copy-start | bytes 1572868
  13.4 16.7 %copy-start.1 = (bf16[64,4096]{1,0:T(8,128)(2,1)S(1)}, bf16[64,4096]{1,0:T(8,128)(2,1)}, u32[]{:S(2)}) copy-start(bf16[64,4096]{1,0:T(8,128)(2,1)} %hidden_ref.1) | copy-start | bytes 1572868
  13.4 16.7 %copy-start.2 = (bf16[64,256]{1,0:T(8,128)(2,1)S(1)}, bf16[64,256]{1,0:T(8,128)(2,1)}, u32[]{:S(2)}) copy-start(bf16[64,256]{1,0:T(8,128)(2,1)} %nk_ref.1) | copy-start | bytes 98308
  13.4 16.7 %copy-start.3 = (bf16[64,256]{1,0:T(8,128)(2,1)S(1)}, bf16[64,256]{1,0:T(8,128)(2,1)}, u32[]{:S(2)}) copy-start(bf16[64,256]{1,0:T(8,128)(2,1)} %nv_ref.1) | copy-start | bytes 98308
  13.4 16.7 %copy-start.4 = (f32[4096]{0:T(1024)S(1)}, f32[4096]{0:T(1024)}, u32[]{:S(2)}) copy-start(f32[4096]{0:T(1024)} %param.22) | copy-start | bytes 49156
  13.4 16.7 %copy-start.5 = (s32[64]{0:T(128)S(1)}, s32[64]{0:T(128)}, u32[]{:S(2)}) copy-start(s32[64]{0:T(128)} %lengths_ref.1) | copy-start | bytes 772
  21.5 26.1 %all-to-all-start.1 = ((bf16[16,2,32,768]{3,2,1,0:T(8,128)(2,1)}), bf16[16,2,32,768]{3,2,1,0:T(8,128)(2,1)}, u32[]{:S(2)}, u32[]{:S(2)}) async-start(bf16[16,2,32,768]{3,2,1,0:T(8,128)(2,1)} %pad_maximum_fusion), calls=%async_computation.1 | async-start | bytes 3145728 | tf_op jit(solution)/shard_map/all_to_all | solution.py:432
  26.2 18.8 %collective-permute-start.1 = (bf16[16,32,768]{2,1,0:T(8,128)(2,1)S(1)}, bf16[16,32,768]{2,1,0:T(8,128)(2,1)S(1)}, u32[]{:S(2)}, u32[]{:S(2)}) collective-permute-start(bf16[16,32,768]{2,1,0:T(8,128)(2,1)S(1)} %all-to-all-done), channel_id=1, source_target_pairs={{0,48},{16,0},{32,16},{48,32},{1,49},{17,1},{33,17},{49,33},{2,50}... | collective-permute-start | bytes 2359304 | tf_op jit(solution)/shard_map/ppermute | solution.py:149
  30.0 17.6 %collective-permute-start = (bf16[16,32,768]{2,1,0:T(8,128)(2,1)S(1)}, bf16[16,32,768]{2,1,0:T(8,128)(2,1)S(1)}, u32[]{:S(2)}, u32[]{:S(2)}) collective-permute-start(bf16[16,32,768]{2,1,0:T(8,128)(2,1)S(1)} %all-to-all-done), channel_id=1, source_target_pairs={{0,16},{16,32},{32,48},{48,0},{1,17},{17,33},{33,49},{49,1},{2,18}... | collective-permute-start | bytes 2359304 | tf_op jit(solution)/shard_map/ppermute | solution.py:148
  47.6 62.1 %all-to-all-start.2 = ((bf16[16,32,4096]{2,1,0:T(8,128)(2,1)}), bf16[16,32,4096]{2,1,0:T(8,128)(2,1)}, u32[]{:S(2)}, u32[]{:S(2)}) async-start(bf16[16,32,4096]{2,1,0:T(8,128)(2,1)} %bitcast.47), calls=%async_computation.2 | async-start | bytes 8388608 | tf_op jit(solution)/shard_map/all_to_all | solution.py:480
  53.9 49.2 %copy-start.11 = (bf16[16,32,768]{2,1,0:T(8,128)(2,1)S(1)}, bf16[16,32,768]{2,1,0:T(8,128)(2,1)}, u32[]{:S(2)}) copy-start(bf16[16,32,768]{2,1,0:T(8,128)(2,1)} %copy-done.10) | copy-start | bytes 2359300
  53.9 34.4 %collective-permute-start.4 = (bf16[16,2,32,768]{3,2,1,0:T(8,128)(2,1)}, bf16[16,2,32,768]{3,2,1,0:T(8,128)(2,1)S(1)}, u32[]{:S(2)}, u32[]{:S(2)}) collective-permute-start(bf16[16,2,32,768]{3,2,1,0:T(8,128)(2,1)} %all-to-all-done.1), channel_id=1, source_target_pairs={{0,48},{16,0},{32,16},{48,32},{1,49},{17,1},{33,17},{49,33},{2,50}... | collective-permute-start | bytes 4718600 | tf_op jit(solution)/shard_map/ppermute | solution.py:149
  57.2 34.9 %collective-permute-start.2 = (bf16[16,2,32,768]{3,2,1,0:T(8,128)(2,1)}, bf16[16,2,32,768]{3,2,1,0:T(8,128)(2,1)S(1)}, u32[]{:S(2)}, u32[]{:S(2)}) collective-permute-start(bf16[16,2,32,768]{3,2,1,0:T(8,128)(2,1)} %all-to-all-done.1), channel_id=1, source_target_pairs={{0,16},{16,32},{32,48},{48,0},{1,17},{17,33},{33,49},{49,1},{2,18}... | collective-permute-start | bytes 4718600 | tf_op jit(solution)/shard_map/ppermute | solution.py:148
  57.2 38.2 %collective-permute-start.6 = (bf16[16,32,768]{2,1,0:T(8,128)(2,1)S(1)}, bf16[16,32,768]{2,1,0:T(8,128)(2,1)S(1)}, u32[]{:S(2)}, u32[]{:S(2)}) collective-permute-start(bf16[16,32,768]{2,1,0:T(8,128)(2,1)S(1)} %all-to-all-done), channel_id=1, source_target_pairs={{0,1},{1,0},{2,3},{3,2},{4,5},{5,4},{6,7},{7,6},{8,9},{9,8},{10,11... | collective-permute-start | bytes 2359304 | tf_op jit(solution)/shard_map/ppermute | solution.py:156
  60.3 44.5 %collective-permute-start.9 = (bf16[16,2,32,768]{3,2,1,0:T(8,128)(2,1)}, bf16[16,2,32,768]{3,2,1,0:T(8,128)(2,1)S(1)}, u32[]{:S(2)}, u32[]{:S(2)}) collective-permute-start(bf16[16,2,32,768]{3,2,1,0:T(8,128)(2,1)} %all-to-all-done.1), channel_id=1, source_target_pairs={{0,1},{1,0},{2,3},{3,2},{4,5},{5,4},{6,7},{7,6},{8,9},{9,8},{10,11... | collective-permute-start | bytes 4718600 | tf_op jit(solution)/shard_map/ppermute | solution.py:156
  88.3 10.4 %copy-start.6 = (bf16[16,2,32,768]{3,2,1,0:T(8,128)(2,1)}, bf16[16,2,32,768]{3,2,1,0:T(8,128)(2,1)S(1)}, u32[]{:S(2)}) copy-start(bf16[16,2,32,768]{3,2,1,0:T(8,128)(2,1)S(1)} %collective-permute-done.4) | copy-start | bytes 4718596
  88.3 19.1 %collective-permute-start.11 = (bf16[16,2,32,768]{3,2,1,0:T(8,128)(2,1)S(1)}, bf16[16,2,32,768]{3,2,1,0:T(8,128)(2,1)S(1)}, u32[]{:S(2)}, u32[]{:S(2)}) collective-permute-start(bf16[16,2,32,768]{3,2,1,0:T(8,128)(2,1)S(1)} %collective-permute-done.4), channel_id=1, source_target_pairs={{0,1},{1,0},{2,3},{3,2},{4,5},{5,4},{6,7},{7,6},{8,9},{9,8},{10,11... | collective-permute-start | bytes 4718600 | tf_op jit(solution)/shard_map/ppermute | solution.py:156
  92.1 16.5 %collective-permute-start.10 = (bf16[16,2,32,768]{3,2,1,0:T(8,128)(2,1)S(1)}, bf16[16,2,32,768]{3,2,1,0:T(8,128)(2,1)}, u32[]{:S(2)}, u32[]{:S(2)}) collective-permute-start(bf16[16,2,32,768]{3,2,1,0:T(8,128)(2,1)S(1)} %collective-permute-done.2), channel_id=1, source_target_pairs={{0,1},{1,0},{2,3},{3,2},{4,5},{5,4},{6,7},{7,6},{8,9},{9,8},{10,11... | collective-permute-start | bytes 4718600 | tf_op jit(solution)/shard_map/ppermute | solution.py:156
  95.4 5.4 %collective-permute-start.8 = (bf16[16,32,768]{2,1,0:T(8,128)(2,1)}, bf16[16,32,768]{2,1,0:T(8,128)(2,1)S(1)}, u32[]{:S(2)}, u32[]{:S(2)}) collective-permute-start(bf16[16,32,768]{2,1,0:T(8,128)(2,1)} %copy-done.10), channel_id=1, source_target_pairs={{0,1},{1,0},{2,3},{3,2},{4,5},{5,4},{6,7},{7,6},{8,9},{9,8},{10,11... | collective-permute-start | bytes 2359304 | tf_op jit(solution)/shard_map/ppermute | solution.py:156
  96.3 6.8 %collective-permute-start.7 = (bf16[16,32,768]{2,1,0:T(8,128)(2,1)S(1)}, bf16[16,32,768]{2,1,0:T(8,128)(2,1)S(1)}, u32[]{:S(2)}, u32[]{:S(2)}) collective-permute-start(bf16[16,32,768]{2,1,0:T(8,128)(2,1)S(1)} %collective-permute-done), channel_id=1, source_target_pairs={{0,1},{1,0},{2,3},{3,2},{4,5},{5,4},{6,7},{7,6},{8,9},{9,8},{10,11... | collective-permute-start | bytes 2359304 | tf_op jit(solution)/shard_map/ppermute | solution.py:156
  100.8 19.6 %collective-permute-start.5 = (bf16[8,2,32,768]{3,2,1,0:T(8,128)(2,1)}, bf16[8,2,32,768]{3,2,1,0:T(8,128)(2,1)}, u32[]{:S(2)}, u32[]{:S(2)}) collective-permute-start(bf16[8,2,32,768]{3,2,1,0:T(8,128)(2,1)} %slice.17), channel_id=1, source_target_pairs={{0,48},{16,0},{32,16},{48,32},{1,49},{17,1},{33,17},{49,33},{2,50}... | collective-permute-start | bytes 2359304 | tf_op jit(solution)/shard_map/ppermute | solution.py:151
  103.1 20.0 %collective-permute-start.3 = (bf16[8,2,32,768]{3,2,1,0:T(8,128)(2,1)}, bf16[8,2,32,768]{3,2,1,0:T(8,128)(2,1)}, u32[]{:S(2)}, u32[]{:S(2)}) collective-permute-start(bf16[8,2,32,768]{3,2,1,0:T(8,128)(2,1)} %slice.16), channel_id=1, source_target_pairs={{0,16},{16,32},{32,48},{48,0},{1,17},{17,33},{33,49},{49,1},{2,18}... | collective-permute-start | bytes 2359304 | tf_op jit(solution)/shard_map/ppermute | solution.py:150
  104.8 23.7 %collective-permute-start.13 = (bf16[8,32,768]{2,1,0:T(8,128)(2,1)}, bf16[8,32,768]{2,1,0:T(8,128)(2,1)S(1)}, u32[]{:S(2)}, u32[]{:S(2)}) collective-permute-start(bf16[8,32,768]{2,1,0:T(8,128)(2,1)} %slice.19), channel_id=1, source_target_pairs={{0,48},{16,0},{32,16},{48,32},{1,49},{17,1},{33,17},{49,33},{2,50}... | collective-permute-start | bytes 1179656 | tf_op jit(solution)/shard_map/ppermute | solution.py:151
  107.4 24.1 %collective-permute-start.12 = (bf16[8,32,768]{2,1,0:T(8,128)(2,1)}, bf16[8,32,768]{2,1,0:T(8,128)(2,1)}, u32[]{:S(2)}, u32[]{:S(2)}) collective-permute-start(bf16[8,32,768]{2,1,0:T(8,128)(2,1)} %slice.18), channel_id=1, source_target_pairs={{0,16},{16,32},{32,48},{48,0},{1,17},{17,33},{33,49},{49,1},{2,18}... | collective-permute-start | bytes 1179656 | tf_op jit(solution)/shard_map/ppermute | solution.py:150
  123.1 11.5 %collective-permute-start.16 = (bf16[8,2,32,768]{3,2,1,0:T(8,128)(2,1)}, bf16[8,2,32,768]{3,2,1,0:T(8,128)(2,1)S(1)}, u32[]{:S(2)}, u32[]{:S(2)}) collective-permute-start(bf16[8,2,32,768]{3,2,1,0:T(8,128)(2,1)} %collective-permute-done.3), channel_id=1, source_target_pairs={{0,1},{1,0},{2,3},{3,2},{4,5},{5,4},{6,7},{7,6},{8,9},{9,8},{10,11... | collective-permute-start | bytes 2359304 | tf_op jit(solution)/shard_map/ppermute | solution.py:156
  126.0 8.6 %collective-permute-start.17 = (bf16[8,2,32,768]{3,2,1,0:T(8,128)(2,1)}, bf16[8,2,32,768]{3,2,1,0:T(8,128)(2,1)S(1)}, u32[]{:S(2)}, u32[]{:S(2)}) collective-permute-start(bf16[8,2,32,768]{3,2,1,0:T(8,128)(2,1)} %collective-permute-done.5), channel_id=1, source_target_pairs={{0,1},{1,0},{2,3},{3,2},{4,5},{5,4},{6,7},{7,6},{8,9},{9,8},{10,11... | collective-permute-start | bytes 2359304 | tf_op jit(solution)/shard_map/ppermute | solution.py:156
  128.5 4.6 %collective-permute-start.15 = (bf16[8,32,768]{2,1,0:T(8,128)(2,1)S(1)}, bf16[8,32,768]{2,1,0:T(8,128)(2,1)S(1)}, u32[]{:S(2)}, u32[]{:S(2)}) collective-permute-start(bf16[8,32,768]{2,1,0:T(8,128)(2,1)S(1)} %collective-permute-done.13), channel_id=1, source_target_pairs={{0,1},{1,0},{2,3},{3,2},{4,5},{5,4},{6,7},{7,6},{8,9},{9,8},{10,11... | collective-permute-start | bytes 1179656 | tf_op jit(solution)/shard_map/ppermute | solution.py:156
  131.5 3.1 %collective-permute-start.14 = (bf16[8,32,768]{2,1,0:T(8,128)(2,1)}, bf16[8,32,768]{2,1,0:T(8,128)(2,1)S(1)}, u32[]{:S(2)}, u32[]{:S(2)}) collective-permute-start(bf16[8,32,768]{2,1,0:T(8,128)(2,1)} %collective-permute-done.12), channel_id=1, source_target_pairs={{0,1},{1,0},{2,3},{3,2},{4,5},{5,4},{6,7},{7,6},{8,9},{9,8},{10,11... | collective-permute-start | bytes 1179656 | tf_op jit(solution)/shard_map/ppermute | solution.py:156
  (12 other events, 37.5 us)

commit v7 on v5

--- a/solution.py
+++ b/solution.py
@@ -358,7 +358,7 @@
     rows, width = middle.shape
     slots = back.shape[0]
     learners = picked.shape[0]
-    step = 1024
+    step = 2048
     whole = lambda shape: pl.BlockSpec(shape, lambda i: (0,) * len(shape))
     column = lambda count: pl.BlockSpec((count, step), lambda i: (0, i))
     return pl.pallas_call(

time: 234 us -> 233 us (level)
  no operation moved by 1% of the time
where the time goes in v7:
time: 233 us
  blocking collectives  80.4 us (35%)
  starting transfers between devices  49.4 us (21%)
  waiting for transfers between devices  47.9 us (21%)
  Pallas kernels  40.1 us (17%)
  local copies, waits for them, and re-layouts  10.7 us (5%)
  other arithmetic  3.06 us (1%)
    all_to_all x1, blocking collectives, shards(): lax.all_to_all(expert_out.reshape(experts, capacity, model_width), PLANE,...  56.2 us
    ppermute x2, waiting for transfers between devices, spread_piece(): succ = lax.ppermute(piece, 'z', ZDOWN)  25.9 us
    all_to_all x1, blocking collectives, shards(): lax.all_to_all(parcel, AXES, split_axis=0, concat_axis=0, tiled=True)  24.3 us
    ppermute x10, starting transfers between devices, with_other_core(): parts = mine + [lax.ppermute(part, 'core', SWAP) for part in mine]  20.3 us
    pallas_call x1, Pallas kernels, attend_call(): pl.pallas_call(attend_kernel, grid=(rows // block,), out_shape=(jax.Shape...  12.9 us
    all_to_all x2, starting transfers between devices, shards(): lax.all_to_all(part, PLANE, split_axis=0, concat_axis=0, tiled=True)  12.4 us
    all_to_all x2, waiting for transfers between devices, shards(): lax.all_to_all(part, PLANE, split_axis=0, concat_axis=0, tiled=True)  11.6 us
    pallas_call x1, Pallas kernels, near_call(): pl.pallas_call(near_kernel, out_shape=(total, total), in_specs=[pl.BlockS...  10.7 us
  transfers between devices with their start and end apart: 21, of which 9 were waited for; matrix products, arithmetic and copies ran while one was open for 4% of the time, Pallas kernels for 10%

profile of v7, /device:TPU:1, one launch (start us, length us, event | category | flops | bytes accessed | tf_op | source)
XLA Modules:
  0.0 232.7 jit_solution(17602746744266563715)
XLA Ops:
  0.7 7.7 %all-to-all-start = ((bf16[16,32,768]{2,1,0:T(8,128)(2,1)}), bf16[16,32,768]{2,1,0:T(8,128)(2,1)S(1)}, u32[]{:S(2)}, u32[]{:S(2)}) async-start(bf16[16,32,768]{2,1,0:T(8,128)(2,1)} %param.27), calls=%async_computation | async-start | bytes 1572864 | tf_op jit(solution)/shard_map/all_to_all | solution.py:432
  8.5 1.3 pad_maximum_fusion
  9.8 11.6 %all-to-all-done = bf16[16,32,768]{2,1,0:T(8,128)(2,1)S(1)} async-done(((bf16[16,32,768]{2,1,0:T(8,128)(2,1)}), bf16[16,32,768]{2,1,0:T(8,128)(2,1)S(1)}, u32[]{:S(2)}, u32[]{:S(2)}) %all-to-all-start) | async-done | bytes 786464 | tf_op jit(solution)/shard_map/all_to_all | solution.py:432
  21.4 4.7 %all-to-all-start.1 = ((bf16[16,2,32,768]{3,2,1,0:T(8,128)(2,1)}), bf16[16,2,32,768]{3,2,1,0:T(8,128)(2,1)}, u32[]{:S(2)}, u32[]{:S(2)}) async-start(bf16[16,2,32,768]{3,2,1,0:T(8,128)(2,1)} %pad_maximum_fusion), calls=%async_computation.1 | async-start | bytes 3145728 | tf_op jit(solution)/shard_map/all_to_all | solution.py:432
  26.2 1.2 select_reduce_fusion
  28.1 3.8 %collective-permute-start.1 = (bf16[16,32,768]{2,1,0:T(8,128)(2,1)S(1)}, bf16[16,32,768]{2,1,0:T(8,128)(2,1)}, u32[]{:S(2)}, u32[]{:S(2)}) collective-permute-start(bf16[16,32,768]{2,1,0:T(8,128)(2,1)S(1)} %all-to-all-done), channel_id=1, source_target_pairs={{0,48},{16,0},{32,16},{48,32},{1,49},{17,1},{33,17},{49,33},{2,50}... | collective-permute-start | bytes 2359304 | tf_op jit(solution)/shard_map/ppermute | solution.py:149
  32.7 12.9 %attend.1 = (f32[64,4096]{1,0:T(8,128)S(1)}, bf16[512,4096]{1,0:T(8,128)(2,1)S(1)}) custom-call(s32[64]{0:T(128)S(1)} %copy-done.5, bf16[64,32,128]{2,1,0:T(8,128)(2,1)S(1)} %bitcast.49, bf16[64,256,256]{2,1,0:T(8,128)(2,1)} %k_ref.1, bf16[64,256,256]{2,1,0:T(8,128)(2,1)} %v_ref.1, bf16[64,256]{1,0:T(8,128)(2,1)S(1)} %copy-done.2, ...), custom_call_target="tpu_custom_call" | custom-call | flops 536870912 | bytes 67108864 | tf_op jit(solution)/shard_map/attend/pallas_call | solution.py:106
  45.6 2.0 copy-done
  47.6 1.8 collective-permute-done
  49.4 6.5 %all-to-all-start.2 = ((bf16[16,32,4096]{2,1,0:T(8,128)(2,1)}), bf16[16,32,4096]{2,1,0:T(8,128)(2,1)}, u32[]{:S(2)}, u32[]{:S(2)}) async-start(bf16[16,32,4096]{2,1,0:T(8,128)(2,1)} %bitcast.47), calls=%async_computation.2 | async-start | bytes 8388608 | tf_op jit(solution)/shard_map/all_to_all | solution.py:479
  55.9 1.2 collective-permute-start.4
  57.5 4.7 %collective-permute-start.6 = (bf16[16,32,768]{2,1,0:T(8,128)(2,1)S(1)}, bf16[16,32,768]{2,1,0:T(8,128)(2,1)S(1)}, u32[]{:S(2)}, u32[]{:S(2)}) collective-permute-start(bf16[16,32,768]{2,1,0:T(8,128)(2,1)S(1)} %all-to-all-done), channel_id=1, source_target_pairs={{0,1},{1,0},{2,3},{3,2},{4,5},{5,4},{6,7},{7,6},{8,9},{9,8},{10,11... | collective-permute-start | bytes 2359304 | tf_op jit(solution)/shard_map/ppermute | solution.py:156
  62.2 25.9 %collective-permute-done.4 = bf16[16,2,32,768]{3,2,1,0:T(8,128)(2,1)S(1)} collective-permute-done((bf16[16,2,32,768]{3,2,1,0:T(8,128)(2,1)}, bf16[16,2,32,768]{3,2,1,0:T(8,128)(2,1)S(1)}, u32[]{:S(2)}, u32[]{:S(2)}) %collective-permute-start.4) | collective-permute-done | bytes 1572896 | tf_op jit(solution)/shard_map/ppermute | solution.py:149
  88.1 4.9 %collective-permute-start.11 = (bf16[16,2,32,768]{3,2,1,0:T(8,128)(2,1)S(1)}, bf16[16,2,32,768]{3,2,1,0:T(8,128)(2,1)S(1)}, u32[]{:S(2)}, u32[]{:S(2)}) collective-permute-start(bf16[16,2,32,768]{3,2,1,0:T(8,128)(2,1)S(1)} %collective-permute-done.4), channel_id=1, source_target_pairs={{0,1},{1,0},{2,3},{3,2},{4,5},{5,4},{6,7},{7,6},{8,9},{9,8},{10,11... | collective-permute-start | bytes 4718600 | tf_op jit(solution)/shard_map/ppermute | solution.py:156
  93.0 2.3 %collective-permute-start.10 = (bf16[16,2,32,768]{3,2,1,0:T(8,128)(2,1)S(1)}, bf16[16,2,32,768]{3,2,1,0:T(8,128)(2,1)}, u32[]{:S(2)}, u32[]{:S(2)}) collective-permute-start(bf16[16,2,32,768]{3,2,1,0:T(8,128)(2,1)S(1)} %collective-permute-done.2), channel_id=1, source_target_pairs={{0,1},{1,0},{2,3},{3,2},{4,5},{5,4},{6,7},{7,6},{8,9},{9,8},{10,11... | collective-permute-start | bytes 4718600 | tf_op jit(solution)/shard_map/ppermute | solution.py:156
  98.7 2.0 collective-permute-done.8
  100.7 2.4 %collective-permute-start.5 = (bf16[8,2,32,768]{3,2,1,0:T(8,128)(2,1)}, bf16[8,2,32,768]{3,2,1,0:T(8,128)(2,1)}, u32[]{:S(2)}, u32[]{:S(2)}) collective-permute-start(bf16[8,2,32,768]{3,2,1,0:T(8,128)(2,1)} %slice.17), channel_id=1, source_target_pairs={{0,48},{16,0},{32,16},{48,32},{1,49},{17,1},{33,17},{49,33},{2,50}... | collective-permute-start | bytes 2359304 | tf_op jit(solution)/shard_map/ppermute | solution.py:151
  103.1 2.1 slice.19
  106.0 2.4 %collective-permute-start.13 = (bf16[8,32,768]{2,1,0:T(8,128)(2,1)}, bf16[8,32,768]{2,1,0:T(8,128)(2,1)S(1)}, u32[]{:S(2)}, u32[]{:S(2)}) collective-permute-start(bf16[8,32,768]{2,1,0:T(8,128)(2,1)} %slice.19), channel_id=1, source_target_pairs={{0,48},{16,0},{32,16},{48,32},{1,49},{17,1},{33,17},{49,33},{2,50}... | collective-permute-start | bytes 1179656 | tf_op jit(solution)/shard_map/ppermute | solution.py:151
  108.5 1.1 copy-done.9
  109.5 2.2 all-to-all-done.2
  111.7 10.7 %near.1 = (f32[512,768]{1,0:T(8,128)}, f32[512,768]{1,0:T(8,128)}) custom-call(s32[2]{0:T(128)S(1)} %pad_add_fusion.place_ref, bf16[512,4096]{1,0:T(8,128)(2,1)} %bitcast.14.rows_any, bf16[2,8,32,768]{3,2,1,0:T(8,128)(2,1)S(1)} %bitcast.48, bf16[2,8,32,768]{3,2,1,0:T(8,128)(2,1)S(1)} %bitcast.50, bf16[2,8,32,768]{3,2,1,0:T(8,128)(2,1)} %bitcast.17.refs_2_, ...), custom_call_target="tpu_custom_call" | custom-call | flops 4831838208 | bytes 13631488 | tf_op jit(solution)/shard_map/near/pallas_call | solution.py:224
  123.1 4.9 %collective-permute-start.16 = (bf16[8,2,32,768]{3,2,1,0:T(8,128)(2,1)}, bf16[8,2,32,768]{3,2,1,0:T(8,128)(2,1)S(1)}, u32[]{:S(2)}, u32[]{:S(2)}) collective-permute-start(bf16[8,2,32,768]{3,2,1,0:T(8,128)(2,1)} %collective-permute-done.3), channel_id=1, source_target_pairs={{0,1},{1,0},{2,3},{3,2},{4,5},{5,4},{6,7},{7,6},{8,9},{9,8},{10,11... | collective-permute-start | bytes 2359304 | tf_op jit(solution)/shard_map/ppermute | solution.py:156
  128.5 1.1 collective-permute-start.15
  129.6 1.9 collective-permute-done.12
  131.5 1.5 collective-permute-start.14
  133.0 1.6 collective-permute-done.14
  135.7 10.6 %rest.1 = bf16[512,4096]{1,0:T(8,128)(2,1)} custom-call(s32[2]{0:T(128)S(1)} %pad_add_fusion.place_ref, f32[512,768]{1,0:T(8,128)} %get-tuple-element.34.gate_sum, f32[512,768]{1,0:T(8,128)} %get-tuple-element.35.up_sum, bf16[512,4096]{1,0:T(8,128)(2,1)} %bitcast.14.rows_any, bf16[1,8,32,768]{3,2,1,0:T(8,128)(2,1)} %bitcast.27.refs_0_, ...), custom_call_target="tpu_custom_call" | custom-call | flops 4831838208 | bytes 13631488 | tf_op jit(solution)/shard_map/rest/pallas_call | solution.py:310
  146.4 56.2 %all_to_all.25 = bf16[16,32,4096]{2,1,0:T(8,128)(2,1)S(1)} all-to-all(bf16[16,32,4096]{2,1,0:T(8,128)(2,1)} %bitcast.55), channel_id=1, replica_groups=mesh['ylo'=2,'z'=4,'x'=4,'yhi'=2,'core'=2] {'ylo','x','yhi'}, dimensions={0} | all-to-all | bytes 8388608 | tf_op jit(solution)/shard_map/all_to_all | solution.py:493
  202.5 3.4 %combine.1 = (bf16[64,4096]{1,0:T(8,128)(2,1)}, bf16[128,32,128]{2,1,0:T(8,128)(2,1)S(1)}) custom-call(bf16[128,512]{1,0:T(8,128)(2,1)S(1)} %pad_maximum_fusion.1.weighs_ref, bf16[128,64]{1,0:T(8,128)(2,1)S(1)} %fusion.4.picked_ref, f32[64,4096]{1,0:T(8,128)S(1)} %get-tuple-element.25.middle_ref, bf16[512,4096]{1,0:T(8,128)(2,1)S(1)} %bitcast.46), custom_call_target="tpu_custom_call" | custom-call | tf_op jit(solution)/shard_map/combine/pallas_call | solution.py:364
  206.0 24.3 %all_to_all.26.lines_ref = bf16[128,32,128]{2,1,0:T(8,128)(2,1)S(1)} all-to-all(bf16[128,32,128]{2,1,0:T(8,128)(2,1)S(1)} %get-tuple-element.39), channel_id=1, replica_groups=mesh['ylo'=2,'z'=4,'x'=4,'yhi'=2,'core'=2] {'ylo','z','x','yhi','core'}, dimensions={0} | all-to-all | bytes 2097152 | tf_op jit(solution)/shard_map/all_to_all | solution.py:502
  230.3 2.5 %unpack.1 = bf16[128,4096]{1,0:T(8,128)(2,1)} custom-call(bf16[128,32,128]{2,1,0:T(8,128)(2,1)S(1)} %all_to_all.26.lines_ref), custom_call_target="tpu_custom_call" | custom-call | tf_op jit(solution)/shard_map/unpack/pallas_call | solution.py:396
  (90 shorter events, 8.2 us)
Async XLA Ops:
  0.6 7.8 %copy-start.18 = (s32[64,8]{0,1:T(8,128)S(1)}, s32[64,8]{0,1:T(8,128)}, u32[]{:S(2)}) copy-start(s32[64,8]{0,1:T(8,128)} %param.23) | copy-start | bytes 6148
  0.6 7.8 %copy-start.12 = (bf16[16,768,32]{1,2,0:T(8,128)(2,1)S(1)}, bf16[16,768,32]{1,2,0:T(8,128)(2,1)}, u32[]{:S(2)}) copy-start(bf16[16,768,32]{1,2,0:T(8,128)(2,1)} %param.29) | copy-start | bytes 2359300
  0.7 7.8 %copy-start.13 = (bf16[16,32,768]{2,1,0:T(8,128)(2,1)S(1)}, bf16[16,32,768]{2,1,0:T(8,128)(2,1)}, u32[]{:S(2)}) copy-start(bf16[16,32,768]{2,1,0:T(8,128)(2,1)} %param.28) | copy-start | bytes 2359300
  0.7 20.8 %all-to-all-start = ((bf16[16,32,768]{2,1,0:T(8,128)(2,1)}), bf16[16,32,768]{2,1,0:T(8,128)(2,1)S(1)}, u32[]{:S(2)}, u32[]{:S(2)}) async-start(bf16[16,32,768]{2,1,0:T(8,128)(2,1)} %param.27), calls=%async_computation | async-start | bytes 1572864 | tf_op jit(solution)/shard_map/all_to_all | solution.py:432
  9.8 18.0 %copy-start.19 = (f32[64,8]{0,1:T(8,128)S(1)}, f32[64,8]{0,1:T(8,128)}, u32[]{:S(2)}) copy-start(f32[64,8]{0,1:T(8,128)} %param.24) | copy-start | bytes 6148
  21.4 28.0 %all-to-all-start.1 = ((bf16[16,2,32,768]{3,2,1,0:T(8,128)(2,1)}), bf16[16,2,32,768]{3,2,1,0:T(8,128)(2,1)}, u32[]{:S(2)}, u32[]{:S(2)}) async-start(bf16[16,2,32,768]{3,2,1,0:T(8,128)(2,1)} %pad_maximum_fusion), calls=%async_computation.1 | async-start | bytes 3145728 | tf_op jit(solution)/shard_map/all_to_all | solution.py:432
  26.2 5.8 %copy-start.20 = (s32[64]{0:T(128)S(1)}, s32[64]{0:T(128)}, u32[]{:S(2)}) copy-start(s32[64]{0:T(128)} %param.26) | copy-start | bytes 772
  26.2 6.4 %copy-start.17 = (bf16[64,4096]{1,0:T(8,128)(2,1)S(1)}, bf16[64,4096]{1,0:T(8,128)(2,1)}, u32[]{:S(2)}) copy-start(bf16[64,4096]{1,0:T(8,128)(2,1)} %param.16) | copy-start | bytes 1572868
  27.8 4.8 %copy-start.1 = (bf16[64,4096]{1,0:T(8,128)(2,1)S(1)}, bf16[64,4096]{1,0:T(8,128)(2,1)}, u32[]{:S(2)}) copy-start(bf16[64,4096]{1,0:T(8,128)(2,1)} %hidden_ref.1) | copy-start | bytes 1572868
  28.1 19.5 %collective-permute-start.1 = (bf16[16,32,768]{2,1,0:T(8,128)(2,1)S(1)}, bf16[16,32,768]{2,1,0:T(8,128)(2,1)}, u32[]{:S(2)}, u32[]{:S(2)}) collective-permute-start(bf16[16,32,768]{2,1,0:T(8,128)(2,1)S(1)} %all-to-all-done), channel_id=1, source_target_pairs={{0,48},{16,0},{32,16},{48,32},{1,49},{17,1},{33,17},{49,33},{2,50}... | collective-permute-start | bytes 2359304 | tf_op jit(solution)/shard_map/ppermute | solution.py:149
  31.9 17.5 %collective-permute-start = (bf16[16,32,768]{2,1,0:T(8,128)(2,1)S(1)}, bf16[16,32,768]{2,1,0:T(8,128)(2,1)S(1)}, u32[]{:S(2)}, u32[]{:S(2)}) collective-permute-start(bf16[16,32,768]{2,1,0:T(8,128)(2,1)S(1)} %all-to-all-done), channel_id=1, source_target_pairs={{0,16},{16,32},{32,48},{48,0},{1,17},{17,33},{33,49},{49,1},{2,18}... | collective-permute-start | bytes 2359304 | tf_op jit(solution)/shard_map/ppermute | solution.py:148
  49.4 62.3 %all-to-all-start.2 = ((bf16[16,32,4096]{2,1,0:T(8,128)(2,1)}), bf16[16,32,4096]{2,1,0:T(8,128)(2,1)}, u32[]{:S(2)}, u32[]{:S(2)}) async-start(bf16[16,32,4096]{2,1,0:T(8,128)(2,1)} %bitcast.47), calls=%async_computation.2 | async-start | bytes 8388608 | tf_op jit(solution)/shard_map/all_to_all | solution.py:479
  55.9 32.1 %collective-permute-start.4 = (bf16[16,2,32,768]{3,2,1,0:T(8,128)(2,1)}, bf16[16,2,32,768]{3,2,1,0:T(8,128)(2,1)S(1)}, u32[]{:S(2)}, u32[]{:S(2)}) collective-permute-start(bf16[16,2,32,768]{3,2,1,0:T(8,128)(2,1)} %all-to-all-done.1), channel_id=1, source_target_pairs={{0,48},{16,0},{32,16},{48,32},{1,49},{17,1},{33,17},{49,33},{2,50}... | collective-permute-start | bytes 4718600 | tf_op jit(solution)/shard_map/ppermute | solution.py:149
  57.1 35.9 %collective-permute-start.2 = (bf16[16,2,32,768]{3,2,1,0:T(8,128)(2,1)}, bf16[16,2,32,768]{3,2,1,0:T(8,128)(2,1)S(1)}, u32[]{:S(2)}, u32[]{:S(2)}) collective-permute-start(bf16[16,2,32,768]{3,2,1,0:T(8,128)(2,1)} %all-to-all-done.1), channel_id=1, source_target_pairs={{0,16},{16,32},{32,48},{48,0},{1,17},{17,33},{33,49},{49,1},{2,18}... | collective-permute-start | bytes 4718600 | tf_op jit(solution)/shard_map/ppermute | solution.py:148
  57.5 37.9 %collective-permute-start.6 = (bf16[16,32,768]{2,1,0:T(8,128)(2,1)S(1)}, bf16[16,32,768]{2,1,0:T(8,128)(2,1)S(1)}, u32[]{:S(2)}, u32[]{:S(2)}) collective-permute-start(bf16[16,32,768]{2,1,0:T(8,128)(2,1)S(1)} %all-to-all-done), channel_id=1, source_target_pairs={{0,1},{1,0},{2,3},{3,2},{4,5},{5,4},{6,7},{7,6},{8,9},{9,8},{10,11... | collective-permute-start | bytes 2359304 | tf_op jit(solution)/shard_map/ppermute | solution.py:156
  62.2 43.8 %collective-permute-start.9 = (bf16[16,2,32,768]{3,2,1,0:T(8,128)(2,1)}, bf16[16,2,32,768]{3,2,1,0:T(8,128)(2,1)S(1)}, u32[]{:S(2)}, u32[]{:S(2)}) collective-permute-start(bf16[16,2,32,768]{3,2,1,0:T(8,128)(2,1)} %all-to-all-done.1), channel_id=1, source_target_pairs={{0,1},{1,0},{2,3},{3,2},{4,5},{5,4},{6,7},{7,6},{8,9},{9,8},{10,11... | collective-permute-start | bytes 4718600 | tf_op jit(solution)/shard_map/ppermute | solution.py:156
  88.1 10.6 %copy-start.6 = (bf16[16,2,32,768]{3,2,1,0:T(8,128)(2,1)}, bf16[16,2,32,768]{3,2,1,0:T(8,128)(2,1)S(1)}, u32[]{:S(2)}) copy-start(bf16[16,2,32,768]{3,2,1,0:T(8,128)(2,1)S(1)} %collective-permute-done.4) | copy-start | bytes 4718596
  88.1 20.3 %collective-permute-start.11 = (bf16[16,2,32,768]{3,2,1,0:T(8,128)(2,1)S(1)}, bf16[16,2,32,768]{3,2,1,0:T(8,128)(2,1)S(1)}, u32[]{:S(2)}, u32[]{:S(2)}) collective-permute-start(bf16[16,2,32,768]{3,2,1,0:T(8,128)(2,1)S(1)} %collective-permute-done.4), channel_id=1, source_target_pairs={{0,1},{1,0},{2,3},{3,2},{4,5},{5,4},{6,7},{7,6},{8,9},{9,8},{10,11... | collective-permute-start | bytes 4718600 | tf_op jit(solution)/shard_map/ppermute | solution.py:156
  93.0 5.7 %copy-start.7 = (bf16[16,2,32,768]{3,2,1,0:T(8,128)(2,1)}, bf16[16,2,32,768]{3,2,1,0:T(8,128)(2,1)S(1)}, u32[]{:S(2)}) copy-start(bf16[16,2,32,768]{3,2,1,0:T(8,128)(2,1)S(1)} %collective-permute-done.2) | copy-start | bytes 4718596
  93.0 16.5 %collective-permute-start.10 = (bf16[16,2,32,768]{3,2,1,0:T(8,128)(2,1)S(1)}, bf16[16,2,32,768]{3,2,1,0:T(8,128)(2,1)}, u32[]{:S(2)}, u32[]{:S(2)}) collective-permute-start(bf16[16,2,32,768]{3,2,1,0:T(8,128)(2,1)S(1)} %collective-permute-done.2), channel_id=1, source_target_pairs={{0,1},{1,0},{2,3},{3,2},{4,5},{5,4},{6,7},{7,6},{8,9},{9,8},{10,11... | collective-permute-start | bytes 4718600 | tf_op jit(solution)/shard_map/ppermute | solution.py:156
  95.4 5.4 %collective-permute-start.8 = (bf16[16,32,768]{2,1,0:T(8,128)(2,1)}, bf16[16,32,768]{2,1,0:T(8,128)(2,1)S(1)}, u32[]{:S(2)}, u32[]{:S(2)}) collective-permute-start(bf16[16,32,768]{2,1,0:T(8,128)(2,1)} %collective-permute-done.1), channel_id=1, source_target_pairs={{0,1},{1,0},{2,3},{3,2},{4,5},{5,4},{6,7},{7,6},{8,9},{9,8},{10,11... | collective-permute-start | bytes 2359304 | tf_op jit(solution)/shard_map/ppermute | solution.py:156
  96.3 6.9 %collective-permute-start.7 = (bf16[16,32,768]{2,1,0:T(8,128)(2,1)S(1)}, bf16[16,32,768]{2,1,0:T(8,128)(2,1)S(1)}, u32[]{:S(2)}, u32[]{:S(2)}) collective-permute-start(bf16[16,32,768]{2,1,0:T(8,128)(2,1)S(1)} %collective-permute-done), channel_id=1, source_target_pairs={{0,1},{1,0},{2,3},{3,2},{4,5},{5,4},{6,7},{7,6},{8,9},{9,8},{10,11... | collective-permute-start | bytes 2359304 | tf_op jit(solution)/shard_map/ppermute | solution.py:156
  100.7 7.7 %copy-start.15 = (bf16[16,32,768]{2,1,0:T(8,128)(2,1)}, bf16[16,32,768]{2,1,0:T(8,128)(2,1)S(1)}, u32[]{:S(2)}) copy-start(bf16[16,32,768]{2,1,0:T(8,128)(2,1)S(1)} %collective-permute-done.8) | copy-start | bytes 2359300
  100.7 21.6 %collective-permute-start.5 = (bf16[8,2,32,768]{3,2,1,0:T(8,128)(2,1)}, bf16[8,2,32,768]{3,2,1,0:T(8,128)(2,1)}, u32[]{:S(2)}, u32[]{:S(2)}) collective-permute-start(bf16[8,2,32,768]{3,2,1,0:T(8,128)(2,1)} %slice.17), channel_id=1, source_target_pairs={{0,48},{16,0},{32,16},{48,32},{1,49},{17,1},{33,17},{49,33},{2,50}... | collective-permute-start | bytes 2359304 | tf_op jit(solution)/shard_map/ppermute | solution.py:151
  103.1 5.4 %copy-start.16 = (bf16[16,32,768]{2,1,0:T(8,128)(2,1)}, bf16[16,32,768]{2,1,0:T(8,128)(2,1)S(1)}, u32[]{:S(2)}) copy-start(bf16[16,32,768]{2,1,0:T(8,128)(2,1)S(1)} %collective-permute-done.7) | copy-start | bytes 2359300
  103.1 20.0 %collective-permute-start.3 = (bf16[8,2,32,768]{3,2,1,0:T(8,128)(2,1)}, bf16[8,2,32,768]{3,2,1,0:T(8,128)(2,1)}, u32[]{:S(2)}, u32[]{:S(2)}) collective-permute-start(bf16[8,2,32,768]{3,2,1,0:T(8,128)(2,1)} %slice.16), channel_id=1, source_target_pairs={{0,16},{16,32},{32,48},{48,0},{1,17},{17,33},{33,49},{49,1},{2,18}... | collective-permute-start | bytes 2359304 | tf_op jit(solution)/shard_map/ppermute | solution.py:150
  106.0 22.5 %collective-permute-start.13 = (bf16[8,32,768]{2,1,0:T(8,128)(2,1)}, bf16[8,32,768]{2,1,0:T(8,128)(2,1)S(1)}, u32[]{:S(2)}, u32[]{:S(2)}) collective-permute-start(bf16[8,32,768]{2,1,0:T(8,128)(2,1)} %slice.19), channel_id=1, source_target_pairs={{0,48},{16,0},{32,16},{48,32},{1,49},{17,1},{33,17},{49,33},{2,50}... | collective-permute-start | bytes 1179656 | tf_op jit(solution)/shard_map/ppermute | solution.py:151
  108.4 23.1 %collective-permute-start.12 = (bf16[8,32,768]{2,1,0:T(8,128)(2,1)}, bf16[8,32,768]{2,1,0:T(8,128)(2,1)}, u32[]{:S(2)}, u32[]{:S(2)}) collective-permute-start(bf16[8,32,768]{2,1,0:T(8,128)(2,1)} %slice.18), channel_id=1, source_target_pairs={{0,16},{16,32},{32,48},{48,0},{1,17},{17,33},{33,49},{49,1},{2,18}... | collective-permute-start | bytes 1179656 | tf_op jit(solution)/shard_map/ppermute | solution.py:150
  123.1 11.5 %collective-permute-start.16 = (bf16[8,2,32,768]{3,2,1,0:T(8,128)(2,1)}, bf16[8,2,32,768]{3,2,1,0:T(8,128)(2,1)S(1)}, u32[]{:S(2)}, u32[]{:S(2)}) collective-permute-start(bf16[8,2,32,768]{3,2,1,0:T(8,128)(2,1)} %collective-permute-done.3), channel_id=1, source_target_pairs={{0,1},{1,0},{2,3},{3,2},{4,5},{5,4},{6,7},{7,6},{8,9},{9,8},{10,11... | collective-permute-start | bytes 2359304 | tf_op jit(solution)/shard_map/ppermute | solution.py:156
  128.0 6.6 %collective-permute-start.17 = (bf16[8,2,32,768]{3,2,1,0:T(8,128)(2,1)}, bf16[8,2,32,768]{3,2,1,0:T(8,128)(2,1)S(1)}, u32[]{:S(2)}, u32[]{:S(2)}) collective-permute-start(bf16[8,2,32,768]{3,2,1,0:T(8,128)(2,1)} %collective-permute-done.5), channel_id=1, source_target_pairs={{0,1},{1,0},{2,3},{3,2},{4,5},{5,4},{6,7},{7,6},{8,9},{9,8},{10,11... | collective-permute-start | bytes 2359304 | tf_op jit(solution)/shard_map/ppermute | solution.py:156
  128.5 4.6 %collective-permute-start.15 = (bf16[8,32,768]{2,1,0:T(8,128)(2,1)S(1)}, bf16[8,32,768]{2,1,0:T(8,128)(2,1)S(1)}, u32[]{:S(2)}, u32[]{:S(2)}) collective-permute-start(bf16[8,32,768]{2,1,0:T(8,128)(2,1)S(1)} %collective-permute-done.13), channel_id=1, source_target_pairs={{0,1},{1,0},{2,3},{3,2},{4,5},{5,4},{6,7},{7,6},{8,9},{9,8},{10,11... | collective-permute-start | bytes 1179656 | tf_op jit(solution)/shard_map/ppermute | solution.py:156
  131.5 3.1 %collective-permute-start.14 = (bf16[8,32,768]{2,1,0:T(8,128)(2,1)}, bf16[8,32,768]{2,1,0:T(8,128)(2,1)S(1)}, u32[]{:S(2)}, u32[]{:S(2)}) collective-permute-start(bf16[8,32,768]{2,1,0:T(8,128)(2,1)} %collective-permute-done.12), channel_id=1, source_target_pairs={{0,1},{1,0},{2,3},{3,2},{4,5},{5,4},{6,7},{7,6},{8,9},{9,8},{10,11... | collective-permute-start | bytes 1179656 | tf_op jit(solution)/shard_map/ppermute | solution.py:156
  (11 other events, 29.6 us)

commit v8 on v6

--- a/solution.py
+++ b/solution.py
@@ -358,7 +358,7 @@
     rows, width = middle.shape
     slots = back.shape[0]
     learners = picked.shape[0]
-    step = 1024
+    step = 2048
     whole = lambda shape: pl.BlockSpec(shape, lambda i: (0,) * len(shape))
     column = lambda count: pl.BlockSpec((count, step), lambda i: (0, i))
     return pl.pallas_call(

time: 234 us -> 233 us (level)
  no operation moved by 1% of the time
where the time goes in v8:
time: 233 us
  blocking collectives  80.4 us (35%)
  waiting for transfers between devices  49.3 us (21%)
  starting transfers between devices  47.4 us (20%)
  Pallas kernels  40.2 us (17%)
  local copies, waits for them, and re-layouts  10.2 us (4%)
  other arithmetic  4.17 us (2%)
    all_to_all x1, blocking collectives, shards(): lax.all_to_all(expert_out.reshape(experts, capacity, model_width), PLANE,...  56.2 us
    ppermute x2, waiting for transfers between devices, spread_piece(): succ = lax.ppermute(piece, 'z', ZDOWN)  28 us
    all_to_all x1, blocking collectives, shards(): lax.all_to_all(parcel, AXES, split_axis=0, concat_axis=0, tiled=True)  24.2 us
    ppermute x10, starting transfers between devices, with_other_core(): parts = mine + [lax.ppermute(part, 'core', SWAP) for part in mine]  16.6 us
    pallas_call x1, Pallas kernels, attend_call(): pl.pallas_call(attend_kernel, grid=(rows // block,), out_shape=(jax.Shape...  12.9 us
    all_to_all x2, starting transfers between devices, shards(): lax.all_to_all(part, PLANE, split_axis=0, concat_axis=0, tiled=True)  12.4 us
    pallas_call x1, Pallas kernels, near_call(): pl.pallas_call(near_kernel, out_shape=(total, total), in_specs=[pl.BlockS...  10.7 us
    pallas_call x1, Pallas kernels, rest_call(): pl.pallas_call(rest_kernel, out_shape=jax.ShapeDtypeStruct((count, depth)...  10.6 us
  transfers between devices with their start and end apart: 21, of which 9 were waited for; matrix products, arithmetic and copies ran while one was open for 4% of the time, Pallas kernels for 10%

profile of v8, /device:TPU:1, one launch (start us, length us, event | category | flops | bytes accessed | tf_op | source)
XLA Modules:
  0.0 232.8 jit_solution(11142145602732918128)
XLA Ops:
  0.7 7.7 %all-to-all-start = ((bf16[16,32,768]{2,1,0:T(8,128)(2,1)}), bf16[16,32,768]{2,1,0:T(8,128)(2,1)S(1)}, u32[]{:S(2)}, u32[]{:S(2)}) async-start(bf16[16,32,768]{2,1,0:T(8,128)(2,1)} %param.27), calls=%async_computation | async-start | bytes 1572864 | tf_op jit(solution)/shard_map/all_to_all | solution.py:432
  8.6 1.2 select_reduce_fusion
  10.9 2.4 %pad_maximum_fusion = bf16[16,2,32,768]{3,2,1,0:T(8,128)(2,1)} fusion(bf16[16,1,32,768]{3,2,1,0:T(8,128)(2,1)S(1)} %bitcast.69, bf16[16,1,32,768]{3,2,1,0:T(8,128)(2,1)} %bitcast.70), kind=kLoop, calls=%fused_computation | loop fusion | flops 786432 | bytes 3145728 | tf_op jit(solution)/shard_map/stack | solution.py:434
  13.5 8.0 %all-to-all-done = bf16[16,32,768]{2,1,0:T(8,128)(2,1)S(1)} async-done(((bf16[16,32,768]{2,1,0:T(8,128)(2,1)}), bf16[16,32,768]{2,1,0:T(8,128)(2,1)S(1)}, u32[]{:S(2)}, u32[]{:S(2)}) %all-to-all-start) | async-done | bytes 786464 | tf_op jit(solution)/shard_map/all_to_all | solution.py:432
  21.5 4.7 %all-to-all-start.1 = ((bf16[16,2,32,768]{3,2,1,0:T(8,128)(2,1)}), bf16[16,2,32,768]{3,2,1,0:T(8,128)(2,1)}, u32[]{:S(2)}, u32[]{:S(2)}) async-start(bf16[16,2,32,768]{3,2,1,0:T(8,128)(2,1)} %pad_maximum_fusion), calls=%async_computation.1 | async-start | bytes 3145728 | tf_op jit(solution)/shard_map/all_to_all | solution.py:432
  26.2 3.8 %collective-permute-start.1 = (bf16[16,32,768]{2,1,0:T(8,128)(2,1)S(1)}, bf16[16,32,768]{2,1,0:T(8,128)(2,1)S(1)}, u32[]{:S(2)}, u32[]{:S(2)}) collective-permute-start(bf16[16,32,768]{2,1,0:T(8,128)(2,1)S(1)} %all-to-all-done), channel_id=1, source_target_pairs={{0,48},{16,0},{32,16},{48,32},{1,49},{17,1},{33,17},{49,33},{2,50}... | collective-permute-start | bytes 2359304 | tf_op jit(solution)/shard_map/ppermute | solution.py:149
  30.1 12.9 %attend.1 = (f32[64,4096]{1,0:T(8,128)S(1)}, bf16[512,4096]{1,0:T(8,128)(2,1)S(1)}) custom-call(s32[64]{0:T(128)S(1)} %copy-done.5, bf16[64,32,128]{2,1,0:T(8,128)(2,1)S(1)} %bitcast.49, bf16[64,256,256]{2,1,0:T(8,128)(2,1)} %k_ref.1, bf16[64,256,256]{2,1,0:T(8,128)(2,1)} %v_ref.1, bf16[64,256]{1,0:T(8,128)(2,1)S(1)} %copy-done.2, ...), custom_call_target="tpu_custom_call" | custom-call | flops 536870912 | bytes 67108864 | tf_op jit(solution)/shard_map/attend/pallas_call | solution.py:106
  43.1 1.9 copy-done
  45.9 1.7 collective-permute-done
  47.6 6.3 %all-to-all-start.2 = ((bf16[16,32,4096]{2,1,0:T(8,128)(2,1)}), bf16[16,32,4096]{2,1,0:T(8,128)(2,1)}, u32[]{:S(2)}, u32[]{:S(2)}) async-start(bf16[16,32,4096]{2,1,0:T(8,128)(2,1)} %bitcast.47), calls=%async_computation.2 | async-start | bytes 8388608 | tf_op jit(solution)/shard_map/all_to_all | solution.py:480
  53.9 3.2 %collective-permute-start.4 = (bf16[16,2,32,768]{3,2,1,0:T(8,128)(2,1)}, bf16[16,2,32,768]{3,2,1,0:T(8,128)(2,1)S(1)}, u32[]{:S(2)}, u32[]{:S(2)}) collective-permute-start(bf16[16,2,32,768]{3,2,1,0:T(8,128)(2,1)} %all-to-all-done.1), channel_id=1, source_target_pairs={{0,48},{16,0},{32,16},{48,32},{1,49},{17,1},{33,17},{49,33},{2,50}... | collective-permute-start | bytes 4718600 | tf_op jit(solution)/shard_map/ppermute | solution.py:149
  57.2 3.1 %collective-permute-start.6 = (bf16[16,32,768]{2,1,0:T(8,128)(2,1)S(1)}, bf16[16,32,768]{2,1,0:T(8,128)(2,1)S(1)}, u32[]{:S(2)}, u32[]{:S(2)}) collective-permute-start(bf16[16,32,768]{2,1,0:T(8,128)(2,1)S(1)} %all-to-all-done), channel_id=1, source_target_pairs={{0,1},{1,0},{2,3},{3,2},{4,5},{5,4},{6,7},{7,6},{8,9},{9,8},{10,11... | collective-permute-start | bytes 2359304 | tf_op jit(solution)/shard_map/ppermute | solution.py:156
  60.3 28.0 %collective-permute-done.4 = bf16[16,2,32,768]{3,2,1,0:T(8,128)(2,1)S(1)} collective-permute-done((bf16[16,2,32,768]{3,2,1,0:T(8,128)(2,1)}, bf16[16,2,32,768]{3,2,1,0:T(8,128)(2,1)S(1)}, u32[]{:S(2)}, u32[]{:S(2)}) %collective-permute-start.4) | collective-permute-done | bytes 1572896 | tf_op jit(solution)/shard_map/ppermute | solution.py:149
  88.3 3.8 %collective-permute-start.11 = (bf16[16,2,32,768]{3,2,1,0:T(8,128)(2,1)S(1)}, bf16[16,2,32,768]{3,2,1,0:T(8,128)(2,1)S(1)}, u32[]{:S(2)}, u32[]{:S(2)}) collective-permute-start(bf16[16,2,32,768]{3,2,1,0:T(8,128)(2,1)S(1)} %collective-permute-done.4), channel_id=1, source_target_pairs={{0,1},{1,0},{2,3},{3,2},{4,5},{5,4},{6,7},{7,6},{8,9},{9,8},{10,11... | collective-permute-start | bytes 4718600 | tf_op jit(solution)/shard_map/ppermute | solution.py:156
  92.1 3.3 %collective-permute-start.10 = (bf16[16,2,32,768]{3,2,1,0:T(8,128)(2,1)S(1)}, bf16[16,2,32,768]{3,2,1,0:T(8,128)(2,1)}, u32[]{:S(2)}, u32[]{:S(2)}) collective-permute-start(bf16[16,2,32,768]{3,2,1,0:T(8,128)(2,1)S(1)} %collective-permute-done.2), channel_id=1, source_target_pairs={{0,1},{1,0},{2,3},{3,2},{4,5},{5,4},{6,7},{7,6},{8,9},{9,8},{10,11... | collective-permute-start | bytes 4718600 | tf_op jit(solution)/shard_map/ppermute | solution.py:156
  98.7 2.0 collective-permute-done.8
  100.8 2.4 %collective-permute-start.5 = (bf16[8,2,32,768]{3,2,1,0:T(8,128)(2,1)}, bf16[8,2,32,768]{3,2,1,0:T(8,128)(2,1)}, u32[]{:S(2)}, u32[]{:S(2)}) collective-permute-start(bf16[8,2,32,768]{3,2,1,0:T(8,128)(2,1)} %slice.17), channel_id=1, source_target_pairs={{0,48},{16,0},{32,16},{48,32},{1,49},{17,1},{33,17},{49,33},{2,50}... | collective-permute-start | bytes 2359304 | tf_op jit(solution)/shard_map/ppermute | solution.py:151
  104.8 2.6 %collective-permute-start.13 = (bf16[8,32,768]{2,1,0:T(8,128)(2,1)}, bf16[8,32,768]{2,1,0:T(8,128)(2,1)S(1)}, u32[]{:S(2)}, u32[]{:S(2)}) collective-permute-start(bf16[8,32,768]{2,1,0:T(8,128)(2,1)} %slice.19), channel_id=1, source_target_pairs={{0,48},{16,0},{32,16},{48,32},{1,49},{17,1},{33,17},{49,33},{2,50}... | collective-permute-start | bytes 1179656 | tf_op jit(solution)/shard_map/ppermute | solution.py:151
  108.6 1.1 all-to-all-done.2
  109.7 10.7 %near.1 = (f32[512,768]{1,0:T(8,128)}, f32[512,768]{1,0:T(8,128)}) custom-call(s32[2]{0:T(128)S(1)} %pad_add_fusion.place_ref, bf16[512,4096]{1,0:T(8,128)(2,1)} %bitcast.14.rows_any, bf16[2,8,32,768]{3,2,1,0:T(8,128)(2,1)S(1)} %bitcast.48, bf16[2,8,32,768]{3,2,1,0:T(8,128)(2,1)S(1)} %bitcast.50, bf16[2,8,32,768]{3,2,1,0:T(8,128)(2,1)} %bitcast.64, ...), custom_call_target="tpu_custom_call" | custom-call | flops 4831838208 | bytes 13631488 | tf_op jit(solution)/shard_map/near/pallas_call | solution.py:224
  120.4 2.7 %collective-permute-done.3 = bf16[8,2,32,768]{3,2,1,0:T(8,128)(2,1)} collective-permute-done((bf16[8,2,32,768]{3,2,1,0:T(8,128)(2,1)}, bf16[8,2,32,768]{3,2,1,0:T(8,128)(2,1)}, u32[]{:S(2)}, u32[]{:S(2)}) %collective-permute-start.3) | collective-permute-done | bytes 786464 | tf_op jit(solution)/shard_map/ppermute | solution.py:150
  123.1 2.9 %collective-permute-start.16 = (bf16[8,2,32,768]{3,2,1,0:T(8,128)(2,1)}, bf16[8,2,32,768]{3,2,1,0:T(8,128)(2,1)S(1)}, u32[]{:S(2)}, u32[]{:S(2)}) collective-permute-start(bf16[8,2,32,768]{3,2,1,0:T(8,128)(2,1)} %collective-permute-done.3), channel_id=1, source_target_pairs={{0,1},{1,0},{2,3},{3,2},{4,5},{5,4},{6,7},{7,6},{8,9},{9,8},{10,11... | collective-permute-start | bytes 2359304 | tf_op jit(solution)/shard_map/ppermute | solution.py:156
  126.3 2.2 collective-permute-done.13
  128.5 1.1 collective-permute-start.15
  129.6 1.9 collective-permute-done.12
  131.5 1.5 collective-permute-start.14
  133.1 1.6 collective-permute-done.14
  135.8 10.6 %rest.1 = bf16[512,4096]{1,0:T(8,128)(2,1)} custom-call(s32[2]{0:T(128)S(1)} %pad_add_fusion.place_ref, f32[512,768]{1,0:T(8,128)} %get-tuple-element.34.gate_sum, f32[512,768]{1,0:T(8,128)} %get-tuple-element.35.up_sum, bf16[512,4096]{1,0:T(8,128)(2,1)} %bitcast.14.rows_any, bf16[1,8,32,768]{3,2,1,0:T(8,128)(2,1)} %bitcast.27.refs_0_, ...), custom_call_target="tpu_custom_call" | custom-call | flops 4831838208 | bytes 13631488 | tf_op jit(solution)/shard_map/rest/pallas_call | solution.py:310
  146.4 56.2 %all_to_all.25 = bf16[16,32,4096]{2,1,0:T(8,128)(2,1)S(1)} all-to-all(bf16[16,32,4096]{2,1,0:T(8,128)(2,1)} %bitcast.55), channel_id=1, replica_groups=mesh['ylo'=2,'z'=4,'x'=4,'yhi'=2,'core'=2] {'ylo','x','yhi'}, dimensions={0} | all-to-all | bytes 8388608 | tf_op jit(solution)/shard_map/all_to_all | solution.py:494
  202.6 3.5 %combine.1 = (bf16[64,4096]{1,0:T(8,128)(2,1)}, bf16[128,32,128]{2,1,0:T(8,128)(2,1)S(1)}) custom-call(bf16[128,512]{1,0:T(8,128)(2,1)S(1)} %pad_maximum_fusion.1.weighs_ref, bf16[128,64]{1,0:T(8,128)(2,1)S(1)} %fusion.4.picked_ref, f32[64,4096]{1,0:T(8,128)S(1)} %get-tuple-element.25.middle_ref, bf16[512,4096]{1,0:T(8,128)(2,1)S(1)} %bitcast.46), custom_call_target="tpu_custom_call" | custom-call | tf_op jit(solution)/shard_map/combine/pallas_call | solution.py:364
  206.2 24.2 %all_to_all.26.lines_ref = bf16[128,32,128]{2,1,0:T(8,128)(2,1)S(1)} all-to-all(bf16[128,32,128]{2,1,0:T(8,128)(2,1)S(1)} %get-tuple-element.39), channel_id=1, replica_groups=mesh['ylo'=2,'z'=4,'x'=4,'yhi'=2,'core'=2] {'ylo','z','x','yhi','core'}, dimensions={0} | all-to-all | bytes 2097152 | tf_op jit(solution)/shard_map/all_to_all | solution.py:503
  230.4 2.5 %unpack.1 = bf16[128,4096]{1,0:T(8,128)(2,1)} custom-call(bf16[128,32,128]{2,1,0:T(8,128)(2,1)S(1)} %all_to_all.26.lines_ref), custom_call_target="tpu_custom_call" | custom-call | tf_op jit(solution)/shard_map/unpack/pallas_call | solution.py:396
  (92 shorter events, 9.8 us)
Async XLA Ops:
  0.6 7.8 %copy-start.19 = (s32[64,8]{0,1:T(8,128)S(1)}, s32[64,8]{0,1:T(8,128)}, u32[]{:S(2)}) copy-start(s32[64,8]{0,1:T(8,128)} %param.23) | copy-start | bytes 6148
  0.7 7.9 %copy-start.20 = (f32[64,8]{0,1:T(8,128)S(1)}, f32[64,8]{0,1:T(8,128)}, u32[]{:S(2)}) copy-start(f32[64,8]{0,1:T(8,128)} %param.24) | copy-start | bytes 6148
  0.7 9.7 %copy-start.21 = (s32[64]{0:T(128)S(1)}, s32[64]{0:T(128)}, u32[]{:S(2)}) copy-start(s32[64]{0:T(128)} %param.26) | copy-start | bytes 772
  0.7 20.8 %all-to-all-start = ((bf16[16,32,768]{2,1,0:T(8,128)(2,1)}), bf16[16,32,768]{2,1,0:T(8,128)(2,1)S(1)}, u32[]{:S(2)}, u32[]{:S(2)}) async-start(bf16[16,32,768]{2,1,0:T(8,128)(2,1)} %param.27), calls=%async_computation | async-start | bytes 1572864 | tf_op jit(solution)/shard_map/all_to_all | solution.py:432
  13.4 16.6 %copy-start.18 = (bf16[64,4096]{1,0:T(8,128)(2,1)S(1)}, bf16[64,4096]{1,0:T(8,128)(2,1)}, u32[]{:S(2)}) copy-start(bf16[64,4096]{1,0:T(8,128)(2,1)} %param.16) | copy-start | bytes 1572868
  13.4 16.7 %copy-start.1 = (bf16[64,4096]{1,0:T(8,128)(2,1)S(1)}, bf16[64,4096]{1,0:T(8,128)(2,1)}, u32[]{:S(2)}) copy-start(bf16[64,4096]{1,0:T(8,128)(2,1)} %hidden_ref.1) | copy-start | bytes 1572868
  13.4 16.7 %copy-start.2 = (bf16[64,256]{1,0:T(8,128)(2,1)S(1)}, bf16[64,256]{1,0:T(8,128)(2,1)}, u32[]{:S(2)}) copy-start(bf16[64,256]{1,0:T(8,128)(2,1)} %nk_ref.1) | copy-start | bytes 98308
  13.4 16.7 %copy-start.3 = (bf16[64,256]{1,0:T(8,128)(2,1)S(1)}, bf16[64,256]{1,0:T(8,128)(2,1)}, u32[]{:S(2)}) copy-start(bf16[64,256]{1,0:T(8,128)(2,1)} %nv_ref.1) | copy-start | bytes 98308
  13.4 16.7 %copy-start.4 = (f32[4096]{0:T(1024)S(1)}, f32[4096]{0:T(1024)}, u32[]{:S(2)}) copy-start(f32[4096]{0:T(1024)} %param.22) | copy-start | bytes 49156
  13.4 16.7 %copy-start.5 = (s32[64]{0:T(128)S(1)}, s32[64]{0:T(128)}, u32[]{:S(2)}) copy-start(s32[64]{0:T(128)} %lengths_ref.1) | copy-start | bytes 772
  21.5 26.1 %all-to-all-start.1 = ((bf16[16,2,32,768]{3,2,1,0:T(8,128)(2,1)}), bf16[16,2,32,768]{3,2,1,0:T(8,128)(2,1)}, u32[]{:S(2)}, u32[]{:S(2)}) async-start(bf16[16,2,32,768]{3,2,1,0:T(8,128)(2,1)} %pad_maximum_fusion), calls=%async_computation.1 | async-start | bytes 3145728 | tf_op jit(solution)/shard_map/all_to_all | solution.py:432
  26.2 18.8 %collective-permute-start.1 = (bf16[16,32,768]{2,1,0:T(8,128)(2,1)S(1)}, bf16[16,32,768]{2,1,0:T(8,128)(2,1)S(1)}, u32[]{:S(2)}, u32[]{:S(2)}) collective-permute-start(bf16[16,32,768]{2,1,0:T(8,128)(2,1)S(1)} %all-to-all-done), channel_id=1, source_target_pairs={{0,48},{16,0},{32,16},{48,32},{1,49},{17,1},{33,17},{49,33},{2,50}... | collective-permute-start | bytes 2359304 | tf_op jit(solution)/shard_map/ppermute | solution.py:149
  30.0 17.6 %collective-permute-start = (bf16[16,32,768]{2,1,0:T(8,128)(2,1)S(1)}, bf16[16,32,768]{2,1,0:T(8,128)(2,1)S(1)}, u32[]{:S(2)}, u32[]{:S(2)}) collective-permute-start(bf16[16,32,768]{2,1,0:T(8,128)(2,1)S(1)} %all-to-all-done), channel_id=1, source_target_pairs={{0,16},{16,32},{32,48},{48,0},{1,17},{17,33},{33,49},{49,1},{2,18}... | collective-permute-start | bytes 2359304 | tf_op jit(solution)/shard_map/ppermute | solution.py:148
  47.6 62.1 %all-to-all-start.2 = ((bf16[16,32,4096]{2,1,0:T(8,128)(2,1)}), bf16[16,32,4096]{2,1,0:T(8,128)(2,1)}, u32[]{:S(2)}, u32[]{:S(2)}) async-start(bf16[16,32,4096]{2,1,0:T(8,128)(2,1)} %bitcast.47), calls=%async_computation.2 | async-start | bytes 8388608 | tf_op jit(solution)/shard_map/all_to_all | solution.py:480
  53.9 49.2 %copy-start.11 = (bf16[16,32,768]{2,1,0:T(8,128)(2,1)S(1)}, bf16[16,32,768]{2,1,0:T(8,128)(2,1)}, u32[]{:S(2)}) copy-start(bf16[16,32,768]{2,1,0:T(8,128)(2,1)} %copy-done.10) | copy-start | bytes 2359300
  53.9 34.4 %collective-permute-start.4 = (bf16[16,2,32,768]{3,2,1,0:T(8,128)(2,1)}, bf16[16,2,32,768]{3,2,1,0:T(8,128)(2,1)S(1)}, u32[]{:S(2)}, u32[]{:S(2)}) collective-permute-start(bf16[16,2,32,768]{3,2,1,0:T(8,128)(2,1)} %all-to-all-done.1), channel_id=1, source_target_pairs={{0,48},{16,0},{32,16},{48,32},{1,49},{17,1},{33,17},{49,33},{2,50}... | collective-permute-start | bytes 4718600 | tf_op jit(solution)/shard_map/ppermute | solution.py:149
  57.2 34.9 %collective-permute-start.2 = (bf16[16,2,32,768]{3,2,1,0:T(8,128)(2,1)}, bf16[16,2,32,768]{3,2,1,0:T(8,128)(2,1)S(1)}, u32[]{:S(2)}, u32[]{:S(2)}) collective-permute-start(bf16[16,2,32,768]{3,2,1,0:T(8,128)(2,1)} %all-to-all-done.1), channel_id=1, source_target_pairs={{0,16},{16,32},{32,48},{48,0},{1,17},{17,33},{33,49},{49,1},{2,18}... | collective-permute-start | bytes 4718600 | tf_op jit(solution)/shard_map/ppermute | solution.py:148
  57.2 38.2 %collective-permute-start.6 = (bf16[16,32,768]{2,1,0:T(8,128)(2,1)S(1)}, bf16[16,32,768]{2,1,0:T(8,128)(2,1)S(1)}, u32[]{:S(2)}, u32[]{:S(2)}) collective-permute-start(bf16[16,32,768]{2,1,0:T(8,128)(2,1)S(1)} %all-to-all-done), channel_id=1, source_target_pairs={{0,1},{1,0},{2,3},{3,2},{4,5},{5,4},{6,7},{7,6},{8,9},{9,8},{10,11... | collective-permute-start | bytes 2359304 | tf_op jit(solution)/shard_map/ppermute | solution.py:156
  60.3 44.5 %collective-permute-start.9 = (bf16[16,2,32,768]{3,2,1,0:T(8,128)(2,1)}, bf16[16,2,32,768]{3,2,1,0:T(8,128)(2,1)S(1)}, u32[]{:S(2)}, u32[]{:S(2)}) collective-permute-start(bf16[16,2,32,768]{3,2,1,0:T(8,128)(2,1)} %all-to-all-done.1), channel_id=1, source_target_pairs={{0,1},{1,0},{2,3},{3,2},{4,5},{5,4},{6,7},{7,6},{8,9},{9,8},{10,11... | collective-permute-start | bytes 4718600 | tf_op jit(solution)/shard_map/ppermute | solution.py:156
  88.3 10.4 %copy-start.6 = (bf16[16,2,32,768]{3,2,1,0:T(8,128)(2,1)}, bf16[16,2,32,768]{3,2,1,0:T(8,128)(2,1)S(1)}, u32[]{:S(2)}) copy-start(bf16[16,2,32,768]{3,2,1,0:T(8,128)(2,1)S(1)} %collective-permute-done.4) | copy-start | bytes 4718596
  88.3 19.1 %collective-permute-start.11 = (bf16[16,2,32,768]{3,2,1,0:T(8,128)(2,1)S(1)}, bf16[16,2,32,768]{3,2,1,0:T(8,128)(2,1)S(1)}, u32[]{:S(2)}, u32[]{:S(2)}) collective-permute-start(bf16[16,2,32,768]{3,2,1,0:T(8,128)(2,1)S(1)} %collective-permute-done.4), channel_id=1, source_target_pairs={{0,1},{1,0},{2,3},{3,2},{4,5},{5,4},{6,7},{7,6},{8,9},{9,8},{10,11... | collective-permute-start | bytes 4718600 | tf_op jit(solution)/shard_map/ppermute | solution.py:156
  92.1 16.5 %collective-permute-start.10 = (bf16[16,2,32,768]{3,2,1,0:T(8,128)(2,1)S(1)}, bf16[16,2,32,768]{3,2,1,0:T(8,128)(2,1)}, u32[]{:S(2)}, u32[]{:S(2)}) collective-permute-start(bf16[16,2,32,768]{3,2,1,0:T(8,128)(2,1)S(1)} %collective-permute-done.2), channel_id=1, source_target_pairs={{0,1},{1,0},{2,3},{3,2},{4,5},{5,4},{6,7},{7,6},{8,9},{9,8},{10,11... | collective-permute-start | bytes 4718600 | tf_op jit(solution)/shard_map/ppermute | solution.py:156
  95.4 5.4 %collective-permute-start.8 = (bf16[16,32,768]{2,1,0:T(8,128)(2,1)}, bf16[16,32,768]{2,1,0:T(8,128)(2,1)S(1)}, u32[]{:S(2)}, u32[]{:S(2)}) collective-permute-start(bf16[16,32,768]{2,1,0:T(8,128)(2,1)} %copy-done.10), channel_id=1, source_target_pairs={{0,1},{1,0},{2,3},{3,2},{4,5},{5,4},{6,7},{7,6},{8,9},{9,8},{10,11... | collective-permute-start | bytes 2359304 | tf_op jit(solution)/shard_map/ppermute | solution.py:156
  96.3 6.8 %collective-permute-start.7 = (bf16[16,32,768]{2,1,0:T(8,128)(2,1)S(1)}, bf16[16,32,768]{2,1,0:T(8,128)(2,1)S(1)}, u32[]{:S(2)}, u32[]{:S(2)}) collective-permute-start(bf16[16,32,768]{2,1,0:T(8,128)(2,1)S(1)} %collective-permute-done), channel_id=1, source_target_pairs={{0,1},{1,0},{2,3},{3,2},{4,5},{5,4},{6,7},{7,6},{8,9},{9,8},{10,11... | collective-permute-start | bytes 2359304 | tf_op jit(solution)/shard_map/ppermute | solution.py:156
  100.8 19.6 %collective-permute-start.5 = (bf16[8,2,32,768]{3,2,1,0:T(8,128)(2,1)}, bf16[8,2,32,768]{3,2,1,0:T(8,128)(2,1)}, u32[]{:S(2)}, u32[]{:S(2)}) collective-permute-start(bf16[8,2,32,768]{3,2,1,0:T(8,128)(2,1)} %slice.17), channel_id=1, source_target_pairs={{0,48},{16,0},{32,16},{48,32},{1,49},{17,1},{33,17},{49,33},{2,50}... | collective-permute-start | bytes 2359304 | tf_op jit(solution)/shard_map/ppermute | solution.py:151
  103.1 20.0 %collective-permute-start.3 = (bf16[8,2,32,768]{3,2,1,0:T(8,128)(2,1)}, bf16[8,2,32,768]{3,2,1,0:T(8,128)(2,1)}, u32[]{:S(2)}, u32[]{:S(2)}) collective-permute-start(bf16[8,2,32,768]{3,2,1,0:T(8,128)(2,1)} %slice.16), channel_id=1, source_target_pairs={{0,16},{16,32},{32,48},{48,0},{1,17},{17,33},{33,49},{49,1},{2,18}... | collective-permute-start | bytes 2359304 | tf_op jit(solution)/shard_map/ppermute | solution.py:150
  104.8 23.7 %collective-permute-start.13 = (bf16[8,32,768]{2,1,0:T(8,128)(2,1)}, bf16[8,32,768]{2,1,0:T(8,128)(2,1)S(1)}, u32[]{:S(2)}, u32[]{:S(2)}) collective-permute-start(bf16[8,32,768]{2,1,0:T(8,128)(2,1)} %slice.19), channel_id=1, source_target_pairs={{0,48},{16,0},{32,16},{48,32},{1,49},{17,1},{33,17},{49,33},{2,50}... | collective-permute-start | bytes 1179656 | tf_op jit(solution)/shard_map/ppermute | solution.py:151
  107.4 24.1 %collective-permute-start.12 = (bf16[8,32,768]{2,1,0:T(8,128)(2,1)}, bf16[8,32,768]{2,1,0:T(8,128)(2,1)}, u32[]{:S(2)}, u32[]{:S(2)}) collective-permute-start(bf16[8,32,768]{2,1,0:T(8,128)(2,1)} %slice.18), channel_id=1, source_target_pairs={{0,16},{16,32},{32,48},{48,0},{1,17},{17,33},{33,49},{49,1},{2,18}... | collective-permute-start | bytes 1179656 | tf_op jit(solution)/shard_map/ppermute | solution.py:150
  123.1 11.5 %collective-permute-start.16 = (bf16[8,2,32,768]{3,2,1,0:T(8,128)(2,1)}, bf16[8,2,32,768]{3,2,1,0:T(8,128)(2,1)S(1)}, u32[]{:S(2)}, u32[]{:S(2)}) collective-permute-start(bf16[8,2,32,768]{3,2,1,0:T(8,128)(2,1)} %collective-permute-done.3), channel_id=1, source_target_pairs={{0,1},{1,0},{2,3},{3,2},{4,5},{5,4},{6,7},{7,6},{8,9},{9,8},{10,11... | collective-permute-start | bytes 2359304 | tf_op jit(solution)/shard_map/ppermute | solution.py:156
  126.0 8.6 %collective-permute-start.17 = (bf16[8,2,32,768]{3,2,1,0:T(8,128)(2,1)}, bf16[8,2,32,768]{3,2,1,0:T(8,128)(2,1)S(1)}, u32[]{:S(2)}, u32[]{:S(2)}) collective-permute-start(bf16[8,2,32,768]{3,2,1,0:T(8,128)(2,1)} %collective-permute-done.5), channel_id=1, source_target_pairs={{0,1},{1,0},{2,3},{3,2},{4,5},{5,4},{6,7},{7,6},{8,9},{9,8},{10,11... | collective-permute-start | bytes 2359304 | tf_op jit(solution)/shard_map/ppermute | solution.py:156
  128.5 4.6 %collective-permute-start.15 = (bf16[8,32,768]{2,1,0:T(8,128)(2,1)S(1)}, bf16[8,32,768]{2,1,0:T(8,128)(2,1)S(1)}, u32[]{:S(2)}, u32[]{:S(2)}) collective-permute-start(bf16[8,32,768]{2,1,0:T(8,128)(2,1)S(1)} %collective-permute-done.13), channel_id=1, source_target_pairs={{0,1},{1,0},{2,3},{3,2},{4,5},{5,4},{6,7},{7,6},{8,9},{9,8},{10,11... | collective-permute-start | bytes 1179656 | tf_op jit(solution)/shard_map/ppermute | solution.py:156
  131.5 3.1 %collective-permute-start.14 = (bf16[8,32,768]{2,1,0:T(8,128)(2,1)}, bf16[8,32,768]{2,1,0:T(8,128)(2,1)S(1)}, u32[]{:S(2)}, u32[]{:S(2)}) collective-permute-start(bf16[8,32,768]{2,1,0:T(8,128)(2,1)} %collective-permute-done.12), channel_id=1, source_target_pairs={{0,1},{1,0},{2,3},{3,2},{4,5},{5,4},{6,7},{7,6},{8,9},{9,8},{10,11... | collective-permute-start | bytes 1179656 | tf_op jit(solution)/shard_map/ppermute | solution.py:156
  (12 other events, 37.5 us)
